TPU v7x, 128 devices: a whole 4x4x4 slice. The times are simulated.
128 devices in a mesh: patch: 32 (over z, y, core), lev: 4 (over x).
Axes of the slice: x: 4, y: 4, z: 4, core: 2. Of those that a mesh axis runs over, the one named last changes fastest.
Arguments:
- background: bfloat16 [128, 4, 512, 6, 256], P('patch', 'lev'), may hold values from -6 to 6
- patch_order: int32 [512], replicated, may hold values from 0 to 511, each once
- tile_counts: int32 [512], P('patch'), may hold values from 1 to 49, as said below
- obs_column: int32 [262144], P('patch'), may hold values from 0 to 255
- obs_operator: bfloat16 [4, 6, 262144], P(None, None, 'patch'), may hold values from -1.25 to 1.25
- obs_value: float32 [262144], P('patch'), may hold values from -6 to 6
- obs_weight: float32 [262144], P('patch'), may hold values from 0.05 to 2
Outputs:
- analysis: bfloat16 [128, 4, 512, 6, 256], P('patch', 'lev')
Inputs may be any that keep to these rules, and one draw needn't show every extreme that they name: `tile_counts`: the entries 16 g to 16 g + 15 sum to at most 64 for every g, and to exactly 64 for some g; no entry exceeds 64 - 15, and some entry equals it.
All inputs are finite; a program needn't handle non-finite values.
Results may differ from a plain program's by a relative error of at most 0.0056.
Values may be sent and summed in bfloat16 or wider, within the bound.
No kernel may reach another device: no remote copies, remote signals or barrier semaphores. Data moves between devices by JAX's collectives and lax.ppermute only.
A program may use at most 128 MiB of HBM per device.

v0:
```python
import functools

import jax
import jax.numpy as jnp
from jax import lax
from jax.experimental import pallas as pl
from jax.experimental.pallas import tpu as pltpu
from jax.sharding import PartitionSpec as P

TILE = 128
ITERS = 10
CHUNKS = (8, 8)
F32 = jnp.float32
BF16 = jnp.bfloat16
AUG = 16


def params(mib):
    return pltpu.CompilerParams(vmem_limit_bytes=mib * 1024 * 1024)


def cost(us):
    return pl.CostEstimate(flops=int(us * 1.15e9), bytes_accessed=0, transcendentals=0)


def vmem():
    return pl.BlockSpec(memory_space=pltpu.VMEM)


def hbm():
    return pl.BlockSpec(memory_space=pl.ANY)


def smem():
    return pl.BlockSpec(memory_space=pltpu.SMEM)


def dot(a, b):
    return jnp.dot(a, b, preferred_element_type=F32)


def dot_nt(a, b):
    return lax.dot_general(a, b, (((1,), (1,)), ((), ())), preferred_element_type=F32)


def split(a):
    hi = a.astype(BF16)
    return hi, (a - hi.astype(F32)).astype(BF16)


def dot3(a, b, mul=dot):
    ah, al = a
    bh, bl = b
    return mul(ah, bh) + (mul(ah, bl) + mul(al, bh))


def start(copies):
    for copy in copies:
        copy.start()


def wait(copies):
    for copy in copies:
        copy.wait()


def slot_hot(order_ref):
    patches = order_ref.shape[1]
    ids = lax.broadcasted_iota(jnp.int32, (patches, patches), 0)
    return (ids == order_ref[...]).astype(F32)


def row_permutation(slots, members, gather):
    size = slots * members * gather
    target = lax.broadcasted_iota(jnp.int32, (size, size), 0)
    per = gather * members
    origin = lax.rem(target, per) * slots + lax.div(target, per)
    return (origin == lax.broadcasted_iota(jnp.int32, (size, size), 1)).astype(BF16)


def send_kernel(first, order_ref, x_ref, out_ref, x_buf, out_buf, x_sem, out_sem):
    fields, members, patches, cols = x_buf.shape
    groups, rows = out_buf.shape[1], out_buf.shape[2]
    slots = rows // members
    loads = [
        pltpu.make_async_copy(x_ref.at[:, f], x_buf.at[f], x_sem.at[f]) for f in range(fields)
    ]
    stores = [
        pltpu.make_async_copy(out_buf.at[f], out_ref.at[:, f], out_sem.at[f])
        for f in range(fields)
    ]
    start(loads)
    hot = slot_hot(order_ref).T.reshape(groups, patches // groups, patches)
    hot = hot[:, first : first + slots].reshape(groups * slots, patches).astype(BF16)
    for f in range(fields):
        loads[f].wait()
        parts = [dot(hot, x_buf[f, m]).reshape(groups, slots, cols) for m in range(members)]
        out_buf[f] = jnp.concatenate(parts, axis=1).astype(BF16)
        stores[f].start()
    wait(stores)


def send(order, x, first, slots, groups):
    members, fields, patches, cols = x.shape
    return pl.pallas_call(
        functools.partial(send_kernel, first),
        in_specs=[vmem(), hbm()],
        out_specs=hbm(),
        out_shape=jax.ShapeDtypeStruct((groups, fields, members * slots, cols), BF16),
        scratch_shapes=[
            pltpu.VMEM((fields, members, patches, cols), BF16),
            pltpu.VMEM((fields, groups, members * slots, cols), BF16),
            pltpu.SemaphoreType.DMA((fields,)),
            pltpu.SemaphoreType.DMA((fields,)),
        ],
        compiler_params=params(58),
        cost_estimate=cost(5),
        name="send_permute",
    )(order, x)


def tile_range(base, count, lev):
    return lax.div(base - lev + 3, 4), lax.div(base + count - lev + 3, 4)


def observe_kernel(first, counts_ref, lev_ref, recv_ref, op_ref, col_ref, *rest):
    x_ref, y_refs, scratch = rest[-16], rest[-15:-11], rest[-11:]
    recv_buf, x_buf, op_buf, col_buf, mean_ref, y_buf, recv_sem, x_sem, op_sem, col_sem, y_sem = scratch
    fields, groups, rows, cols = recv_buf.shape
    slots, members = x_buf.shape[1], x_buf.shape[2]
    members_local = rows // slots
    gather = 256 // rows
    part = members_local * gather
    loads = [
        pltpu.make_async_copy(recv_ref.at[:, f], recv_buf.at[f], recv_sem.at[f])
        for f in range(fields)
    ]
    stores = [
        pltpu.make_async_copy(x_buf.at[f], x_ref.at[f], x_sem.at[f]) for f in range(fields)
    ]
    small = [
        pltpu.make_async_copy(op_ref, op_buf, op_sem),
        pltpu.make_async_copy(col_ref, col_buf, col_sem),
    ]
    start(loads)
    start(small)
    perm = row_permutation(slots, members_local, gather)
    mean_ref[...] = jnp.zeros_like(mean_ref)
    for f in range(fields):
        loads[f].wait()
        for b in range(groups // gather):
            block = recv_buf[f, b * gather : (b + 1) * gather].reshape(gather * rows, cols)
            moved = dot(perm, block).astype(BF16).reshape(slots, part, cols)
            x_buf[f, :, b * part : (b + 1) * part, :] = moved
        stores[f].start()
    wait(small)

    begin = jnp.int32(0)
    for s in range(first):
        begin = begin + counts_ref[s]
    column_ids = lax.broadcasted_iota(jnp.int32, (cols, TILE), 0)

    def table_of(row):
        hit = (column_ids == col_buf[pl.ds(row, 1), :]).astype(BF16)
        weights = op_buf[row]
        return jnp.concatenate(
            [hit * weights[f : f + 1, :].astype(BF16) for f in range(fields)], axis=0
        )

    def store(local, y, mean):
        offset = lax.rem(local + 4 - lev_ref[0], 4)
        place = lax.div(local, 4)
        mean_ref[offset, pl.ds(place, 1), :] = mean
        y_buf[offset, pl.ds(pl.multiple_of(place * members, members), members), :] = (
            y - mean
        ).astype(BF16)

    def slot_step(s, base):
        count = counts_ref[first + s]

        def pair_step(i, carry):
            one = base + 2 * i
            two = jnp.minimum(one + 1, base + count - 1)
            table = jnp.concatenate([table_of(begin + one), table_of(begin + two)], axis=1)
            x = jnp.concatenate([x_buf[f, s] for f in range(fields)], axis=1)
            y = dot(x, table)
            mean = jnp.mean(y, axis=0, keepdims=True)
            store(one, y[:, :TILE], mean[:, :TILE])
            store(two, y[:, TILE:], mean[:, TILE:])
            return carry

        lax.fori_loop(0, lax.div(count + 1, 2), pair_step, 0)
        return base + count

    lax.fori_loop(0, slots, slot_step, jnp.int32(0))
    for d in range(4):
        mean = mean_ref[d]
        hi = mean.astype(BF16)
        mid = (mean - hi.astype(F32)).astype(BF16)
        low = (mean - hi.astype(F32) - mid.astype(F32)).astype(BF16)
        y_buf[d, y_buf.shape[1] - 48 :, :] = jnp.concatenate([hi, mid, low], axis=0)
    outs = [pltpu.make_async_copy(y_buf.at[d], y_refs[d], y_sem.at[d]) for d in range(4)]
    start(outs)
    wait(outs)
    wait(stores)


def observe(counts, lev, recv, op, col, first, slots, tiles, us, after):
    groups, fields, rows, cols = recv.shape
    members = groups * rows // slots
    length = tiles // 4 * members + 48
    return pl.pallas_call(
        functools.partial(observe_kernel, first),
        in_specs=[smem(), smem(), hbm(), hbm(), hbm()] + [hbm() for _ in after],
        out_specs=[hbm()] * 5,
        out_shape=[jax.ShapeDtypeStruct((fields, slots, members, cols), BF16)]
        + [jax.ShapeDtypeStruct((length, TILE), BF16)] * 4,
        scratch_shapes=[
            pltpu.VMEM((fields, groups, rows, cols), BF16),
            pltpu.VMEM((fields, slots, members, cols), BF16),
            pltpu.VMEM(op.shape, F32),
            pltpu.VMEM(col.shape, jnp.int32),
            pltpu.VMEM((4, 16, TILE), F32),
            pltpu.VMEM((4, length, TILE), BF16),
            pltpu.SemaphoreType.DMA((fields,)),
            pltpu.SemaphoreType.DMA((fields,)),
            pltpu.SemaphoreType.DMA,
            pltpu.SemaphoreType.DMA,
            pltpu.SemaphoreType.DMA((4,)),
        ],
        compiler_params=params(58),
        cost_estimate=cost(us),
        name="observe",
    )(counts, lev, recv, op, col, *after)


def gram_kernel(first, counts_ref, lev_ref, y0, y1, y2, y3, value_ref, weight_ref, *rest):
    out_refs, mean_ref = rest[-5:-1], rest[-1]
    per, _, members = out_refs[0].shape
    lev = lev_ref[0]
    start = jnp.int32(0)
    for s in range(first):
        start = start + counts_ref[s]
    tail = y0.shape[0] - 48
    total = (y0[tail:].astype(F32) + y1[tail:].astype(F32)) + (
        y2[tail:].astype(F32) + y3[tail:].astype(F32)
    )
    mean_ref[...] = total[0:16] + (total[16:32] + total[32:48])
    for d, out_ref in enumerate(out_refs):
        out_ref[...] = jnp.zeros_like(out_ref)
        owned = lax.rem(lev + d, 4) * per
        base = lax.fori_loop(0, owned, lambda s, b: b + counts_ref[first + s], jnp.int32(0))
        for s in range(per):
            count = counts_ref[first + owned + s]

            def tile_step(i, carry, s=s, out_ref=out_ref):
                row = start + 4 * i + lev
                rows = pl.ds(pl.multiple_of(i * members, members), members)
                pert = (y0[rows, :].astype(F32) + y1[rows, :].astype(F32)) + (
                    y2[rows, :].astype(F32) + y3[rows, :].astype(F32)
                )
                mean = mean_ref[pl.ds(i, 1), :]
                weight = weight_ref[pl.ds(row, 1), :]
                depart = value_ref[pl.ds(row, 1), :] - mean
                aug = jnp.concatenate([pert, depart, jnp.zeros((AUG - 1, TILE), F32)], axis=0)
                out_ref[s] += dot3(split(aug * weight), split(pert), dot_nt)
                return carry

            low, high = tile_range(base, count, lev)
            lax.fori_loop(low, high, tile_step, 0)
            base = base + count


def partial_gram(counts, lev, ys, value, weight, first, slots, members, us, after):
    return pl.pallas_call(
        functools.partial(gram_kernel, first),
        in_specs=[smem(), smem()] + [vmem()] * 6 + [hbm() for _ in after],
        out_specs=[vmem()] * 4,
        out_shape=[jax.ShapeDtypeStruct((slots // 4, members + AUG, members), F32)] * 4,
        scratch_shapes=[pltpu.VMEM((16, TILE), F32)],
        compiler_params=params(24),
        cost_estimate=cost(us),
        name="gram",
    )(counts, lev, *ys, value, weight, *after)


def solve_kernel(g0, g1, g2, g3, *rest):
    out_ref = rest[-1]
    slots, members = out_ref.shape[0], out_ref.shape[1]
    row = lax.broadcasted_iota(jnp.int32, (members, members), 0)
    eye = (row == lax.broadcasted_iota(jnp.int32, (members, members), 1)).astype(F32)
    uppers, lowers, scales, sides = [], [], [], []
    for s in range(slots):
        total = (g0[s] + g1[s]) + (g2[s] + g3[s])
        system = total[0:members] + (members - 1.0) * eye
        square = jnp.sum(jnp.sum(system * system, axis=1, keepdims=True), axis=0, keepdims=True)
        scale = jnp.sqrt(square)
        uppers.append(system / scale)
        lowers.append(eye)
        scales.append(scale)
        sides.append(total[members : members + 8])

    for step in range(ITERS):
        for s in range(slots):
            upper = split(uppers[s])
            if step == 0:
                middle = 1.5 * eye - 0.5 * uppers[s]
                lowers[s] = middle
                uppers[s] = dot3(upper, split(middle))
                continue
            lower = split(lowers[s])
            middle = split(1.5 * eye - 0.5 * dot3(lower, upper))
            lowers[s] = dot3(middle, lower)
            if step < ITERS - 1:
                uppers[s] = dot3(upper, middle)
    for s in range(slots):
        root = lowers[s] / jnp.sqrt(scales[s])
        parts = split(root)
        inner = dot3(split(sides[s]), parts, dot_nt)
        wmean = dot3(split(inner), parts, dot_nt)[0:1]
        out_ref[s] = (jnp.sqrt(jnp.float32(members - 1.0)) * root + wmean).astype(BF16)


def solve(gs, us, after):
    slots, _, members = gs[0].shape
    return pl.pallas_call(
        solve_kernel,
        in_specs=[vmem()] * 4 + [hbm() for _ in after],
        out_specs=vmem(),
        out_shape=jax.ShapeDtypeStruct((slots, members, members), BF16),
        compiler_params=params(24),
        cost_estimate=cost(us),
        name="newton_schulz",
    )(*gs, *after)


def apply_kernel(lev_ref, w0, w1, w2, w3, x_ref, *rest):
    out_ref, x_buf, mixed_ref, out_buf, x_sem, out_sem = rest[-6:]
    fields, slots, members, cols = x_buf.shape
    groups, rows = out_buf.shape[1], out_buf.shape[2]
    members_local = rows // slots
    gather = 256 // rows
    part = members_local * gather
    per = slots // 4
    loads = [
        pltpu.make_async_copy(x_ref.at[f], x_buf.at[f], x_sem.at[f]) for f in range(fields)
    ]
    stores = [
        pltpu.make_async_copy(out_buf.at[f], out_ref.at[:, f], out_sem.at[f])
        for f in range(fields)
    ]
    start(loads)
    perm = row_permutation(slots, members_local, gather).astype(F32).T.astype(BF16)
    for f in range(fields):
        loads[f].wait()
        for d, w_ref in enumerate((w0, w1, w2, w3)):
            owned = lax.rem(lev_ref[0] + 4 - d, 4) * per
            for s in range(per):
                x = x_buf[f, owned + s].astype(F32)
                mean = jnp.mean(x, axis=0, keepdims=True)
                mixed = dot(w_ref[s], (x - mean).astype(BF16))
                mixed_ref[owned + s] = (mean + mixed).astype(BF16)
        for b in range(groups // gather):
            block = mixed_ref[:, b * part : (b + 1) * part, :].reshape(slots * part, cols)
            moved = dot(perm, block).astype(BF16).reshape(gather, rows, cols)
            out_buf[f, b * gather : (b + 1) * gather] = moved
        stores[f].start()
    wait(stores)


def apply(lev, ws, x, groups, us, after):
    fields, slots, members, cols = x.shape
    rows = slots * members // groups
    return pl.pallas_call(
        apply_kernel,
        in_specs=[smem()] + [vmem()] * 4 + [hbm()] + [hbm() for _ in after],
        out_specs=hbm(),
        out_shape=jax.ShapeDtypeStruct((groups, fields, rows, cols), BF16),
        scratch_shapes=[
            pltpu.VMEM((fields, slots, members, cols), BF16),
            pltpu.VMEM((slots, members, cols), BF16),
            pltpu.VMEM((fields, groups, rows, cols), BF16),
            pltpu.SemaphoreType.DMA((fields,)),
            pltpu.SemaphoreType.DMA((fields,)),
        ],
        compiler_params=params(58),
        cost_estimate=cost(us),
        name="apply_weights",
    )(lev, *ws, x, *after)


def restore_kernel(order_ref, *refs):
    half = (len(refs) - 4) // 2
    recvs, out_ref, bufs = refs[:half], refs[half], refs[half + 1 : 2 * half + 1]
    out_buf, recv_sem, out_sem = refs[-3:]
    fields, members, patches, cols = out_buf.shape
    loads = [
        [
            pltpu.make_async_copy(r.at[:, f], b.at[f], recv_sem.at[f, c])
            for c, (r, b) in enumerate(zip(recvs, bufs))
        ]
        for f in range(fields)
    ]
    stores = [
        pltpu.make_async_copy(out_buf.at[f], out_ref.at[:, f], out_sem.at[f])
        for f in range(fields)
    ]
    for f in range(fields):
        start(loads[f])
    hot = slot_hot(order_ref).astype(BF16)
    for f in range(fields):
        wait(loads[f])
        blocks = [b[f].astype(F32) for b in bufs]
        for m in range(members):
            parts = []
            for block in blocks:
                slots = block.shape[1] // members
                parts.append(block[:, m * slots : (m + 1) * slots])
            stacked = jnp.concatenate(parts, axis=1).reshape(patches, cols).astype(BF16)
            out_buf[f, m] = dot(hot, stacked).astype(BF16)
        stores[f].start()
    wait(stores)


def restore(order, recvs, members):
    fields, cols = recvs[0].shape[1], recvs[0].shape[3]
    patches = order.shape[1]
    return pl.pallas_call(
        restore_kernel,
        in_specs=[vmem()] + [hbm()] * len(recvs),
        out_specs=hbm(),
        out_shape=jax.ShapeDtypeStruct((members, fields, patches, cols), BF16),
        scratch_shapes=[
            pltpu.VMEM((fields, r.shape[0], r.shape[2], cols), BF16) for r in recvs
        ]
        + [
            pltpu.VMEM((fields, members, patches, cols), BF16),
            pltpu.SemaphoreType.DMA((fields, len(recvs))),
            pltpu.SemaphoreType.DMA((fields,)),
        ],
        compiler_params=params(58),
        cost_estimate=cost(6),
        name="restore_order",
    )(order, *recvs)


def exchange(blocks):
    return [blocks[0]] + [
        lax.ppermute(blocks[d], "lev", [(i, (i + d) % 4) for i in range(4)]) for d in range(1, 4)
    ]


def body(background, patch_order, tile_counts, obs_column, obs_operator, obs_value, obs_weight):
    members_local, _, patches, fields, columns = background.shape
    slots_dev = tile_counts.shape[0]
    groups = patches // slots_dev
    tiles = obs_column.shape[0] // TILE
    level = lax.axis_index("lev")
    lev = jnp.reshape(level, (1,)).astype(jnp.int32)
    x = jnp.transpose(background[:, 0], (0, 2, 1, 3))
    order = patch_order.reshape(1, patches)
    col = obs_column.reshape(tiles, TILE)
    value = obs_value.reshape(tiles, TILE)
    weight = obs_weight.reshape(tiles, TILE)
    op = lax.dynamic_index_in_dim(obs_operator, level, 0, keepdims=False)
    op = jnp.transpose(op.reshape(fields, tiles, TILE), (1, 0, 2)).astype(F32)
    op = jnp.pad(op, ((0, 0), (0, 8 - fields), (0, 0)))

    gathered, firsts = [], []
    first = 0
    for slots in CHUNKS:
        if first > 0:
            order, op = lax.optimization_barrier((order, op))
        sent = send(order, x, first, slots, groups)
        gathered.append(lax.all_to_all(sent, "patch", split_axis=0, concat_axis=0, tiled=True))
        firsts.append(first)
        first += slots

    chunks = list(zip(CHUNKS, firsts, gathered))

    def see(c, us, after):
        slots, first, recv = chunks[c]
        room = tiles - (slots_dev - slots)
        x, *ys = observe(tile_counts, lev, recv, op, col, first, slots, room, us, after)
        return x, ys

    def weigh(c, ys, us, after):
        slots, first, _ = chunks[c]
        return partial_gram(tile_counts, lev, ys, value, weight, first, slots, members, us, after)

    def analyse(x, w, us, after):
        out = apply(lev, exchange([w] * 4), x, groups, us, after)
        return out, lax.all_to_all(out, "patch", split_axis=0, concat_axis=0, tiled=True)

    members = members_local * groups
    x0, ys0 = see(0, 200, [sent])
    gs0 = weigh(0, exchange(ys0), 1, [])
    x1, ys1 = see(1, 20, [gs0[0]])
    w0 = solve(exchange(gs0), 7, [ys1[0]])
    out0, back0 = analyse(x0, w0, 100, [])
    gs1 = weigh(1, exchange(ys1), 200, [out0])
    w1 = solve(exchange(gs1), 1, [])
    _, back1 = analyse(x1, w1, 1, [])
    backs = [back0, back1]

    result = restore(order, backs, members_local)
    return jnp.transpose(result, (0, 2, 1, 3))[:, None]


def solution(mesh):
    in_specs = (
        P("patch", "lev", None, None, None),
        P(),
        P("patch"),
        P("patch"),
        P(None, None, "patch"),
        P("patch"),
        P("patch"),
    )
    out_specs = P("patch", "lev", None, None, None)
    return jax.shard_map(body, mesh=mesh, in_specs=in_specs, out_specs=out_specs, check_vma=False)
```

profile of v0, /device:TPU:1, one launch (start us, length us, event | category | flops | bytes accessed | tf_op | source)
XLA Modules:
  0.0 250.0 jit_solution(258916801895784508)
XLA Ops:
  0.0 5.5 %send_permute.2 = bf16[32,6,32,256]{3,2,1,0:T(8,128)(2,1)} custom-call(s32[1,512]{1,0:T(1,128)} %bitcast.25, bf16[4,6,512,256]{3,2,1,0:T(8,128)(2,1)} %bitcast.21), custom_call_target="tpu_custom_call" | custom-call | flops 5750000128 | tf_op jit(solution)/shard_map/send_permute/pallas_call | solution.py:105
  5.5 9.6 %all-to-all-start = ((bf16[32,6,32,256]{3,2,1,0:T(8,128)(2,1)}), bf16[32,6,32,256]{3,2,1,0:T(8,128)(2,1)S(1)}, u32[]{:S(2)}, u32[]{:S(2)}) async-start(bf16[32,6,32,256]{3,2,1,0:T(8,128)(2,1)} %send_permute.2), calls=%async_computation | async-start | bytes 6291456 | tf_op jit(solution)/shard_map/all_to_all | solution.py:475
  16.5 5.5 %send_permute.3.rest_0_ = bf16[32,6,32,256]{3,2,1,0:T(8,128)(2,1)} custom-call(s32[1,512]{1,0:T(1,128)} %bitcast.26, bf16[4,6,512,256]{3,2,1,0:T(8,128)(2,1)} %bitcast.22), custom_call_target="tpu_custom_call" | custom-call | flops 5750000128 | tf_op jit(solution)/shard_map/send_permute/pallas_call | solution.py:105
  21.9 32.4 %all-to-all-done.recv_ref = bf16[32,6,32,256]{3,2,1,0:T(8,128)(2,1)S(1)} async-done(((bf16[32,6,32,256]{3,2,1,0:T(8,128)(2,1)}), bf16[32,6,32,256]{3,2,1,0:T(8,128)(2,1)S(1)}, u32[]{:S(2)}, u32[]{:S(2)}) %all-to-all-start) | async-done | bytes 3145760 | tf_op jit(solution)/shard_map/all_to_all | solution.py:475
  54.3 1.7 copy-done.15
  56.0 7.2 %all-to-all-start.1 = ((bf16[32,6,32,256]{3,2,1,0:T(8,128)(2,1)}), bf16[32,6,32,256]{3,2,1,0:T(8,128)(2,1)}, u32[]{:S(2)}, u32[]{:S(2)}) async-start(bf16[32,6,32,256]{3,2,1,0:T(8,128)(2,1)} %send_permute.3.rest_0_), calls=%async_computation.1 | async-start | bytes 6291456 | tf_op jit(solution)/shard_map/all_to_all | solution.py:475
  63.3 10.9 %observe.2 = (bf16[6,8,128,256]{3,2,1,0:T(8,128)(2,1)}, bf16[1840,128]{1,0:T(8,128)(2,1)}, bf16[1840,128]{1,0:T(8,128)(2,1)}, bf16[1840,128]{1,0:T(8,128)(2,1)}, bf16[1840,128]{1,0:T(8,128)(2,1)}) custom-call(s32[16]{0:T(128)} %counts_ref.7, s32[1]{0:T(128)} %bitcast.2.lev_ref, bf16[32,6,32,256]{3,2,1,0:T(8,128)(2,1)} %copy-done.15, ...), custom_call_target="tpu_custom_call" | custom-call | flops 230000001024 | tf_op jit(solution)/shard_map/observe/pallas_call | solution.py:212
  75.5 2.5 collective-permute-start.1
  79.1 8.9 %collective-permute-done.y1 = bf16[1840,128]{1,0:T(8,128)(2,1)S(1)} collective-permute-done((bf16[1840,128]{1,0:T(8,128)(2,1)}, bf16[1840,128]{1,0:T(8,128)(2,1)S(1)}, u32[]{:S(2)}, u32[]{:S(2)}) %collective-permute-start) | collective-permute-done | bytes 471072 | tf_op jit(solution)/shard_map/ppermute | solution.py:449
  87.9 11.1 %collective-permute-done.1.y2 = bf16[1840,128]{1,0:T(8,128)(2,1)S(1)} collective-permute-done((bf16[1840,128]{1,0:T(8,128)(2,1)}, bf16[1840,128]{1,0:T(8,128)(2,1)S(1)}, u32[]{:S(2)}, u32[]{:S(2)}) %collective-permute-start.1) | collective-permute-done | bytes 471072 | tf_op jit(solution)/shard_map/ppermute | solution.py:449
  100.1 2.6 %gram.2 = (f32[2,144,128]{2,1,0:T(8,128)S(1)}, f32[2,144,128]{2,1,0:T(8,128)S(1)}, f32[2,144,128]{2,1,0:T(8,128)S(1)}, f32[2,144,128]{2,1,0:T(8,128)S(1)}) custom-call(s32[16]{0:T(128)S(1)} %copy-done.8, s32[1]{0:T(128)} %bitcast.2.lev_ref, bf16[1840,128]{1,0:T(8,128)(2,1)S(1)} %copy-done.10, bf16[1840,128]{1,0:T(8,128)(2,1)S(1)} %collective-permute-done.y1, ...), custom_call_target="tpu_custom_call" | custom-call | flops 1150000000 | tf_op jit(solution)/shard_map/gram/pallas_call | solution.py:275
  103.3 1.5 collective-permute-start.3
  104.8 2.0 collective-permute-start.4
  106.7 1.3 collective-permute-start.5
  108.0 10.7 %observe.3 = (bf16[6,8,128,256]{3,2,1,0:T(8,128)(2,1)}, bf16[1840,128]{1,0:T(8,128)(2,1)}, bf16[1840,128]{1,0:T(8,128)(2,1)}, bf16[1840,128]{1,0:T(8,128)(2,1)}, bf16[1840,128]{1,0:T(8,128)(2,1)}) custom-call(s32[16]{0:T(128)} %counts_ref.7, s32[1]{0:T(128)} %bitcast.2.lev_ref, bf16[32,6,32,256]{3,2,1,0:T(8,128)(2,1)} %all-to-all-done.1.recv_ref, ...), custom_call_target="tpu_custom_call" | custom-call | flops 23000000512 | tf_op jit(solution)/shard_map/observe/pallas_call | solution.py:212
  119.8 4.7 %newton_schulz.2.w0 = bf16[2,128,128]{2,1,0:T(8,128)(2,1)S(1)} custom-call(f32[2,144,128]{2,1,0:T(8,128)S(1)} %copy-done.12, f32[2,144,128]{2,1,0:T(8,128)S(1)} %collective-permute-done.3.g1, f32[2,144,128]{2,1,0:T(8,128)S(1)} %collective-permute-done.4.g2, f32[2,144,128]{2,1,0:T(8,128)S(1)} %collective-permute-done.5.g3, bf16[1840,128]{1,0:T(8,128)(2,1)S(1)} %copy-done.13), custom_call_target="tpu_custom_call" | custom-call | flops 8049999872 | tf_op jit(solution)/shard_map/newton_schulz/pallas_call | solution.py:326
  125.7 1.5 collective-permute-start.8
  127.2 2.4 collective-permute-start.10
  132.6 6.7 %apply_weights.2.rest_0_ = bf16[32,6,32,256]{3,2,1,0:T(8,128)(2,1)} custom-call(s32[1]{0:T(128)} %bitcast.2.lev_ref, bf16[2,128,128]{2,1,0:T(8,128)(2,1)} %copy-done.3, bf16[2,128,128]{2,1,0:T(8,128)(2,1)} %copy-done.19, bf16[2,128,128]{2,1,0:T(8,128)(2,1)} %copy-done.20, bf16[2,128,128]{2,1,0:T(8,128)(2,1)} %copy-done.21, ...), custom_call_target="tpu_custom_call" | custom-call | flops 115000000512 | tf_op jit(solution)/shard_map/apply_weights/pallas_call | solution.py:374
  139.3 16.9 %all-to-all-start.2 = ((bf16[32,6,32,256]{3,2,1,0:T(8,128)(2,1)}), bf16[32,6,32,256]{3,2,1,0:T(8,128)(2,1)}, u32[]{:S(2)}, u32[]{:S(2)}) async-start(bf16[32,6,32,256]{3,2,1,0:T(8,128)(2,1)} %apply_weights.2.rest_0_), calls=%async_computation.2 | async-start | bytes 6291456 | tf_op jit(solution)/shard_map/all_to_all | solution.py:493
  158.9 3.3 %gram.3 = (f32[2,144,128]{2,1,0:T(8,128)S(1)}, f32[2,144,128]{2,1,0:T(8,128)S(1)}, f32[2,144,128]{2,1,0:T(8,128)S(1)}, f32[2,144,128]{2,1,0:T(8,128)S(1)}) custom-call(s32[16]{0:T(128)S(1)} %copy-done.9, s32[1]{0:T(128)} %bitcast.2.lev_ref, bf16[1840,128]{1,0:T(8,128)(2,1)S(1)} %copy-done.14, bf16[1840,128]{1,0:T(8,128)(2,1)} %collective-permute-done.9.y1, ...), custom_call_target="tpu_custom_call" | custom-call | flops 230000001024 | tf_op jit(solution)/shard_map/gram/pallas_call | solution.py:275
  162.2 3.3 %collective-permute-start.12 = (f32[2,144,128]{2,1,0:T(8,128)S(1)}, f32[2,144,128]{2,1,0:T(8,128)S(1)}, u32[]{:S(2)}, u32[]{:S(2)}) collective-permute-start(f32[2,144,128]{2,1,0:T(8,128)S(1)} %get-tuple-element.41), channel_id=1, source_target_pairs={{0,1},{1,2},{2,3},{3,0},{4,5},{5,6},{6,7},{7,4},{8,9},{9,10},{10,1... | collective-permute-start | bytes 442376 | tf_op jit(solution)/shard_map/ppermute | solution.py:449
  165.5 1.6 collective-permute-start.13
  168.2 1.8 collective-permute-done.12.g1
  170.0 4.6 %collective-permute-done.13.g2 = f32[2,144,128]{2,1,0:T(8,128)S(1)} collective-permute-done((f32[2,144,128]{2,1,0:T(8,128)S(1)}, f32[2,144,128]{2,1,0:T(8,128)S(1)}, u32[]{:S(2)}, u32[]{:S(2)}) %collective-permute-start.13) | collective-permute-done | bytes 147488 | tf_op jit(solution)/shard_map/ppermute | solution.py:449
  174.7 4.7 %newton_schulz.3.w0 = bf16[2,128,128]{2,1,0:T(8,128)(2,1)S(1)} custom-call(f32[2,144,128]{2,1,0:T(8,128)S(1)} %get-tuple-element.40.g0, f32[2,144,128]{2,1,0:T(8,128)S(1)} %collective-permute-done.12.g1, f32[2,144,128]{2,1,0:T(8,128)S(1)} %collective-permute-done.13.g2, f32[2,144,128]{2,1,0:T(8,128)S(1)} %collective-permute-done.14.g3), custom_call_target="tpu_custom_call" | custom-call | flops 1150000000 | tf_op jit(solution)/shard_map/newton_schulz/pallas_call | solution.py:326
  180.6 2.1 collective-permute-start.16
  184.3 2.0 collective-permute-done.16.w2
  186.9 6.7 %apply_weights.3 = bf16[32,6,32,256]{3,2,1,0:T(8,128)(2,1)} custom-call(s32[1]{0:T(128)} %bitcast.2.lev_ref, bf16[2,128,128]{2,1,0:T(8,128)(2,1)} %copy-done.2, bf16[2,128,128]{2,1,0:T(8,128)(2,1)} %copy-done.16, bf16[2,128,128]{2,1,0:T(8,128)(2,1)} %copy-done.17, bf16[2,128,128]{2,1,0:T(8,128)(2,1)} %copy-done.18, ...), custom_call_target="tpu_custom_call" | custom-call | flops 1150000000 | tf_op jit(solution)/shard_map/apply_weights/pallas_call | solution.py:374
  193.6 1.9 all-to-all-done.2.refs_0_
  195.5 47.0 %all_to_all.20.refs_1_ = bf16[32,6,32,256]{3,2,1,0:T(8,128)(2,1)} all-to-all(bf16[32,6,32,256]{3,2,1,0:T(8,128)(2,1)} %apply_weights.3), channel_id=1, replica_groups=mesh['patch'=32,'lev'=4] {'patch'}, dimensions={0} | all-to-all | bytes 6291456 | tf_op jit(solution)/shard_map/all_to_all | solution.py:493
  242.5 7.3 %restore_order.1 = bf16[4,6,512,256]{3,2,1,0:T(8,128)(2,1)} custom-call(s32[1,512]{1,0:T(1,128)} %bitcast.27, bf16[32,6,32,256]{3,2,1,0:T(8,128)(2,1)} %all-to-all-done.2.refs_0_, bf16[32,6,32,256]{3,2,1,0:T(8,128)(2,1)} %all_to_all.20.refs_1_), custom_call_target="tpu_custom_call" | custom-call | flops 6899999744 | tf_op jit(solution)/shard_map/restore_order/pallas_call | solution.py:428
  (68 shorter events, 17.9 us)
Async XLA Ops:
  0.0 15.1 %copy-start = (bf16[4,6,8192]{2,0,1:T(4,128)(2,1)S(1)}, bf16[4,6,8192]{2,0,1:T(4,128)(2,1)}, u32[]{:S(2)}) copy-start(bf16[4,6,8192]{2,0,1:T(4,128)(2,1)} %param.11) | copy-start | bytes 1179652
  5.5 48.8 %all-to-all-start = ((bf16[32,6,32,256]{3,2,1,0:T(8,128)(2,1)}), bf16[32,6,32,256]{3,2,1,0:T(8,128)(2,1)S(1)}, u32[]{:S(2)}, u32[]{:S(2)}) async-start(bf16[32,6,32,256]{3,2,1,0:T(8,128)(2,1)} %send_permute.2), calls=%async_computation | async-start | bytes 6291456 | tf_op jit(solution)/shard_map/all_to_all | solution.py:475
  56.0 52.1 %all-to-all-start.1 = ((bf16[32,6,32,256]{3,2,1,0:T(8,128)(2,1)}), bf16[32,6,32,256]{3,2,1,0:T(8,128)(2,1)}, u32[]{:S(2)}, u32[]{:S(2)}) async-start(bf16[32,6,32,256]{3,2,1,0:T(8,128)(2,1)} %send_permute.3.rest_0_), calls=%async_computation.1 | async-start | bytes 6291456 | tf_op jit(solution)/shard_map/all_to_all | solution.py:475
  63.2 35.8 %copy-start.4 = (f32[8192]{0:T(1024)S(1)}, f32[8192]{0:T(1024)}, u32[]{:S(2)}) copy-start(f32[8192]{0:T(1024)} %param.12) | copy-start | bytes 98308
  63.2 35.8 %copy-start.6 = (f32[8192]{0:T(1024)S(1)}, f32[8192]{0:T(1024)}, u32[]{:S(2)}) copy-start(f32[8192]{0:T(1024)} %param.13) | copy-start | bytes 98308
  63.2 35.8 %copy-start.8 = (s32[16]{0:T(128)S(1)}, s32[16]{0:T(128)}, u32[]{:S(2)}) copy-start(s32[16]{0:T(128)} %counts_ref.7) | copy-start | bytes 196
  74.2 13.8 %collective-permute-start = (bf16[1840,128]{1,0:T(8,128)(2,1)}, bf16[1840,128]{1,0:T(8,128)(2,1)S(1)}, u32[]{:S(2)}, u32[]{:S(2)}) collective-permute-start(bf16[1840,128]{1,0:T(8,128)(2,1)} %get-tuple-element.28), channel_id=1, source_target_pairs={{0,1},{1,2},{2,3},{3,0},{4,5},{5,6},{6,7},{7,4},{8,9},{9,10},{10,1... | collective-permute-start | bytes 1413128 | tf_op jit(solution)/shard_map/ppermute | solution.py:449
  75.5 23.6 %collective-permute-start.1 = (bf16[1840,128]{1,0:T(8,128)(2,1)}, bf16[1840,128]{1,0:T(8,128)(2,1)S(1)}, u32[]{:S(2)}, u32[]{:S(2)}) collective-permute-start(bf16[1840,128]{1,0:T(8,128)(2,1)} %get-tuple-element.29), channel_id=1, source_target_pairs={{0,2},{1,3},{2,0},{3,1},{4,6},{5,7},{6,4},{7,5},{8,10},{9,11},{10,... | collective-permute-start | bytes 1413128 | tf_op jit(solution)/shard_map/ppermute | solution.py:449
  77.9 21.1 %collective-permute-start.2 = (bf16[1840,128]{1,0:T(8,128)(2,1)}, bf16[1840,128]{1,0:T(8,128)(2,1)S(1)}, u32[]{:S(2)}, u32[]{:S(2)}) collective-permute-start(bf16[1840,128]{1,0:T(8,128)(2,1)} %get-tuple-element.30), channel_id=1, source_target_pairs={{0,3},{1,0},{2,1},{3,2},{4,7},{5,4},{6,5},{7,6},{8,11},{9,8},{10,9... | collective-permute-start | bytes 1413128 | tf_op jit(solution)/shard_map/ppermute | solution.py:449
  103.3 15.4 %collective-permute-start.3 = (f32[2,144,128]{2,1,0:T(8,128)S(1)}, f32[2,144,128]{2,1,0:T(8,128)S(1)}, u32[]{:S(2)}, u32[]{:S(2)}) collective-permute-start(f32[2,144,128]{2,1,0:T(8,128)S(1)} %get-tuple-element.32), channel_id=1, source_target_pairs={{0,1},{1,2},{2,3},{3,0},{4,5},{5,6},{6,7},{7,4},{8,9},{9,10},{10,1... | collective-permute-start | bytes 442376 | tf_op jit(solution)/shard_map/ppermute | solution.py:449
  104.8 14.0 %collective-permute-start.4 = (f32[2,144,128]{2,1,0:T(8,128)S(1)}, f32[2,144,128]{2,1,0:T(8,128)S(1)}, u32[]{:S(2)}, u32[]{:S(2)}) collective-permute-start(f32[2,144,128]{2,1,0:T(8,128)S(1)} %get-tuple-element.33), channel_id=1, source_target_pairs={{0,2},{1,3},{2,0},{3,1},{4,6},{5,7},{6,4},{7,5},{8,10},{9,11},{10,... | collective-permute-start | bytes 442376 | tf_op jit(solution)/shard_map/ppermute | solution.py:449
  106.7 12.0 %collective-permute-start.5 = (f32[2,144,128]{2,1,0:T(8,128)S(1)}, f32[2,144,128]{2,1,0:T(8,128)S(1)}, u32[]{:S(2)}, u32[]{:S(2)}) collective-permute-start(f32[2,144,128]{2,1,0:T(8,128)S(1)} %get-tuple-element.34), channel_id=1, source_target_pairs={{0,3},{1,0},{2,1},{3,2},{4,7},{5,4},{6,5},{7,6},{8,11},{9,8},{10,9... | collective-permute-start | bytes 442376 | tf_op jit(solution)/shard_map/ppermute | solution.py:449
  108.0 10.7 %copy-start.12 = (f32[2,144,128]{2,1,0:T(8,128)S(1)}, f32[2,144,128]{2,1,0:T(8,128)}, u32[]{:S(2)}) copy-start(f32[2,144,128]{2,1,0:T(8,128)} %copy-done.11) | copy-start | bytes 442372
  124.5 7.5 %copy-start.3 = (bf16[2,128,128]{2,1,0:T(8,128)(2,1)}, bf16[2,128,128]{2,1,0:T(8,128)(2,1)S(1)}, u32[]{:S(2)}) copy-start(bf16[2,128,128]{2,1,0:T(8,128)(2,1)S(1)} %newton_schulz.2.w0) | copy-start | bytes 196612
  124.5 5.7 %collective-permute-start.6 = (bf16[2,128,128]{2,1,0:T(8,128)(2,1)S(1)}, bf16[2,128,128]{2,1,0:T(8,128)(2,1)S(1)}, u32[]{:S(2)}, u32[]{:S(2)}) collective-permute-start(bf16[2,128,128]{2,1,0:T(8,128)(2,1)S(1)} %newton_schulz.2.w0), channel_id=1, source_target_pairs={{0,1},{1,2},{2,3},{3,0},{4,5},{5,6},{6,7},{7,4},{8,9},{9,10},{10,1... | collective-permute-start | bytes 196616 | tf_op jit(solution)/shard_map/ppermute | solution.py:449
  124.7 6.3 %collective-permute-start.7 = (bf16[2,128,128]{2,1,0:T(8,128)(2,1)S(1)}, bf16[2,128,128]{2,1,0:T(8,128)(2,1)S(1)}, u32[]{:S(2)}, u32[]{:S(2)}) collective-permute-start(bf16[2,128,128]{2,1,0:T(8,128)(2,1)S(1)} %newton_schulz.2.w0), channel_id=1, source_target_pairs={{0,2},{1,3},{2,0},{3,1},{4,6},{5,7},{6,4},{7,5},{8,10},{9,11},{10,... | collective-permute-start | bytes 196616 | tf_op jit(solution)/shard_map/ppermute | solution.py:449
  125.7 6.3 %collective-permute-start.8 = (bf16[2,128,128]{2,1,0:T(8,128)(2,1)S(1)}, bf16[2,128,128]{2,1,0:T(8,128)(2,1)S(1)}, u32[]{:S(2)}, u32[]{:S(2)}) collective-permute-start(bf16[2,128,128]{2,1,0:T(8,128)(2,1)S(1)} %newton_schulz.2.w0), channel_id=1, source_target_pairs={{0,3},{1,0},{2,1},{3,2},{4,7},{5,4},{6,5},{7,6},{8,11},{9,8},{10,9... | collective-permute-start | bytes 196616 | tf_op jit(solution)/shard_map/ppermute | solution.py:449
  127.2 29.1 %collective-permute-start.10 = (bf16[1840,128]{1,0:T(8,128)(2,1)}, bf16[1840,128]{1,0:T(8,128)(2,1)}, u32[]{:S(2)}, u32[]{:S(2)}) collective-permute-start(bf16[1840,128]{1,0:T(8,128)(2,1)} %get-tuple-element.38), channel_id=1, source_target_pairs={{0,2},{1,3},{2,0},{3,1},{4,6},{5,7},{6,4},{7,5},{8,10},{9,11},{10,... | collective-permute-start | bytes 1413128 | tf_op jit(solution)/shard_map/ppermute | solution.py:449
  129.5 26.7 %collective-permute-start.11 = (bf16[1840,128]{1,0:T(8,128)(2,1)}, bf16[1840,128]{1,0:T(8,128)(2,1)}, u32[]{:S(2)}, u32[]{:S(2)}) collective-permute-start(bf16[1840,128]{1,0:T(8,128)(2,1)} %get-tuple-element.39), channel_id=1, source_target_pairs={{0,3},{1,0},{2,1},{3,2},{4,7},{5,4},{6,5},{7,6},{8,11},{9,8},{10,9... | collective-permute-start | bytes 1413128 | tf_op jit(solution)/shard_map/ppermute | solution.py:449
  130.2 1.8 copy-start.19
  130.2 26.1 %collective-permute-start.9 = (bf16[1840,128]{1,0:T(8,128)(2,1)}, bf16[1840,128]{1,0:T(8,128)(2,1)}, u32[]{:S(2)}, u32[]{:S(2)}) collective-permute-start(bf16[1840,128]{1,0:T(8,128)(2,1)} %get-tuple-element.37), channel_id=1, source_target_pairs={{0,1},{1,2},{2,3},{3,0},{4,5},{5,6},{6,7},{7,4},{8,9},{9,10},{10,1... | collective-permute-start | bytes 1413128 | tf_op jit(solution)/shard_map/ppermute | solution.py:449
  139.3 17.0 %copy-start.1 = (bf16[32,6,32,256]{3,2,1,0:T(8,128)(2,1)S(1)}, bf16[32,6,32,256]{3,2,1,0:T(8,128)(2,1)}, u32[]{:S(2)}) copy-start(bf16[32,6,32,256]{3,2,1,0:T(8,128)(2,1)} %apply_weights.2.rest_0_) | copy-start | bytes 9437188
  139.3 17.0 %copy-start.9 = (s32[16]{0:T(128)S(1)}, s32[16]{0:T(128)}, u32[]{:S(2)}) copy-start(s32[16]{0:T(128)} %counts_ref.7) | copy-start | bytes 196
  139.3 56.1 %all-to-all-start.2 = ((bf16[32,6,32,256]{3,2,1,0:T(8,128)(2,1)}), bf16[32,6,32,256]{3,2,1,0:T(8,128)(2,1)}, u32[]{:S(2)}, u32[]{:S(2)}) async-start(bf16[32,6,32,256]{3,2,1,0:T(8,128)(2,1)} %apply_weights.2.rest_0_), calls=%async_computation.2 | async-start | bytes 6291456 | tf_op jit(solution)/shard_map/all_to_all | solution.py:493
  162.2 7.9 %collective-permute-start.12 = (f32[2,144,128]{2,1,0:T(8,128)S(1)}, f32[2,144,128]{2,1,0:T(8,128)S(1)}, u32[]{:S(2)}, u32[]{:S(2)}) collective-permute-start(f32[2,144,128]{2,1,0:T(8,128)S(1)} %get-tuple-element.41), channel_id=1, source_target_pairs={{0,1},{1,2},{2,3},{3,0},{4,5},{5,6},{6,7},{7,4},{8,9},{9,10},{10,1... | collective-permute-start | bytes 442376 | tf_op jit(solution)/shard_map/ppermute | solution.py:449
  165.5 9.1 %collective-permute-start.13 = (f32[2,144,128]{2,1,0:T(8,128)S(1)}, f32[2,144,128]{2,1,0:T(8,128)S(1)}, u32[]{:S(2)}, u32[]{:S(2)}) collective-permute-start(f32[2,144,128]{2,1,0:T(8,128)S(1)} %get-tuple-element.42), channel_id=1, source_target_pairs={{0,2},{1,3},{2,0},{3,1},{4,6},{5,7},{6,4},{7,5},{8,10},{9,11},{10,... | collective-permute-start | bytes 442376 | tf_op jit(solution)/shard_map/ppermute | solution.py:449
  167.1 7.5 %collective-permute-start.14 = (f32[2,144,128]{2,1,0:T(8,128)S(1)}, f32[2,144,128]{2,1,0:T(8,128)S(1)}, u32[]{:S(2)}, u32[]{:S(2)}) collective-permute-start(f32[2,144,128]{2,1,0:T(8,128)S(1)} %get-tuple-element.43), channel_id=1, source_target_pairs={{0,3},{1,0},{2,1},{3,2},{4,7},{5,4},{6,5},{7,6},{8,11},{9,8},{10,9... | collective-permute-start | bytes 442376 | tf_op jit(solution)/shard_map/ppermute | solution.py:449
  179.3 7.0 %copy-start.2 = (bf16[2,128,128]{2,1,0:T(8,128)(2,1)}, bf16[2,128,128]{2,1,0:T(8,128)(2,1)S(1)}, u32[]{:S(2)}) copy-start(bf16[2,128,128]{2,1,0:T(8,128)(2,1)S(1)} %newton_schulz.3.w0) | copy-start | bytes 196612
  179.3 4.9 %collective-permute-start.15 = (bf16[2,128,128]{2,1,0:T(8,128)(2,1)S(1)}, bf16[2,128,128]{2,1,0:T(8,128)(2,1)S(1)}, u32[]{:S(2)}, u32[]{:S(2)}) collective-permute-start(bf16[2,128,128]{2,1,0:T(8,128)(2,1)S(1)} %newton_schulz.3.w0), channel_id=1, source_target_pairs={{0,1},{1,2},{2,3},{3,0},{4,5},{5,6},{6,7},{7,4},{8,9},{9,10},{10,1... | collective-permute-start | bytes 196616 | tf_op jit(solution)/shard_map/ppermute | solution.py:449
  180.6 5.7 %collective-permute-start.16 = (bf16[2,128,128]{2,1,0:T(8,128)(2,1)S(1)}, bf16[2,128,128]{2,1,0:T(8,128)(2,1)S(1)}, u32[]{:S(2)}, u32[]{:S(2)}) collective-permute-start(bf16[2,128,128]{2,1,0:T(8,128)(2,1)S(1)} %newton_schulz.3.w0), channel_id=1, source_target_pairs={{0,2},{1,3},{2,0},{3,1},{4,6},{5,7},{6,4},{7,5},{8,10},{9,11},{10,... | collective-permute-start | bytes 196616 | tf_op jit(solution)/shard_map/ppermute | solution.py:449
  182.6 3.6 %collective-permute-start.17 = (bf16[2,128,128]{2,1,0:T(8,128)(2,1)S(1)}, bf16[2,128,128]{2,1,0:T(8,128)(2,1)S(1)}, u32[]{:S(2)}, u32[]{:S(2)}) collective-permute-start(bf16[2,128,128]{2,1,0:T(8,128)(2,1)S(1)} %newton_schulz.3.w0), channel_id=1, source_target_pairs={{0,3},{1,0},{2,1},{3,2},{4,7},{5,4},{6,5},{7,6},{8,11},{9,8},{10,9... | collective-permute-start | bytes 196616 | tf_op jit(solution)/shard_map/ppermute | solution.py:449
  184.3 2.0 copy-start.16
  (11 other events, 9.8 us)
where the time goes:
time: 251 us; the launch traced here: 250 us
  Pallas kernels  68.5 us (27%)
  waiting for transfers between devices  64.1 us (26%)
  starting transfers between devices  60.4 us (24%)
  blocking collectives  47 us (19%)
  local copies, waits for them, and re-layouts  8.78 us (3%)
    all_to_all x1, blocking collectives, analyse(): lax.all_to_all(out, 'patch', split_axis=0, concat_axis=0, tiled=True)  47 us
    all_to_all x2, waiting for transfers between devices, body(): lax.all_to_all(sent, 'patch', split_axis=0, concat_axis=0, tiled=True)  32.4 us
    ppermute x18, waiting for transfers between devices, exchange(): lax.ppermute(blocks[d], 'lev', [(i, (i + d) % 4) for i in range(4)])  29.8 us
    ppermute x18, starting transfers between devices, exchange(): lax.ppermute(blocks[d], 'lev', [(i, (i + d) % 4) for i in range(4)])  26.6 us
    pallas_call x2, Pallas kernels, observe(): pl.pallas_call(functools.partial(observe_kernel, first), in_specs=[smem()...  21.6 us
    all_to_all x1, starting transfers between devices, analyse(): lax.all_to_all(out, 'patch', split_axis=0, concat_axis=0, tiled=True)  16.9 us
    all_to_all x2, starting transfers between devices, body(): lax.all_to_all(sent, 'patch', split_axis=0, concat_axis=0, tiled=True)  16.9 us
    pallas_call x2, Pallas kernels, apply(): pl.pallas_call(apply_kernel, in_specs=[smem()] + [vmem()] * 4 + [hbm()] +...  13.4 us
  transfers between devices with their start and end apart: 21, of which 9 were waited for; matrix products, arithmetic and copies ran while one was open for 1% of the time, Pallas kernels for 20%

commit v1 on v0

--- a/solution.py
+++ b/solution.py
@@ -113,7 +113,7 @@
             pltpu.SemaphoreType.DMA((fields,)),
             pltpu.SemaphoreType.DMA((fields,)),
         ],
-        compiler_params=params(58),
+        compiler_params=params(62),
         cost_estimate=cost(5),
         name="send_permute",
     )(order, x)
@@ -148,10 +148,8 @@
     mean_ref[...] = jnp.zeros_like(mean_ref)
     for f in range(fields):
         loads[f].wait()
-        for b in range(groups // gather):
-            block = recv_buf[f, b * gather : (b + 1) * gather].reshape(gather * rows, cols)
-            moved = dot(perm, block).astype(BF16).reshape(slots, part, cols)
-            x_buf[f, :, b * part : (b + 1) * part, :] = moved
+        block = recv_buf[f].astype(F32).reshape(members, slots, cols)
+        x_buf[f] = jnp.transpose(block, (1, 0, 2)).astype(BF16)
         stores[f].start()
     wait(small)
 
@@ -178,18 +176,41 @@
     def slot_step(s, base):
         count = counts_ref[first + s]
 
+        def observed(one, two):
+            table = jnp.concatenate([table_of(begin + one), table_of(begin + two)], axis=1)
+            x = jnp.concatenate([x_buf[f, s] for f in range(fields)], axis=1)
+            y = dot(x, table)
+            return y, jnp.mean(y, axis=0, keepdims=True)
+
+        def store_both(one, two, result):
+            y, mean = result
+            store(one, y[:, :TILE], mean[:, :TILE])
+            store(two, y[:, TILE:], mean[:, TILE:])
+
+        def quad_step(i, carry):
+            one = base + 4 * i
+            results = observed(one, one + 1), observed(one + 2, one + 3)
+            store_both(one, one + 1, results[0])
+            store_both(one + 2, one + 3, results[1])
+            return carry
+
+        def oct_step(i, carry):
+            ones = [base + 8 * i + 2 * n for n in range(4)]
+            results = [observed(one, one + 1) for one in ones]
+            for one, result in zip(ones, results):
+                store_both(one, one + 1, result)
+            return carry
+
         def pair_step(i, carry):
             one = base + 2 * i
             two = jnp.minimum(one + 1, base + count - 1)
-            table = jnp.concatenate([table_of(begin + one), table_of(begin + two)], axis=1)
-            x = jnp.concatenate([x_buf[f, s] for f in range(fields)], axis=1)
-            y = dot(x, table)
-            mean = jnp.mean(y, axis=0, keepdims=True)
-            store(one, y[:, :TILE], mean[:, :TILE])
-            store(two, y[:, TILE:], mean[:, TILE:])
+            store_both(one, two, observed(one, two))
             return carry
 
-        lax.fori_loop(0, lax.div(count + 1, 2), pair_step, 0)
+        octs, quads = lax.div(count, 8), lax.div(count, 4)
+        lax.fori_loop(0, octs, oct_step, 0)
+        lax.fori_loop(2 * octs, quads, quad_step, 0)
+        lax.fori_loop(2 * quads, lax.div(count + 1, 2), pair_step, 0)
         return base + count
 
     lax.fori_loop(0, slots, slot_step, jnp.int32(0))
@@ -205,7 +226,7 @@
     wait(stores)
 
 
-def observe(counts, lev, recv, op, col, first, slots, tiles, us, after):
+def observe(counts, lev, recv, op, col, first, slots, tiles, us, mib, after):
     groups, fields, rows, cols = recv.shape
     members = groups * rows // slots
     length = tiles // 4 * members + 48
@@ -228,7 +249,7 @@
             pltpu.SemaphoreType.DMA,
             pltpu.SemaphoreType.DMA((4,)),
         ],
-        compiler_params=params(58),
+        compiler_params=params(mib),
         cost_estimate=cost(us),
         name="observe",
     )(counts, lev, recv, op, col, *after)
@@ -359,16 +380,14 @@
                 x = x_buf[f, owned + s].astype(F32)
                 mean = jnp.mean(x, axis=0, keepdims=True)
                 mixed = dot(w_ref[s], (x - mean).astype(BF16))
-                mixed_ref[owned + s] = (mean + mixed).astype(BF16)
-        for b in range(groups // gather):
-            block = mixed_ref[:, b * part : (b + 1) * part, :].reshape(slots * part, cols)
-            moved = dot(perm, block).astype(BF16).reshape(gather, rows, cols)
-            out_buf[f, b * gather : (b + 1) * gather] = moved
+                mixed_ref[owned + s] = mean + mixed
+        moved = jnp.transpose(mixed_ref[...], (1, 0, 2)).reshape(groups, rows, cols)
+        out_buf[f] = moved.astype(BF16)
         stores[f].start()
     wait(stores)
 
 
-def apply(lev, ws, x, groups, us, after):
+def apply(lev, ws, x, groups, us, mib, after):
     fields, slots, members, cols = x.shape
     rows = slots * members // groups
     return pl.pallas_call(
@@ -378,12 +397,12 @@
         out_shape=jax.ShapeDtypeStruct((groups, fields, rows, cols), BF16),
         scratch_shapes=[
             pltpu.VMEM((fields, slots, members, cols), BF16),
-            pltpu.VMEM((slots, members, cols), BF16),
+            pltpu.VMEM((slots, members, cols), F32),
             pltpu.VMEM((fields, groups, rows, cols), BF16),
             pltpu.SemaphoreType.DMA((fields,)),
             pltpu.SemaphoreType.DMA((fields,)),
         ],
-        compiler_params=params(58),
+        compiler_params=params(mib),
         cost_estimate=cost(us),
         name="apply_weights",
     )(lev, *ws, x, *after)
@@ -438,7 +457,7 @@
             pltpu.SemaphoreType.DMA((fields, len(recvs))),
             pltpu.SemaphoreType.DMA((fields,)),
         ],
-        compiler_params=params(58),
+        compiler_params=params(62),
         cost_estimate=cost(6),
         name="restore_order",
     )(order, *recvs)
@@ -481,26 +500,26 @@
     def see(c, us, after):
         slots, first, recv = chunks[c]
         room = tiles - (slots_dev - slots)
-        x, *ys = observe(tile_counts, lev, recv, op, col, first, slots, room, us, after)
+        x, *ys = observe(tile_counts, lev, recv, op, col, first, slots, room, us, (62, 62)[c], after)
         return x, ys
 
     def weigh(c, ys, us, after):
         slots, first, _ = chunks[c]
         return partial_gram(tile_counts, lev, ys, value, weight, first, slots, members, us, after)
 
-    def analyse(x, w, us, after):
-        out = apply(lev, exchange([w] * 4), x, groups, us, after)
+    def analyse(x, w, us, mib, after):
+        out = apply(lev, exchange([w] * 4), x, groups, us, mib, after)
         return out, lax.all_to_all(out, "patch", split_axis=0, concat_axis=0, tiled=True)
 
     members = members_local * groups
-    x0, ys0 = see(0, 200, [sent])
-    gs0 = weigh(0, exchange(ys0), 1, [])
-    x1, ys1 = see(1, 20, [gs0[0]])
-    w0 = solve(exchange(gs0), 7, [ys1[0]])
-    out0, back0 = analyse(x0, w0, 100, [])
+    x0, ys0 = see(0, 1, [sent])
+    gs0 = weigh(0, exchange(ys0), 200, [])
+    w0 = solve(exchange(gs0), 7, [])
+    x1, ys1 = see(1, 20, [w0])
+    out0, back0 = analyse(x0, w0, 100, 62, [ys1[0]])
     gs1 = weigh(1, exchange(ys1), 200, [out0])
     w1 = solve(exchange(gs1), 1, [])
-    _, back1 = analyse(x1, w1, 1, [])
+    _, back1 = analyse(x1, w1, 1, 62, [])
     backs = [back0, back1]
 
     result = restore(order, backs, members_local)

time: 251 us -> 241 us (0.960)
  waiting for transfers between devices: 64.1 us -> 73.9 us
  starting transfers between devices: 60.4 us -> 50.6 us
  Pallas kernels: 68.5 us -> 63.9 us
  local copies, waits for them, and re-layouts: 8.78 us -> 4.42 us
    all_to_all x2, waiting for transfers between devices: 32.4 us -> 43 us  [body(): lax.all_to_all(sent, 'patch', split_axis=0, concat_axis=0, tiled=True)]
    all_to_all x1, starting transfers between devices: 16.9 us -> 7.01 us  [analyse(): lax.all_to_all(out, 'patch', split_axis=0, concat_axis=0, tiled=True)]
    unnamed x44 -> x36, local copies, waits for them, and re-layouts: 8.2 us -> 3.84 us
    pallas_call x2, Pallas kernels: 21.6 us -> 17.8 us  [observe(): pl.pallas_call(functools.partial(observe_kernel, first), in_specs=[smem()...]
    all_to_all x2, starting transfers between devices: 16.9 us -> 19.7 us  [body(): lax.all_to_all(sent, 'patch', split_axis=0, concat_axis=0, tiled=True)]
    ppermute x18, starting transfers between devices: 26.6 us -> 23.9 us  [exchange(): lax.ppermute(blocks[d], 'lev', [(i, (i + d) % 4) for i in range(4)])]
  transfers between devices with their start and end apart: 21 -> 21, of which waited for: 9 -> 13; matrix products, arithmetic and copies ran while one was open for 1% -> 1% of each run, Pallas kernels for 20% -> 17%
where the time goes in v1:
time: 241 us; the launch traced here: 242 us
  waiting for transfers between devices  73.9 us (31%)
  Pallas kernels  63.9 us (27%)
  starting transfers between devices  50.6 us (21%)
  blocking collectives  48.3 us (20%)
  local copies, waits for them, and re-layouts  4.42 us (2%)
    all_to_all x1, blocking collectives, analyse(): lax.all_to_all(out, 'patch', split_axis=0, concat_axis=0, tiled=True)  48.3 us
    all_to_all x2, waiting for transfers between devices, body(): lax.all_to_all(sent, 'patch', split_axis=0, concat_axis=0, tiled=True)  43 us
    ppermute x18, waiting for transfers between devices, exchange(): lax.ppermute(blocks[d], 'lev', [(i, (i + d) % 4) for i in range(4)])  30.9 us
    ppermute x18, starting transfers between devices, exchange(): lax.ppermute(blocks[d], 'lev', [(i, (i + d) % 4) for i in range(4)])  23.9 us
    all_to_all x2, starting transfers between devices, body(): lax.all_to_all(sent, 'patch', split_axis=0, concat_axis=0, tiled=True)  19.7 us
    pallas_call x2, Pallas kernels, observe(): pl.pallas_call(functools.partial(observe_kernel, first), in_specs=[smem()...  17.8 us
    pallas_call x2, Pallas kernels, apply(): pl.pallas_call(apply_kernel, in_specs=[smem()] + [vmem()] * 4 + [hbm()] +...  12.3 us
    pallas_call x2, Pallas kernels, send(): pl.pallas_call(functools.partial(send_kernel, first), in_specs=[vmem(), h...  11 us
  transfers between devices with their start and end apart: 21, of which 13 were waited for; matrix products, arithmetic and copies ran while one was open for 1% of the time, Pallas kernels for 17%

profile of v1, /device:TPU:1, one launch (start us, length us, event | category | flops | bytes accessed | tf_op | source)
XLA Modules:
  0.0 242.4 jit_solution(16962182082976428560)
XLA Ops:
  0.0 5.5 %send_permute.2 = bf16[32,6,32,256]{3,2,1,0:T(8,128)(2,1)} custom-call(s32[1,512]{1,0:T(1,128)} %bitcast.25, bf16[4,6,512,256]{3,2,1,0:T(8,128)(2,1)} %bitcast.23), custom_call_target="tpu_custom_call" | custom-call | flops 5750000128 | tf_op jit(solution)/shard_map/send_permute/pallas_call | solution.py:105
  5.5 9.7 %all-to-all-start = ((bf16[32,6,32,256]{3,2,1,0:T(8,128)(2,1)}), bf16[32,6,32,256]{3,2,1,0:T(8,128)(2,1)}, u32[]{:S(2)}, u32[]{:S(2)}) async-start(bf16[32,6,32,256]{3,2,1,0:T(8,128)(2,1)} %send_permute.2), calls=%async_computation | async-start | bytes 6291456 | tf_op jit(solution)/shard_map/all_to_all | solution.py:494
  16.5 5.5 %send_permute.3.rest_0_ = bf16[32,6,32,256]{3,2,1,0:T(8,128)(2,1)} custom-call(s32[1,512]{1,0:T(1,128)} %bitcast.26, bf16[4,6,512,256]{3,2,1,0:T(8,128)(2,1)} %bitcast.24), custom_call_target="tpu_custom_call" | custom-call | flops 5750000128 | tf_op jit(solution)/shard_map/send_permute/pallas_call | solution.py:105
  22.0 32.4 %all-to-all-done.recv_ref = bf16[32,6,32,256]{3,2,1,0:T(8,128)(2,1)} async-done(((bf16[32,6,32,256]{3,2,1,0:T(8,128)(2,1)}), bf16[32,6,32,256]{3,2,1,0:T(8,128)(2,1)}, u32[]{:S(2)}, u32[]{:S(2)}) %all-to-all-start) | async-done | bytes 3145760 | tf_op jit(solution)/shard_map/all_to_all | solution.py:494
  54.4 9.4 %observe.2 = (bf16[6,8,128,256]{3,2,1,0:T(8,128)(2,1)}, bf16[1840,128]{1,0:T(8,128)(2,1)}, bf16[1840,128]{1,0:T(8,128)(2,1)}, bf16[1840,128]{1,0:T(8,128)(2,1)}, bf16[1840,128]{1,0:T(8,128)(2,1)}) custom-call(s32[16]{0:T(128)} %counts_ref.7, s32[1]{0:T(128)} %bitcast.2.lev_ref, bf16[32,6,32,256]{3,2,1,0:T(8,128)(2,1)} %all-to-all-done.recv_ref, ...), custom_call_target="tpu_custom_call" | custom-call | flops 1150000000 | tf_op jit(solution)/shard_map/observe/pallas_call | solution.py:233
  65.1 2.5 %collective-permute-start.1 = (bf16[1840,128]{1,0:T(8,128)(2,1)}, bf16[1840,128]{1,0:T(8,128)(2,1)S(1)}, u32[]{:S(2)}, u32[]{:S(2)}) collective-permute-start(bf16[1840,128]{1,0:T(8,128)(2,1)} %get-tuple-element.29), channel_id=1, source_target_pairs={{0,2},{1,3},{2,0},{3,1},{4,6},{5,7},{6,4},{7,5},{8,10},{9,11},{10,... | collective-permute-start | bytes 1413128 | tf_op jit(solution)/shard_map/ppermute | solution.py:468
  68.8 10.0 %all-to-all-start.1 = ((bf16[32,6,32,256]{3,2,1,0:T(8,128)(2,1)}), bf16[32,6,32,256]{3,2,1,0:T(8,128)(2,1)}, u32[]{:S(2)}, u32[]{:S(2)}) async-start(bf16[32,6,32,256]{3,2,1,0:T(8,128)(2,1)} %send_permute.3.rest_0_), calls=%async_computation.1 | async-start | bytes 6291456 | tf_op jit(solution)/shard_map/all_to_all | solution.py:494
  78.8 4.7 %collective-permute-done.1.y2 = bf16[1840,128]{1,0:T(8,128)(2,1)S(1)} collective-permute-done((bf16[1840,128]{1,0:T(8,128)(2,1)}, bf16[1840,128]{1,0:T(8,128)(2,1)S(1)}, u32[]{:S(2)}, u32[]{:S(2)}) %collective-permute-start.1) | collective-permute-done | bytes 471072 | tf_op jit(solution)/shard_map/ppermute | solution.py:468
  83.5 2.7 %collective-permute-done.2.y3 = bf16[1840,128]{1,0:T(8,128)(2,1)S(1)} collective-permute-done((bf16[1840,128]{1,0:T(8,128)(2,1)}, bf16[1840,128]{1,0:T(8,128)(2,1)S(1)}, u32[]{:S(2)}, u32[]{:S(2)}) %collective-permute-start.2) | collective-permute-done | bytes 471072 | tf_op jit(solution)/shard_map/ppermute | solution.py:468
  86.2 2.8 %gram.2 = (f32[2,144,128]{2,1,0:T(8,128)S(1)}, f32[2,144,128]{2,1,0:T(8,128)S(1)}, f32[2,144,128]{2,1,0:T(8,128)S(1)}, f32[2,144,128]{2,1,0:T(8,128)S(1)}) custom-call(s32[16]{0:T(128)S(1)} %copy-done.3, s32[1]{0:T(128)} %bitcast.2.lev_ref, bf16[1840,128]{1,0:T(8,128)(2,1)S(1)} %copy-done.5, bf16[1840,128]{1,0:T(8,128)(2,1)S(1)} %collective-permute-done.y1, ...), custom_call_target="tpu_custom_call" | custom-call | flops 230000001024 | tf_op jit(solution)/shard_map/gram/pallas_call | solution.py:296
  89.0 3.5 %collective-permute-start.3 = (f32[2,144,128]{2,1,0:T(8,128)S(1)}, f32[2,144,128]{2,1,0:T(8,128)S(1)}, u32[]{:S(2)}, u32[]{:S(2)}) collective-permute-start(f32[2,144,128]{2,1,0:T(8,128)S(1)} %get-tuple-element.32), channel_id=1, source_target_pairs={{0,1},{1,2},{2,3},{3,0},{4,5},{5,6},{6,7},{7,4},{8,9},{9,10},{10,1... | collective-permute-start | bytes 442376 | tf_op jit(solution)/shard_map/ppermute | solution.py:468
  95.4 3.0 %collective-permute-done.4.g2 = f32[2,144,128]{2,1,0:T(8,128)S(1)} collective-permute-done((f32[2,144,128]{2,1,0:T(8,128)S(1)}, f32[2,144,128]{2,1,0:T(8,128)S(1)}, u32[]{:S(2)}, u32[]{:S(2)}) %collective-permute-start.4) | collective-permute-done | bytes 147488 | tf_op jit(solution)/shard_map/ppermute | solution.py:468
  98.4 4.7 %newton_schulz.2.rest_0_.w0 = bf16[2,128,128]{2,1,0:T(8,128)(2,1)S(1)} custom-call(f32[2,144,128]{2,1,0:T(8,128)S(1)} %get-tuple-element.31.g0, f32[2,144,128]{2,1,0:T(8,128)S(1)} %collective-permute-done.3.g1, f32[2,144,128]{2,1,0:T(8,128)S(1)} %collective-permute-done.4.g2, f32[2,144,128]{2,1,0:T(8,128)S(1)} %collective-permute-done.5.g3), custom_call_target="tpu_custom_call" | custom-call | flops 8049999872 | tf_op jit(solution)/shard_map/newton_schulz/pallas_call | solution.py:347
  103.1 1.3 collective-permute-start.6
  104.4 2.1 collective-permute-start.7
  107.5 10.6 %all-to-all-done.1.recv_ref = bf16[32,6,32,256]{3,2,1,0:T(8,128)(2,1)} async-done(((bf16[32,6,32,256]{3,2,1,0:T(8,128)(2,1)}), bf16[32,6,32,256]{3,2,1,0:T(8,128)(2,1)}, u32[]{:S(2)}, u32[]{:S(2)}) %all-to-all-start.1) | async-done | bytes 3145760 | tf_op jit(solution)/shard_map/all_to_all | solution.py:494
  118.1 8.4 %observe.3 = (bf16[6,8,128,256]{3,2,1,0:T(8,128)(2,1)}, bf16[1840,128]{1,0:T(8,128)(2,1)}, bf16[1840,128]{1,0:T(8,128)(2,1)}, bf16[1840,128]{1,0:T(8,128)(2,1)}, bf16[1840,128]{1,0:T(8,128)(2,1)}) custom-call(s32[16]{0:T(128)} %counts_ref.7, s32[1]{0:T(128)} %bitcast.2.lev_ref, bf16[32,6,32,256]{3,2,1,0:T(8,128)(2,1)} %all-to-all-done.1.recv_ref, ...), custom_call_target="tpu_custom_call" | custom-call | flops 23000000512 | tf_op jit(solution)/shard_map/observe/pallas_call | solution.py:233
  126.8 2.5 %collective-permute-start.11 = (bf16[1840,128]{1,0:T(8,128)(2,1)}, bf16[1840,128]{1,0:T(8,128)(2,1)}, u32[]{:S(2)}, u32[]{:S(2)}) collective-permute-start(bf16[1840,128]{1,0:T(8,128)(2,1)} %get-tuple-element.39), channel_id=1, source_target_pairs={{0,3},{1,0},{2,1},{3,2},{4,7},{5,4},{6,5},{7,6},{8,11},{9,8},{10,9... | collective-permute-start | bytes 1413128 | tf_op jit(solution)/shard_map/ppermute | solution.py:468
  130.0 6.2 %apply_weights.2.rest_0_ = bf16[32,6,32,256]{3,2,1,0:T(8,128)(2,1)} custom-call(s32[1]{0:T(128)} %bitcast.2.lev_ref, bf16[2,128,128]{2,1,0:T(8,128)(2,1)} %copy-done.6, bf16[2,128,128]{2,1,0:T(8,128)(2,1)} %copy-done.15, bf16[2,128,128]{2,1,0:T(8,128)(2,1)} %copy-done.16, bf16[2,128,128]{2,1,0:T(8,128)(2,1)} %copy-done.17, ...), custom_call_target="tpu_custom_call" | custom-call | flops 115000000512 | tf_op jit(solution)/shard_map/apply_weights/pallas_call | solution.py:393
  136.2 7.0 %all-to-all-start.2 = ((bf16[32,6,32,256]{3,2,1,0:T(8,128)(2,1)}), bf16[32,6,32,256]{3,2,1,0:T(8,128)(2,1)}, u32[]{:S(2)}, u32[]{:S(2)}) async-start(bf16[32,6,32,256]{3,2,1,0:T(8,128)(2,1)} %apply_weights.2.rest_0_), calls=%async_computation.2 | async-start | bytes 6291456 | tf_op jit(solution)/shard_map/all_to_all | solution.py:512
  143.3 4.4 %collective-permute-done.11.y3 = bf16[1840,128]{1,0:T(8,128)(2,1)} collective-permute-done((bf16[1840,128]{1,0:T(8,128)(2,1)}, bf16[1840,128]{1,0:T(8,128)(2,1)}, u32[]{:S(2)}, u32[]{:S(2)}) %collective-permute-start.11) | collective-permute-done | bytes 471072 | tf_op jit(solution)/shard_map/ppermute | solution.py:468
  147.7 3.5 %collective-permute-done.9.y1 = bf16[1840,128]{1,0:T(8,128)(2,1)} collective-permute-done((bf16[1840,128]{1,0:T(8,128)(2,1)}, bf16[1840,128]{1,0:T(8,128)(2,1)}, u32[]{:S(2)}, u32[]{:S(2)}) %collective-permute-start.9) | collective-permute-done | bytes 471072 | tf_op jit(solution)/shard_map/ppermute | solution.py:468
  153.8 3.3 %gram.3 = (f32[2,144,128]{2,1,0:T(8,128)S(1)}, f32[2,144,128]{2,1,0:T(8,128)S(1)}, f32[2,144,128]{2,1,0:T(8,128)S(1)}, f32[2,144,128]{2,1,0:T(8,128)S(1)}) custom-call(s32[16]{0:T(128)S(1)} %copy-done.4, s32[1]{0:T(128)} %bitcast.2.lev_ref, bf16[1840,128]{1,0:T(8,128)(2,1)S(1)} %copy-done.11, bf16[1840,128]{1,0:T(8,128)(2,1)} %collective-permute-done.9.y1, ...), custom_call_target="tpu_custom_call" | custom-call | flops 230000001024 | tf_op jit(solution)/shard_map/gram/pallas_call | solution.py:296
  158.0 1.8 collective-permute-start.14
  159.8 7.5 %collective-permute-done.12.g1 = f32[2,144,128]{2,1,0:T(8,128)S(1)} collective-permute-done((f32[2,144,128]{2,1,0:T(8,128)S(1)}, f32[2,144,128]{2,1,0:T(8,128)S(1)}, u32[]{:S(2)}, u32[]{:S(2)}) %collective-permute-start.12) | collective-permute-done | bytes 147488 | tf_op jit(solution)/shard_map/ppermute | solution.py:468
  168.0 4.7 %newton_schulz.3.w0 = bf16[2,128,128]{2,1,0:T(8,128)(2,1)S(1)} custom-call(f32[2,144,128]{2,1,0:T(8,128)S(1)} %get-tuple-element.40.g0, f32[2,144,128]{2,1,0:T(8,128)S(1)} %collective-permute-done.12.g1, f32[2,144,128]{2,1,0:T(8,128)S(1)} %collective-permute-done.13.g2, f32[2,144,128]{2,1,0:T(8,128)S(1)} %collective-permute-done.14.g3), custom_call_target="tpu_custom_call" | custom-call | flops 1150000000 | tf_op jit(solution)/shard_map/newton_schulz/pallas_call | solution.py:347
  172.8 3.0 %collective-permute-start.16 = (bf16[2,128,128]{2,1,0:T(8,128)(2,1)S(1)}, bf16[2,128,128]{2,1,0:T(8,128)(2,1)S(1)}, u32[]{:S(2)}, u32[]{:S(2)}) collective-permute-start(bf16[2,128,128]{2,1,0:T(8,128)(2,1)S(1)} %newton_schulz.3.w0), channel_id=1, source_target_pairs={{0,2},{1,3},{2,0},{3,1},{4,6},{5,7},{6,4},{7,5},{8,10},{9,11},{10,... | collective-permute-start | bytes 196616 | tf_op jit(solution)/shard_map/ppermute | solution.py:468
  175.7 1.7 collective-permute-done.15.w1
  177.5 1.3 collective-permute-done.16.w2
  180.4 6.1 %apply_weights.3 = bf16[32,6,32,256]{3,2,1,0:T(8,128)(2,1)} custom-call(s32[1]{0:T(128)} %bitcast.2.lev_ref, bf16[2,128,128]{2,1,0:T(8,128)(2,1)} %copy-done.2, bf16[2,128,128]{2,1,0:T(8,128)(2,1)} %copy-done.12, bf16[2,128,128]{2,1,0:T(8,128)(2,1)} %copy-done.13, bf16[2,128,128]{2,1,0:T(8,128)(2,1)} %copy-done.14, ...), custom_call_target="tpu_custom_call" | custom-call | flops 1150000000 | tf_op jit(solution)/shard_map/apply_weights/pallas_call | solution.py:393
  186.5 48.3 %all_to_all.20.refs_1_ = bf16[32,6,32,256]{3,2,1,0:T(8,128)(2,1)} all-to-all(bf16[32,6,32,256]{3,2,1,0:T(8,128)(2,1)} %apply_weights.3), channel_id=1, replica_groups=mesh['patch'=32,'lev'=4] {'patch'}, dimensions={0} | all-to-all | bytes 6291456 | tf_op jit(solution)/shard_map/all_to_all | solution.py:512
  234.8 7.3 %restore_order.1 = bf16[4,6,512,256]{3,2,1,0:T(8,128)(2,1)} custom-call(s32[1,512]{1,0:T(1,128)} %bitcast.27, bf16[32,6,32,256]{3,2,1,0:T(8,128)(2,1)} %all-to-all-done.2.refs_0_, bf16[32,6,32,256]{3,2,1,0:T(8,128)(2,1)} %all_to_all.20.refs_1_), custom_call_target="tpu_custom_call" | custom-call | flops 6899999744 | tf_op jit(solution)/shard_map/restore_order/pallas_call | solution.py:447
  (60 shorter events, 14.6 us)
Async XLA Ops:
  0.0 15.2 %copy-start = (bf16[4,6,8192]{2,0,1:T(4,128)(2,1)S(1)}, bf16[4,6,8192]{2,0,1:T(4,128)(2,1)}, u32[]{:S(2)}) copy-start(bf16[4,6,8192]{2,0,1:T(4,128)(2,1)} %param.11) | copy-start | bytes 1179652
  5.5 48.9 %all-to-all-start = ((bf16[32,6,32,256]{3,2,1,0:T(8,128)(2,1)}), bf16[32,6,32,256]{3,2,1,0:T(8,128)(2,1)}, u32[]{:S(2)}, u32[]{:S(2)}) async-start(bf16[32,6,32,256]{3,2,1,0:T(8,128)(2,1)} %send_permute.2), calls=%async_computation | async-start | bytes 6291456 | tf_op jit(solution)/shard_map/all_to_all | solution.py:494
  63.8 15.0 %collective-permute-start = (bf16[1840,128]{1,0:T(8,128)(2,1)}, bf16[1840,128]{1,0:T(8,128)(2,1)S(1)}, u32[]{:S(2)}, u32[]{:S(2)}) collective-permute-start(bf16[1840,128]{1,0:T(8,128)(2,1)} %get-tuple-element.28), channel_id=1, source_target_pairs={{0,1},{1,2},{2,3},{3,0},{4,5},{5,6},{6,7},{7,4},{8,9},{9,10},{10,1... | collective-permute-start | bytes 1413128 | tf_op jit(solution)/shard_map/ppermute | solution.py:468
  65.1 18.5 %collective-permute-start.1 = (bf16[1840,128]{1,0:T(8,128)(2,1)}, bf16[1840,128]{1,0:T(8,128)(2,1)S(1)}, u32[]{:S(2)}, u32[]{:S(2)}) collective-permute-start(bf16[1840,128]{1,0:T(8,128)(2,1)} %get-tuple-element.29), channel_id=1, source_target_pairs={{0,2},{1,3},{2,0},{3,1},{4,6},{5,7},{6,4},{7,5},{8,10},{9,11},{10,... | collective-permute-start | bytes 1413128 | tf_op jit(solution)/shard_map/ppermute | solution.py:468
  67.5 18.7 %copy-start.3 = (s32[16]{0:T(128)S(1)}, s32[16]{0:T(128)}, u32[]{:S(2)}) copy-start(s32[16]{0:T(128)} %counts_ref.7) | copy-start | bytes 196
  67.5 18.7 %copy-start.5 = (bf16[1840,128]{1,0:T(8,128)(2,1)S(1)}, bf16[1840,128]{1,0:T(8,128)(2,1)}, u32[]{:S(2)}) copy-start(bf16[1840,128]{1,0:T(8,128)(2,1)} %get-tuple-element.27.y0) | copy-start | bytes 1413124
  67.5 18.7 %copy-start.7 = (f32[8192]{0:T(1024)S(1)}, f32[8192]{0:T(1024)}, u32[]{:S(2)}) copy-start(f32[8192]{0:T(1024)} %param.12) | copy-start | bytes 98308
  67.5 18.7 %copy-start.9 = (f32[8192]{0:T(1024)S(1)}, f32[8192]{0:T(1024)}, u32[]{:S(2)}) copy-start(f32[8192]{0:T(1024)} %param.13) | copy-start | bytes 98308
  67.5 18.7 %collective-permute-start.2 = (bf16[1840,128]{1,0:T(8,128)(2,1)}, bf16[1840,128]{1,0:T(8,128)(2,1)S(1)}, u32[]{:S(2)}, u32[]{:S(2)}) collective-permute-start(bf16[1840,128]{1,0:T(8,128)(2,1)} %get-tuple-element.30), channel_id=1, source_target_pairs={{0,3},{1,0},{2,1},{3,2},{4,7},{5,4},{6,5},{7,6},{8,11},{9,8},{10,9... | collective-permute-start | bytes 1413128 | tf_op jit(solution)/shard_map/ppermute | solution.py:468
  68.8 49.4 %all-to-all-start.1 = ((bf16[32,6,32,256]{3,2,1,0:T(8,128)(2,1)}), bf16[32,6,32,256]{3,2,1,0:T(8,128)(2,1)}, u32[]{:S(2)}, u32[]{:S(2)}) async-start(bf16[32,6,32,256]{3,2,1,0:T(8,128)(2,1)} %send_permute.3.rest_0_), calls=%async_computation.1 | async-start | bytes 6291456 | tf_op jit(solution)/shard_map/all_to_all | solution.py:494
  89.0 6.4 %collective-permute-start.3 = (f32[2,144,128]{2,1,0:T(8,128)S(1)}, f32[2,144,128]{2,1,0:T(8,128)S(1)}, u32[]{:S(2)}, u32[]{:S(2)}) collective-permute-start(f32[2,144,128]{2,1,0:T(8,128)S(1)} %get-tuple-element.32), channel_id=1, source_target_pairs={{0,1},{1,2},{2,3},{3,0},{4,5},{5,6},{6,7},{7,4},{8,9},{9,10},{10,1... | collective-permute-start | bytes 442376 | tf_op jit(solution)/shard_map/ppermute | solution.py:468
  92.5 5.9 %collective-permute-start.4 = (f32[2,144,128]{2,1,0:T(8,128)S(1)}, f32[2,144,128]{2,1,0:T(8,128)S(1)}, u32[]{:S(2)}, u32[]{:S(2)}) collective-permute-start(f32[2,144,128]{2,1,0:T(8,128)S(1)} %get-tuple-element.33), channel_id=1, source_target_pairs={{0,2},{1,3},{2,0},{3,1},{4,6},{5,7},{6,4},{7,5},{8,10},{9,11},{10,... | collective-permute-start | bytes 442376 | tf_op jit(solution)/shard_map/ppermute | solution.py:468
  93.7 4.7 %collective-permute-start.5 = (f32[2,144,128]{2,1,0:T(8,128)S(1)}, f32[2,144,128]{2,1,0:T(8,128)S(1)}, u32[]{:S(2)}, u32[]{:S(2)}) collective-permute-start(f32[2,144,128]{2,1,0:T(8,128)S(1)} %get-tuple-element.34), channel_id=1, source_target_pairs={{0,3},{1,0},{2,1},{3,2},{4,7},{5,4},{6,5},{7,6},{8,11},{9,8},{10,9... | collective-permute-start | bytes 442376 | tf_op jit(solution)/shard_map/ppermute | solution.py:468
  103.1 15.1 %copy-start.6 = (bf16[2,128,128]{2,1,0:T(8,128)(2,1)}, bf16[2,128,128]{2,1,0:T(8,128)(2,1)S(1)}, u32[]{:S(2)}) copy-start(bf16[2,128,128]{2,1,0:T(8,128)(2,1)S(1)} %newton_schulz.2.rest_0_.w0) | copy-start | bytes 196612
  103.1 26.3 %collective-permute-start.6 = (bf16[2,128,128]{2,1,0:T(8,128)(2,1)S(1)}, bf16[2,128,128]{2,1,0:T(8,128)(2,1)S(1)}, u32[]{:S(2)}, u32[]{:S(2)}) collective-permute-start(bf16[2,128,128]{2,1,0:T(8,128)(2,1)S(1)} %newton_schulz.2.rest_0_.w0), channel_id=1, source_target_pairs={{0,1},{1,2},{2,3},{3,0},{4,5},{5,6},{6,7},{7,4},{8,9},{9,10},{10,1... | collective-permute-start | bytes 196616 | tf_op jit(solution)/shard_map/ppermute | solution.py:468
  104.4 25.0 %collective-permute-start.7 = (bf16[2,128,128]{2,1,0:T(8,128)(2,1)S(1)}, bf16[2,128,128]{2,1,0:T(8,128)(2,1)S(1)}, u32[]{:S(2)}, u32[]{:S(2)}) collective-permute-start(bf16[2,128,128]{2,1,0:T(8,128)(2,1)S(1)} %newton_schulz.2.rest_0_.w0), channel_id=1, source_target_pairs={{0,2},{1,3},{2,0},{3,1},{4,6},{5,7},{6,4},{7,5},{8,10},{9,11},{10,... | collective-permute-start | bytes 196616 | tf_op jit(solution)/shard_map/ppermute | solution.py:468
  106.5 22.9 %collective-permute-start.8 = (bf16[2,128,128]{2,1,0:T(8,128)(2,1)S(1)}, bf16[2,128,128]{2,1,0:T(8,128)(2,1)S(1)}, u32[]{:S(2)}, u32[]{:S(2)}) collective-permute-start(bf16[2,128,128]{2,1,0:T(8,128)(2,1)S(1)} %newton_schulz.2.rest_0_.w0), channel_id=1, source_target_pairs={{0,3},{1,0},{2,1},{3,2},{4,7},{5,4},{6,5},{7,6},{8,11},{9,8},{10,9... | collective-permute-start | bytes 196616 | tf_op jit(solution)/shard_map/ppermute | solution.py:468
  126.5 16.7 %collective-permute-start.10 = (bf16[1840,128]{1,0:T(8,128)(2,1)}, bf16[1840,128]{1,0:T(8,128)(2,1)}, u32[]{:S(2)}, u32[]{:S(2)}) collective-permute-start(bf16[1840,128]{1,0:T(8,128)(2,1)} %get-tuple-element.38), channel_id=1, source_target_pairs={{0,2},{1,3},{2,0},{3,1},{4,6},{5,7},{6,4},{7,5},{8,10},{9,11},{10,... | collective-permute-start | bytes 1413128 | tf_op jit(solution)/shard_map/ppermute | solution.py:468
  126.8 20.8 %collective-permute-start.11 = (bf16[1840,128]{1,0:T(8,128)(2,1)}, bf16[1840,128]{1,0:T(8,128)(2,1)}, u32[]{:S(2)}, u32[]{:S(2)}) collective-permute-start(bf16[1840,128]{1,0:T(8,128)(2,1)} %get-tuple-element.39), channel_id=1, source_target_pairs={{0,3},{1,0},{2,1},{3,2},{4,7},{5,4},{6,5},{7,6},{8,11},{9,8},{10,9... | collective-permute-start | bytes 1413128 | tf_op jit(solution)/shard_map/ppermute | solution.py:468
  129.3 21.9 %collective-permute-start.9 = (bf16[1840,128]{1,0:T(8,128)(2,1)}, bf16[1840,128]{1,0:T(8,128)(2,1)}, u32[]{:S(2)}, u32[]{:S(2)}) collective-permute-start(bf16[1840,128]{1,0:T(8,128)(2,1)} %get-tuple-element.37), channel_id=1, source_target_pairs={{0,1},{1,2},{2,3},{3,0},{4,5},{5,6},{6,7},{7,4},{8,9},{9,10},{10,1... | collective-permute-start | bytes 1413128 | tf_op jit(solution)/shard_map/ppermute | solution.py:468
  136.2 15.0 %copy-start.1 = (bf16[32,6,32,256]{3,2,1,0:T(8,128)(2,1)S(1)}, bf16[32,6,32,256]{3,2,1,0:T(8,128)(2,1)}, u32[]{:S(2)}) copy-start(bf16[32,6,32,256]{3,2,1,0:T(8,128)(2,1)} %apply_weights.2.rest_0_) | copy-start | bytes 9437188
  136.2 15.0 %copy-start.4 = (s32[16]{0:T(128)S(1)}, s32[16]{0:T(128)}, u32[]{:S(2)}) copy-start(s32[16]{0:T(128)} %counts_ref.7) | copy-start | bytes 196
  136.2 50.3 %all-to-all-start.2 = ((bf16[32,6,32,256]{3,2,1,0:T(8,128)(2,1)}), bf16[32,6,32,256]{3,2,1,0:T(8,128)(2,1)}, u32[]{:S(2)}, u32[]{:S(2)}) async-start(bf16[32,6,32,256]{3,2,1,0:T(8,128)(2,1)} %apply_weights.2.rest_0_), calls=%async_computation.2 | async-start | bytes 6291456 | tf_op jit(solution)/shard_map/all_to_all | solution.py:512
  152.8 1.0 copy-start.11
  157.1 10.2 %collective-permute-start.12 = (f32[2,144,128]{2,1,0:T(8,128)S(1)}, f32[2,144,128]{2,1,0:T(8,128)S(1)}, u32[]{:S(2)}, u32[]{:S(2)}) collective-permute-start(f32[2,144,128]{2,1,0:T(8,128)S(1)} %get-tuple-element.41), channel_id=1, source_target_pairs={{0,1},{1,2},{2,3},{3,0},{4,5},{5,6},{6,7},{7,4},{8,9},{9,10},{10,1... | collective-permute-start | bytes 442376 | tf_op jit(solution)/shard_map/ppermute | solution.py:468
  157.2 10.2 %collective-permute-start.13 = (f32[2,144,128]{2,1,0:T(8,128)S(1)}, f32[2,144,128]{2,1,0:T(8,128)S(1)}, u32[]{:S(2)}, u32[]{:S(2)}) collective-permute-start(f32[2,144,128]{2,1,0:T(8,128)S(1)} %get-tuple-element.42), channel_id=1, source_target_pairs={{0,2},{1,3},{2,0},{3,1},{4,6},{5,7},{6,4},{7,5},{8,10},{9,11},{10,... | collective-permute-start | bytes 442376 | tf_op jit(solution)/shard_map/ppermute | solution.py:468
  158.0 10.0 %collective-permute-start.14 = (f32[2,144,128]{2,1,0:T(8,128)S(1)}, f32[2,144,128]{2,1,0:T(8,128)S(1)}, u32[]{:S(2)}, u32[]{:S(2)}) collective-permute-start(f32[2,144,128]{2,1,0:T(8,128)S(1)} %get-tuple-element.43), channel_id=1, source_target_pairs={{0,3},{1,0},{2,1},{3,2},{4,7},{5,4},{6,5},{7,6},{8,11},{9,8},{10,9... | collective-permute-start | bytes 442376 | tf_op jit(solution)/shard_map/ppermute | solution.py:468
  172.7 7.1 %copy-start.2 = (bf16[2,128,128]{2,1,0:T(8,128)(2,1)}, bf16[2,128,128]{2,1,0:T(8,128)(2,1)S(1)}, u32[]{:S(2)}) copy-start(bf16[2,128,128]{2,1,0:T(8,128)(2,1)S(1)} %newton_schulz.3.w0) | copy-start | bytes 196612
  172.7 4.8 %collective-permute-start.15 = (bf16[2,128,128]{2,1,0:T(8,128)(2,1)S(1)}, bf16[2,128,128]{2,1,0:T(8,128)(2,1)S(1)}, u32[]{:S(2)}, u32[]{:S(2)}) collective-permute-start(bf16[2,128,128]{2,1,0:T(8,128)(2,1)S(1)} %newton_schulz.3.w0), channel_id=1, source_target_pairs={{0,1},{1,2},{2,3},{3,0},{4,5},{5,6},{6,7},{7,4},{8,9},{9,10},{10,1... | collective-permute-start | bytes 196616 | tf_op jit(solution)/shard_map/ppermute | solution.py:468
  172.8 6.0 %collective-permute-start.16 = (bf16[2,128,128]{2,1,0:T(8,128)(2,1)S(1)}, bf16[2,128,128]{2,1,0:T(8,128)(2,1)S(1)}, u32[]{:S(2)}, u32[]{:S(2)}) collective-permute-start(bf16[2,128,128]{2,1,0:T(8,128)(2,1)S(1)} %newton_schulz.3.w0), channel_id=1, source_target_pairs={{0,2},{1,3},{2,0},{3,1},{4,6},{5,7},{6,4},{7,5},{8,10},{9,11},{10,... | collective-permute-start | bytes 196616 | tf_op jit(solution)/shard_map/ppermute | solution.py:468
  175.7 4.0 %collective-permute-start.17 = (bf16[2,128,128]{2,1,0:T(8,128)(2,1)S(1)}, bf16[2,128,128]{2,1,0:T(8,128)(2,1)S(1)}, u32[]{:S(2)}, u32[]{:S(2)}) collective-permute-start(bf16[2,128,128]{2,1,0:T(8,128)(2,1)S(1)} %newton_schulz.3.w0), channel_id=1, source_target_pairs={{0,3},{1,0},{2,1},{3,2},{4,7},{5,4},{6,5},{7,6},{8,11},{9,8},{10,9... | collective-permute-start | bytes 196616 | tf_op jit(solution)/shard_map/ppermute | solution.py:468
  177.5 2.3 copy-start.12
  (7 other events, 5.0 us)

commit v2 on v1

--- a/solution.py
+++ b/solution.py
@@ -13,6 +13,7 @@
 F32 = jnp.float32
 BF16 = jnp.bfloat16
 AUG = 16
+AHEAD = 3
 
 
 def params(mib):
@@ -68,14 +69,6 @@
     patches = order_ref.shape[1]
     ids = lax.broadcasted_iota(jnp.int32, (patches, patches), 0)
     return (ids == order_ref[...]).astype(F32)
-
-
-def row_permutation(slots, members, gather):
-    size = slots * members * gather
-    target = lax.broadcasted_iota(jnp.int32, (size, size), 0)
-    per = gather * members
-    origin = lax.rem(target, per) * slots + lax.div(target, per)
-    return (origin == lax.broadcasted_iota(jnp.int32, (size, size), 1)).astype(BF16)
 
 
 def send_kernel(first, order_ref, x_ref, out_ref, x_buf, out_buf, x_sem, out_sem):
@@ -128,9 +121,6 @@
     recv_buf, x_buf, op_buf, col_buf, mean_ref, y_buf, recv_sem, x_sem, op_sem, col_sem, y_sem = scratch
     fields, groups, rows, cols = recv_buf.shape
     slots, members = x_buf.shape[1], x_buf.shape[2]
-    members_local = rows // slots
-    gather = 256 // rows
-    part = members_local * gather
     loads = [
         pltpu.make_async_copy(recv_ref.at[:, f], recv_buf.at[f], recv_sem.at[f])
         for f in range(fields)
@@ -144,7 +134,6 @@
     ]
     start(loads)
     start(small)
-    perm = row_permutation(slots, members_local, gather)
     mean_ref[...] = jnp.zeros_like(mean_ref)
     for f in range(fields):
         loads[f].wait()
@@ -255,8 +244,27 @@
     )(counts, lev, recv, op, col, *after)
 
 
+def pack_rows(a):
+    half = a.shape[1] // 2
+    quarter = half // 2
+    left = lax.broadcasted_iota(jnp.int32, (quarter, 2 * half), 1) < half
+    corner = jnp.where(left, a[:quarter], pltpu.roll(a[quarter:half], half, 1))
+    return jnp.concatenate([corner, a[half : 2 * half + 8]], axis=0)
+
+
+def unpack_rows(a):
+    half = a.shape[1] // 2
+    quarter = half // 2
+    top = jnp.concatenate([a[:quarter], pltpu.roll(a[:quarter], half, 1)], axis=0)
+    lower = jnp.concatenate([top, a[quarter : quarter + half]], axis=0)
+    row = lax.broadcasted_iota(jnp.int32, lower.shape, 0)
+    col = lax.broadcasted_iota(jnp.int32, lower.shape, 1)
+    matrix = jnp.where((row < half) & (col >= half), lower.T, lower)
+    return matrix, a[quarter + half :]
+
+
 def gram_kernel(first, counts_ref, lev_ref, y0, y1, y2, y3, value_ref, weight_ref, *rest):
-    out_refs, mean_ref = rest[-5:-1], rest[-1]
+    out_refs, mean_ref, sum_ref = rest[-6:-2], rest[-2], rest[-1]
     per, _, members = out_refs[0].shape
     lev = lev_ref[0]
     start = jnp.int32(0)
@@ -268,13 +276,13 @@
     )
     mean_ref[...] = total[0:16] + (total[16:32] + total[32:48])
     for d, out_ref in enumerate(out_refs):
-        out_ref[...] = jnp.zeros_like(out_ref)
         owned = lax.rem(lev + d, 4) * per
         base = lax.fori_loop(0, owned, lambda s, b: b + counts_ref[first + s], jnp.int32(0))
         for s in range(per):
             count = counts_ref[first + owned + s]
-
-            def tile_step(i, carry, s=s, out_ref=out_ref):
+            sum_ref[...] = jnp.zeros_like(sum_ref)
+
+            def tile_step(i, carry):
                 row = start + 4 * i + lev
                 rows = pl.ds(pl.multiple_of(i * members, members), members)
                 pert = (y0[rows, :].astype(F32) + y1[rows, :].astype(F32)) + (
@@ -284,12 +292,13 @@
                 weight = weight_ref[pl.ds(row, 1), :]
                 depart = value_ref[pl.ds(row, 1), :] - mean
                 aug = jnp.concatenate([pert, depart, jnp.zeros((AUG - 1, TILE), F32)], axis=0)
-                out_ref[s] += dot3(split(aug * weight), split(pert), dot_nt)
+                sum_ref[...] += dot3(split(aug * weight), split(pert), dot_nt)
                 return carry
 
             low, high = tile_range(base, count, lev)
             lax.fori_loop(low, high, tile_step, 0)
             base = base + count
+            out_ref[s] = pack_rows(sum_ref[...])
 
 
 def partial_gram(counts, lev, ys, value, weight, first, slots, members, us, after):
@@ -297,8 +306,11 @@
         functools.partial(gram_kernel, first),
         in_specs=[smem(), smem()] + [vmem()] * 6 + [hbm() for _ in after],
         out_specs=[vmem()] * 4,
-        out_shape=[jax.ShapeDtypeStruct((slots // 4, members + AUG, members), F32)] * 4,
-        scratch_shapes=[pltpu.VMEM((16, TILE), F32)],
+        out_shape=[jax.ShapeDtypeStruct((slots // 4, members * 3 // 4 + 8, members), F32)] * 4,
+        scratch_shapes=[
+            pltpu.VMEM((16, TILE), F32),
+            pltpu.VMEM((members + AUG, members), F32),
+        ],
         compiler_params=params(24),
         cost_estimate=cost(us),
         name="gram",
@@ -313,13 +325,14 @@
     uppers, lowers, scales, sides = [], [], [], []
     for s in range(slots):
         total = (g0[s] + g1[s]) + (g2[s] + g3[s])
-        system = total[0:members] + (members - 1.0) * eye
+        gram, side = unpack_rows(total)
+        system = gram + (members - 1.0) * eye
         square = jnp.sum(jnp.sum(system * system, axis=1, keepdims=True), axis=0, keepdims=True)
         scale = jnp.sqrt(square)
         uppers.append(system / scale)
         lowers.append(eye)
         scales.append(scale)
-        sides.append(total[members : members + 8])
+        sides.append(side)
 
     for step in range(ITERS):
         for s in range(slots):
@@ -355,13 +368,12 @@
     )(*gs, *after)
 
 
-def apply_kernel(lev_ref, w0, w1, w2, w3, x_ref, *rest):
-    out_ref, x_buf, mixed_ref, out_buf, x_sem, out_sem = rest[-6:]
+def apply_kernel(lev_ref, *rest):
+    x_ref = rest[4]
+    out_ref, x_buf, mixed_ref, out_buf, w_buf, x_sem, out_sem, w_sem = rest[-8:]
+    weights = [pltpu.make_async_copy(rest[d], w_buf.at[d], w_sem.at[d]) for d in range(4)]
     fields, slots, members, cols = x_buf.shape
     groups, rows = out_buf.shape[1], out_buf.shape[2]
-    members_local = rows // slots
-    gather = 256 // rows
-    part = members_local * gather
     per = slots // 4
     loads = [
         pltpu.make_async_copy(x_ref.at[f], x_buf.at[f], x_sem.at[f]) for f in range(fields)
@@ -370,16 +382,18 @@
         pltpu.make_async_copy(out_buf.at[f], out_ref.at[:, f], out_sem.at[f])
         for f in range(fields)
     ]
-    start(loads)
-    perm = row_permutation(slots, members_local, gather).astype(F32).T.astype(BF16)
+    start(weights)
+    start(loads[:AHEAD])
+    wait(weights)
     for f in range(fields):
         loads[f].wait()
-        for d, w_ref in enumerate((w0, w1, w2, w3)):
+        start(loads[f + AHEAD : f + AHEAD + 1])
+        for d in range(4):
             owned = lax.rem(lev_ref[0] + 4 - d, 4) * per
             for s in range(per):
                 x = x_buf[f, owned + s].astype(F32)
                 mean = jnp.mean(x, axis=0, keepdims=True)
-                mixed = dot(w_ref[s], (x - mean).astype(BF16))
+                mixed = dot(w_buf[d, s], (x - mean).astype(BF16))
                 mixed_ref[owned + s] = mean + mixed
         moved = jnp.transpose(mixed_ref[...], (1, 0, 2)).reshape(groups, rows, cols)
         out_buf[f] = moved.astype(BF16)
@@ -392,15 +406,17 @@
     rows = slots * members // groups
     return pl.pallas_call(
         apply_kernel,
-        in_specs=[smem()] + [vmem()] * 4 + [hbm()] + [hbm() for _ in after],
+        in_specs=[smem()] + [hbm()] * 5 + [hbm() for _ in after],
         out_specs=hbm(),
         out_shape=jax.ShapeDtypeStruct((groups, fields, rows, cols), BF16),
         scratch_shapes=[
             pltpu.VMEM((fields, slots, members, cols), BF16),
             pltpu.VMEM((slots, members, cols), F32),
             pltpu.VMEM((fields, groups, rows, cols), BF16),
-            pltpu.SemaphoreType.DMA((fields,)),
-            pltpu.SemaphoreType.DMA((fields,)),
+            pltpu.VMEM((4,) + ws[0].shape, BF16),
+            pltpu.SemaphoreType.DMA((fields,)),
+            pltpu.SemaphoreType.DMA((fields,)),
+            pltpu.SemaphoreType.DMA((4,)),
         ],
         compiler_params=params(mib),
         cost_estimate=cost(us),

time: 241 us -> 238 us (0.988)
  blocking collectives: 48.3 us -> 45.6 us
  starting transfers between devices: 50.6 us -> 48.1 us
    all_to_all x1, blocking collectives: 48.3 us -> 45.6 us  [analyse(): lax.all_to_all(out, 'patch', split_axis=0, concat_axis=0, tiled=True)]
  transfers between devices with their start and end apart: 21 -> 21, of which waited for: 13 -> 14; matrix products, arithmetic and copies ran while one was open for 1% -> 1% of each run, Pallas kernels for 17% -> 18%
where the time goes in v2:
time: 238 us
  waiting for transfers between devices  75 us (32%)
  Pallas kernels  63.5 us (27%)
  starting transfers between devices  48.1 us (20%)
  blocking collectives  45.6 us (19%)
  local copies, waits for them, and re-layouts  4.42 us (2%)
    all_to_all x1, blocking collectives, analyse(): lax.all_to_all(out, 'patch', split_axis=0, concat_axis=0, tiled=True)  45.6 us
    all_to_all x2, waiting for transfers between devices, body(): lax.all_to_all(sent, 'patch', split_axis=0, concat_axis=0, tiled=True)  42.6 us
    ppermute x18, waiting for transfers between devices, exchange(): lax.ppermute(blocks[d], 'lev', [(i, (i + d) % 4) for i in range(4)])  32.4 us
    ppermute x18, starting transfers between devices, exchange(): lax.ppermute(blocks[d], 'lev', [(i, (i + d) % 4) for i in range(4)])  23.1 us
    all_to_all x2, starting transfers between devices, body(): lax.all_to_all(sent, 'patch', split_axis=0, concat_axis=0, tiled=True)  18.7 us
    pallas_call x2, Pallas kernels, observe(): pl.pallas_call(functools.partial(observe_kernel, first), in_specs=[smem()...  18.4 us
    pallas_call x2, Pallas kernels, send(): pl.pallas_call(functools.partial(send_kernel, first), in_specs=[vmem(), h...  11 us
    pallas_call x2, Pallas kernels, apply(): pl.pallas_call(apply_kernel, in_specs=[smem()] + [hbm()] * 5 + [hbm() for...  10.9 us
  transfers between devices with their start and end apart: 21, of which 14 were waited for; matrix products, arithmetic and copies ran while one was open for 1% of the time, Pallas kernels for 18%

profile of v2, /device:TPU:1, one launch (start us, length us, event | category | flops | bytes accessed | tf_op | source)
XLA Modules:
  0.0 237.8 jit_solution(5372696032581510450)
XLA Ops:
  0.0 5.5 %send_permute.2 = bf16[32,6,32,256]{3,2,1,0:T(8,128)(2,1)} custom-call(s32[1,512]{1,0:T(1,128)} %bitcast.25, bf16[4,6,512,256]{3,2,1,0:T(8,128)(2,1)} %bitcast.23), custom_call_target="tpu_custom_call" | custom-call | flops 5750000128 | tf_op jit(solution)/shard_map/send_permute/pallas_call | solution.py:98
  5.5 9.7 %all-to-all-start = ((bf16[32,6,32,256]{3,2,1,0:T(8,128)(2,1)}), bf16[32,6,32,256]{3,2,1,0:T(8,128)(2,1)}, u32[]{:S(2)}, u32[]{:S(2)}) async-start(bf16[32,6,32,256]{3,2,1,0:T(8,128)(2,1)} %send_permute.2), calls=%async_computation | async-start | bytes 6291456 | tf_op jit(solution)/shard_map/all_to_all | solution.py:510
  16.5 5.5 %send_permute.3.rest_0_ = bf16[32,6,32,256]{3,2,1,0:T(8,128)(2,1)} custom-call(s32[1,512]{1,0:T(1,128)} %bitcast.26, bf16[4,6,512,256]{3,2,1,0:T(8,128)(2,1)} %bitcast.24), custom_call_target="tpu_custom_call" | custom-call | flops 5750000128 | tf_op jit(solution)/shard_map/send_permute/pallas_call | solution.py:98
  22.0 32.4 %all-to-all-done.recv_ref = bf16[32,6,32,256]{3,2,1,0:T(8,128)(2,1)} async-done(((bf16[32,6,32,256]{3,2,1,0:T(8,128)(2,1)}), bf16[32,6,32,256]{3,2,1,0:T(8,128)(2,1)}, u32[]{:S(2)}, u32[]{:S(2)}) %all-to-all-start) | async-done | bytes 3145760 | tf_op jit(solution)/shard_map/all_to_all | solution.py:510
  54.4 8.2 %observe.2 = (bf16[6,8,128,256]{3,2,1,0:T(8,128)(2,1)}, bf16[1840,128]{1,0:T(8,128)(2,1)}, bf16[1840,128]{1,0:T(8,128)(2,1)}, bf16[1840,128]{1,0:T(8,128)(2,1)}, bf16[1840,128]{1,0:T(8,128)(2,1)}) custom-call(s32[16]{0:T(128)} %counts_ref.7, s32[1]{0:T(128)} %bitcast.2.lev_ref, bf16[32,6,32,256]{3,2,1,0:T(8,128)(2,1)} %all-to-all-done.recv_ref, ...), custom_call_target="tpu_custom_call" | custom-call | flops 1150000000 | tf_op jit(solution)/shard_map/observe/pallas_call | solution.py:222
  63.9 2.4 %collective-permute-start.1 = (bf16[1840,128]{1,0:T(8,128)(2,1)}, bf16[1840,128]{1,0:T(8,128)(2,1)S(1)}, u32[]{:S(2)}, u32[]{:S(2)}) collective-permute-start(bf16[1840,128]{1,0:T(8,128)(2,1)} %get-tuple-element.29), channel_id=1, source_target_pairs={{0,2},{1,3},{2,0},{3,1},{4,6},{5,7},{6,4},{7,5},{8,10},{9,11},{10,... | collective-permute-start | bytes 1413128 | tf_op jit(solution)/shard_map/ppermute | solution.py:484
  67.6 9.0 %all-to-all-start.1 = ((bf16[32,6,32,256]{3,2,1,0:T(8,128)(2,1)}), bf16[32,6,32,256]{3,2,1,0:T(8,128)(2,1)}, u32[]{:S(2)}, u32[]{:S(2)}) async-start(bf16[32,6,32,256]{3,2,1,0:T(8,128)(2,1)} %send_permute.3.rest_0_), calls=%async_computation.1 | async-start | bytes 6291456 | tf_op jit(solution)/shard_map/all_to_all | solution.py:510
  76.7 7.1 %collective-permute-done.1.y2 = bf16[1840,128]{1,0:T(8,128)(2,1)S(1)} collective-permute-done((bf16[1840,128]{1,0:T(8,128)(2,1)}, bf16[1840,128]{1,0:T(8,128)(2,1)S(1)}, u32[]{:S(2)}, u32[]{:S(2)}) %collective-permute-start.1) | collective-permute-done | bytes 471072 | tf_op jit(solution)/shard_map/ppermute | solution.py:484
  83.8 2.2 collective-permute-done.2.y3
  86.0 2.1 gram.2
  88.1 2.5 %collective-permute-start.3 = (f32[2,104,128]{2,1,0:T(8,128)S(1)}, f32[2,104,128]{2,1,0:T(8,128)S(1)}, u32[]{:S(2)}, u32[]{:S(2)}) collective-permute-start(f32[2,104,128]{2,1,0:T(8,128)S(1)} %get-tuple-element.32), channel_id=1, source_target_pairs={{0,1},{1,2},{2,3},{3,0},{4,5},{5,6},{6,7},{7,4},{8,9},{9,10},{10,1... | collective-permute-start | bytes 319496 | tf_op jit(solution)/shard_map/ppermute | solution.py:484
  90.6 1.9 collective-permute-start.4
  93.8 2.3 collective-permute-done.4.g2
  96.5 4.8 %newton_schulz.2.rest_0_ = bf16[2,128,128]{2,1,0:T(8,128)(2,1)S(1)} custom-call(f32[2,104,128]{2,1,0:T(8,128)S(1)} %get-tuple-element.31.g0, f32[2,104,128]{2,1,0:T(8,128)S(1)} %collective-permute-done.3.g1, f32[2,104,128]{2,1,0:T(8,128)S(1)} %collective-permute-done.4.g2, f32[2,104,128]{2,1,0:T(8,128)S(1)} %collective-permute-done.5.g3), custom_call_target="tpu_custom_call" | custom-call | flops 8049999872 | tf_op jit(solution)/shard_map/newton_schulz/pallas_call | solution.py:360
  101.9 2.4 collective-permute-start.7
  105.7 10.3 %all-to-all-done.1.recv_ref = bf16[32,6,32,256]{3,2,1,0:T(8,128)(2,1)} async-done(((bf16[32,6,32,256]{3,2,1,0:T(8,128)(2,1)}), bf16[32,6,32,256]{3,2,1,0:T(8,128)(2,1)}, u32[]{:S(2)}, u32[]{:S(2)}) %all-to-all-start.1) | async-done | bytes 3145760 | tf_op jit(solution)/shard_map/all_to_all | solution.py:510
  116.0 10.2 %observe.3 = (bf16[6,8,128,256]{3,2,1,0:T(8,128)(2,1)}, bf16[1840,128]{1,0:T(8,128)(2,1)}, bf16[1840,128]{1,0:T(8,128)(2,1)}, bf16[1840,128]{1,0:T(8,128)(2,1)}, bf16[1840,128]{1,0:T(8,128)(2,1)}) custom-call(s32[16]{0:T(128)} %counts_ref.7, s32[1]{0:T(128)} %bitcast.2.lev_ref, bf16[32,6,32,256]{3,2,1,0:T(8,128)(2,1)} %all-to-all-done.1.recv_ref, ...), custom_call_target="tpu_custom_call" | custom-call | flops 23000000512 | tf_op jit(solution)/shard_map/observe/pallas_call | solution.py:222
  126.5 2.5 %collective-permute-start.11 = (bf16[1840,128]{1,0:T(8,128)(2,1)}, bf16[1840,128]{1,0:T(8,128)(2,1)}, u32[]{:S(2)}, u32[]{:S(2)}) collective-permute-start(bf16[1840,128]{1,0:T(8,128)(2,1)} %get-tuple-element.39), channel_id=1, source_target_pairs={{0,3},{1,0},{2,1},{3,2},{4,7},{5,4},{6,5},{7,6},{8,11},{9,8},{10,9... | collective-permute-start | bytes 1413128 | tf_op jit(solution)/shard_map/ppermute | solution.py:484
  129.6 5.5 %apply_weights.2.rest_0_ = bf16[32,6,32,256]{3,2,1,0:T(8,128)(2,1)} custom-call(s32[1]{0:T(128)} %bitcast.2.lev_ref, bf16[2,128,128]{2,1,0:T(8,128)(2,1)} %copy-done.6, bf16[2,128,128]{2,1,0:T(8,128)(2,1)} %copy-done.15, bf16[2,128,128]{2,1,0:T(8,128)(2,1)} %copy-done.16, bf16[2,128,128]{2,1,0:T(8,128)(2,1)} %copy-done.17, ...), custom_call_target="tpu_custom_call" | custom-call | flops 115000000512 | tf_op jit(solution)/shard_map/apply_weights/pallas_call | solution.py:407
  135.2 6.3 %all-to-all-start.2 = ((bf16[32,6,32,256]{3,2,1,0:T(8,128)(2,1)}), bf16[32,6,32,256]{3,2,1,0:T(8,128)(2,1)}, u32[]{:S(2)}, u32[]{:S(2)}) async-start(bf16[32,6,32,256]{3,2,1,0:T(8,128)(2,1)} %apply_weights.2.rest_0_), calls=%async_computation.2 | async-start | bytes 6291456 | tf_op jit(solution)/shard_map/all_to_all | solution.py:528
  141.4 5.9 %collective-permute-done.11.y3 = bf16[1840,128]{1,0:T(8,128)(2,1)} collective-permute-done((bf16[1840,128]{1,0:T(8,128)(2,1)}, bf16[1840,128]{1,0:T(8,128)(2,1)}, u32[]{:S(2)}, u32[]{:S(2)}) %collective-permute-start.11) | collective-permute-done | bytes 471072 | tf_op jit(solution)/shard_map/ppermute | solution.py:484
  147.3 3.5 %collective-permute-done.9.y1 = bf16[1840,128]{1,0:T(8,128)(2,1)} collective-permute-done((bf16[1840,128]{1,0:T(8,128)(2,1)}, bf16[1840,128]{1,0:T(8,128)(2,1)}, u32[]{:S(2)}, u32[]{:S(2)}) %collective-permute-start.9) | collective-permute-done | bytes 471072 | tf_op jit(solution)/shard_map/ppermute | solution.py:484
  153.4 4.2 %gram.3 = (f32[2,104,128]{2,1,0:T(8,128)S(1)}, f32[2,104,128]{2,1,0:T(8,128)S(1)}, f32[2,104,128]{2,1,0:T(8,128)S(1)}, f32[2,104,128]{2,1,0:T(8,128)S(1)}) custom-call(s32[16]{0:T(128)S(1)} %copy-done.4, s32[1]{0:T(128)} %bitcast.2.lev_ref, bf16[1840,128]{1,0:T(8,128)(2,1)S(1)} %copy-done.11, bf16[1840,128]{1,0:T(8,128)(2,1)} %collective-permute-done.9.y1, ...), custom_call_target="tpu_custom_call" | custom-call | flops 230000001024 | tf_op jit(solution)/shard_map/gram/pallas_call | solution.py:305
  158.7 1.6 collective-permute-start.14
  160.3 5.9 %collective-permute-done.12.g1 = f32[2,104,128]{2,1,0:T(8,128)S(1)} collective-permute-done((f32[2,104,128]{2,1,0:T(8,128)S(1)}, f32[2,104,128]{2,1,0:T(8,128)S(1)}, u32[]{:S(2)}, u32[]{:S(2)}) %collective-permute-start.12) | collective-permute-done | bytes 106528 | tf_op jit(solution)/shard_map/ppermute | solution.py:484
  166.5 4.8 %newton_schulz.3.rest_0_ = bf16[2,128,128]{2,1,0:T(8,128)(2,1)S(1)} custom-call(f32[2,104,128]{2,1,0:T(8,128)S(1)} %get-tuple-element.40.g0, f32[2,104,128]{2,1,0:T(8,128)S(1)} %collective-permute-done.12.g1, f32[2,104,128]{2,1,0:T(8,128)S(1)} %collective-permute-done.13.g2, f32[2,104,128]{2,1,0:T(8,128)S(1)} %collective-permute-done.14.g3), custom_call_target="tpu_custom_call" | custom-call | flops 1150000000 | tf_op jit(solution)/shard_map/newton_schulz/pallas_call | solution.py:360
  171.6 3.0 %collective-permute-start.16 = (bf16[2,128,128]{2,1,0:T(8,128)(2,1)S(1)}, bf16[2,128,128]{2,1,0:T(8,128)(2,1)S(1)}, u32[]{:S(2)}, u32[]{:S(2)}) collective-permute-start(bf16[2,128,128]{2,1,0:T(8,128)(2,1)S(1)} %newton_schulz.3.rest_0_), channel_id=1, source_target_pairs={{0,2},{1,3},{2,0},{3,1},{4,6},{5,7},{6,4},{7,5},{8,10},{9,11},{10,... | collective-permute-start | bytes 196616 | tf_op jit(solution)/shard_map/ppermute | solution.py:484
  174.6 1.5 collective-permute-done.15.rest_1_
  176.1 1.4 collective-permute-done.16.rest_2_
  179.2 5.4 %apply_weights.3 = bf16[32,6,32,256]{3,2,1,0:T(8,128)(2,1)} custom-call(s32[1]{0:T(128)} %bitcast.2.lev_ref, bf16[2,128,128]{2,1,0:T(8,128)(2,1)} %copy-done.2, bf16[2,128,128]{2,1,0:T(8,128)(2,1)} %copy-done.12, bf16[2,128,128]{2,1,0:T(8,128)(2,1)} %copy-done.13, bf16[2,128,128]{2,1,0:T(8,128)(2,1)} %copy-done.14, ...), custom_call_target="tpu_custom_call" | custom-call | flops 1150000000 | tf_op jit(solution)/shard_map/apply_weights/pallas_call | solution.py:407
  184.7 45.6 %all_to_all.20.refs_1_ = bf16[32,6,32,256]{3,2,1,0:T(8,128)(2,1)} all-to-all(bf16[32,6,32,256]{3,2,1,0:T(8,128)(2,1)} %apply_weights.3), channel_id=1, replica_groups=mesh['patch'=32,'lev'=4] {'patch'}, dimensions={0} | all-to-all | bytes 6291456 | tf_op jit(solution)/shard_map/all_to_all | solution.py:528
  230.3 7.3 %restore_order.1 = bf16[4,6,512,256]{3,2,1,0:T(8,128)(2,1)} custom-call(s32[1,512]{1,0:T(1,128)} %bitcast.27, bf16[32,6,32,256]{3,2,1,0:T(8,128)(2,1)} %all-to-all-done.2.refs_0_, bf16[32,6,32,256]{3,2,1,0:T(8,128)(2,1)} %all_to_all.20.refs_1_), custom_call_target="tpu_custom_call" | custom-call | flops 6899999744 | tf_op jit(solution)/shard_map/restore_order/pallas_call | solution.py:463
  (60 shorter events, 14.5 us)
Async XLA Ops:
  0.0 15.2 %copy-start = (bf16[4,6,8192]{2,0,1:T(4,128)(2,1)S(1)}, bf16[4,6,8192]{2,0,1:T(4,128)(2,1)}, u32[]{:S(2)}) copy-start(bf16[4,6,8192]{2,0,1:T(4,128)(2,1)} %param.11) | copy-start | bytes 1179652
  5.5 48.9 %all-to-all-start = ((bf16[32,6,32,256]{3,2,1,0:T(8,128)(2,1)}), bf16[32,6,32,256]{3,2,1,0:T(8,128)(2,1)}, u32[]{:S(2)}, u32[]{:S(2)}) async-start(bf16[32,6,32,256]{3,2,1,0:T(8,128)(2,1)} %send_permute.2), calls=%async_computation | async-start | bytes 6291456 | tf_op jit(solution)/shard_map/all_to_all | solution.py:510
  62.6 14.0 %collective-permute-start = (bf16[1840,128]{1,0:T(8,128)(2,1)}, bf16[1840,128]{1,0:T(8,128)(2,1)S(1)}, u32[]{:S(2)}, u32[]{:S(2)}) collective-permute-start(bf16[1840,128]{1,0:T(8,128)(2,1)} %get-tuple-element.28), channel_id=1, source_target_pairs={{0,1},{1,2},{2,3},{3,0},{4,5},{5,6},{6,7},{7,4},{8,9},{9,10},{10,1... | collective-permute-start | bytes 1413128 | tf_op jit(solution)/shard_map/ppermute | solution.py:484
  63.9 19.8 %collective-permute-start.1 = (bf16[1840,128]{1,0:T(8,128)(2,1)}, bf16[1840,128]{1,0:T(8,128)(2,1)S(1)}, u32[]{:S(2)}, u32[]{:S(2)}) collective-permute-start(bf16[1840,128]{1,0:T(8,128)(2,1)} %get-tuple-element.29), channel_id=1, source_target_pairs={{0,2},{1,3},{2,0},{3,1},{4,6},{5,7},{6,4},{7,5},{8,10},{9,11},{10,... | collective-permute-start | bytes 1413128 | tf_op jit(solution)/shard_map/ppermute | solution.py:484
  66.4 19.6 %copy-start.3 = (s32[16]{0:T(128)S(1)}, s32[16]{0:T(128)}, u32[]{:S(2)}) copy-start(s32[16]{0:T(128)} %counts_ref.7) | copy-start | bytes 196
  66.4 19.6 %copy-start.5 = (bf16[1840,128]{1,0:T(8,128)(2,1)S(1)}, bf16[1840,128]{1,0:T(8,128)(2,1)}, u32[]{:S(2)}) copy-start(bf16[1840,128]{1,0:T(8,128)(2,1)} %get-tuple-element.27.y0) | copy-start | bytes 1413124
  66.4 19.6 %copy-start.7 = (f32[8192]{0:T(1024)S(1)}, f32[8192]{0:T(1024)}, u32[]{:S(2)}) copy-start(f32[8192]{0:T(1024)} %param.12) | copy-start | bytes 98308
  66.4 19.6 %copy-start.9 = (f32[8192]{0:T(1024)S(1)}, f32[8192]{0:T(1024)}, u32[]{:S(2)}) copy-start(f32[8192]{0:T(1024)} %param.13) | copy-start | bytes 98308
  66.4 19.6 %collective-permute-start.2 = (bf16[1840,128]{1,0:T(8,128)(2,1)}, bf16[1840,128]{1,0:T(8,128)(2,1)S(1)}, u32[]{:S(2)}, u32[]{:S(2)}) collective-permute-start(bf16[1840,128]{1,0:T(8,128)(2,1)} %get-tuple-element.30), channel_id=1, source_target_pairs={{0,3},{1,0},{2,1},{3,2},{4,7},{5,4},{6,5},{7,6},{8,11},{9,8},{10,9... | collective-permute-start | bytes 1413128 | tf_op jit(solution)/shard_map/ppermute | solution.py:484
  67.6 48.4 %all-to-all-start.1 = ((bf16[32,6,32,256]{3,2,1,0:T(8,128)(2,1)}), bf16[32,6,32,256]{3,2,1,0:T(8,128)(2,1)}, u32[]{:S(2)}, u32[]{:S(2)}) async-start(bf16[32,6,32,256]{3,2,1,0:T(8,128)(2,1)} %send_permute.3.rest_0_), calls=%async_computation.1 | async-start | bytes 6291456 | tf_op jit(solution)/shard_map/all_to_all | solution.py:510
  88.1 5.7 %collective-permute-start.3 = (f32[2,104,128]{2,1,0:T(8,128)S(1)}, f32[2,104,128]{2,1,0:T(8,128)S(1)}, u32[]{:S(2)}, u32[]{:S(2)}) collective-permute-start(f32[2,104,128]{2,1,0:T(8,128)S(1)} %get-tuple-element.32), channel_id=1, source_target_pairs={{0,1},{1,2},{2,3},{3,0},{4,5},{5,6},{6,7},{7,4},{8,9},{9,10},{10,1... | collective-permute-start | bytes 319496 | tf_op jit(solution)/shard_map/ppermute | solution.py:484
  90.6 5.5 %collective-permute-start.4 = (f32[2,104,128]{2,1,0:T(8,128)S(1)}, f32[2,104,128]{2,1,0:T(8,128)S(1)}, u32[]{:S(2)}, u32[]{:S(2)}) collective-permute-start(f32[2,104,128]{2,1,0:T(8,128)S(1)} %get-tuple-element.33), channel_id=1, source_target_pairs={{0,2},{1,3},{2,0},{3,1},{4,6},{5,7},{6,4},{7,5},{8,10},{9,11},{10,... | collective-permute-start | bytes 319496 | tf_op jit(solution)/shard_map/ppermute | solution.py:484
  92.5 4.0 %collective-permute-start.5 = (f32[2,104,128]{2,1,0:T(8,128)S(1)}, f32[2,104,128]{2,1,0:T(8,128)S(1)}, u32[]{:S(2)}, u32[]{:S(2)}) collective-permute-start(f32[2,104,128]{2,1,0:T(8,128)S(1)} %get-tuple-element.34), channel_id=1, source_target_pairs={{0,3},{1,0},{2,1},{3,2},{4,7},{5,4},{6,5},{7,6},{8,11},{9,8},{10,9... | collective-permute-start | bytes 319496 | tf_op jit(solution)/shard_map/ppermute | solution.py:484
  101.3 14.7 %copy-start.6 = (bf16[2,128,128]{2,1,0:T(8,128)(2,1)}, bf16[2,128,128]{2,1,0:T(8,128)(2,1)S(1)}, u32[]{:S(2)}) copy-start(bf16[2,128,128]{2,1,0:T(8,128)(2,1)S(1)} %newton_schulz.2.rest_0_) | copy-start | bytes 196612
  101.3 27.7 %collective-permute-start.6 = (bf16[2,128,128]{2,1,0:T(8,128)(2,1)S(1)}, bf16[2,128,128]{2,1,0:T(8,128)(2,1)S(1)}, u32[]{:S(2)}, u32[]{:S(2)}) collective-permute-start(bf16[2,128,128]{2,1,0:T(8,128)(2,1)S(1)} %newton_schulz.2.rest_0_), channel_id=1, source_target_pairs={{0,1},{1,2},{2,3},{3,0},{4,5},{5,6},{6,7},{7,4},{8,9},{9,10},{10,1... | collective-permute-start | bytes 196616 | tf_op jit(solution)/shard_map/ppermute | solution.py:484
  101.9 27.0 %collective-permute-start.7 = (bf16[2,128,128]{2,1,0:T(8,128)(2,1)S(1)}, bf16[2,128,128]{2,1,0:T(8,128)(2,1)S(1)}, u32[]{:S(2)}, u32[]{:S(2)}) collective-permute-start(bf16[2,128,128]{2,1,0:T(8,128)(2,1)S(1)} %newton_schulz.2.rest_0_), channel_id=1, source_target_pairs={{0,2},{1,3},{2,0},{3,1},{4,6},{5,7},{6,4},{7,5},{8,10},{9,11},{10,... | collective-permute-start | bytes 196616 | tf_op jit(solution)/shard_map/ppermute | solution.py:484
  104.3 24.7 %collective-permute-start.8 = (bf16[2,128,128]{2,1,0:T(8,128)(2,1)S(1)}, bf16[2,128,128]{2,1,0:T(8,128)(2,1)S(1)}, u32[]{:S(2)}, u32[]{:S(2)}) collective-permute-start(bf16[2,128,128]{2,1,0:T(8,128)(2,1)S(1)} %newton_schulz.2.rest_0_), channel_id=1, source_target_pairs={{0,3},{1,0},{2,1},{3,2},{4,7},{5,4},{6,5},{7,6},{8,11},{9,8},{10,9... | collective-permute-start | bytes 196616 | tf_op jit(solution)/shard_map/ppermute | solution.py:484
  126.2 15.3 %collective-permute-start.10 = (bf16[1840,128]{1,0:T(8,128)(2,1)}, bf16[1840,128]{1,0:T(8,128)(2,1)}, u32[]{:S(2)}, u32[]{:S(2)}) collective-permute-start(bf16[1840,128]{1,0:T(8,128)(2,1)} %get-tuple-element.38), channel_id=1, source_target_pairs={{0,2},{1,3},{2,0},{3,1},{4,6},{5,7},{6,4},{7,5},{8,10},{9,11},{10,... | collective-permute-start | bytes 1413128 | tf_op jit(solution)/shard_map/ppermute | solution.py:484
  126.5 20.9 %collective-permute-start.11 = (bf16[1840,128]{1,0:T(8,128)(2,1)}, bf16[1840,128]{1,0:T(8,128)(2,1)}, u32[]{:S(2)}, u32[]{:S(2)}) collective-permute-start(bf16[1840,128]{1,0:T(8,128)(2,1)} %get-tuple-element.39), channel_id=1, source_target_pairs={{0,3},{1,0},{2,1},{3,2},{4,7},{5,4},{6,5},{7,6},{8,11},{9,8},{10,9... | collective-permute-start | bytes 1413128 | tf_op jit(solution)/shard_map/ppermute | solution.py:484
  129.0 21.9 %collective-permute-start.9 = (bf16[1840,128]{1,0:T(8,128)(2,1)}, bf16[1840,128]{1,0:T(8,128)(2,1)}, u32[]{:S(2)}, u32[]{:S(2)}) collective-permute-start(bf16[1840,128]{1,0:T(8,128)(2,1)} %get-tuple-element.37), channel_id=1, source_target_pairs={{0,1},{1,2},{2,3},{3,0},{4,5},{5,6},{6,7},{7,4},{8,9},{9,10},{10,1... | collective-permute-start | bytes 1413128 | tf_op jit(solution)/shard_map/ppermute | solution.py:484
  135.1 15.7 %copy-start.1 = (bf16[32,6,32,256]{3,2,1,0:T(8,128)(2,1)S(1)}, bf16[32,6,32,256]{3,2,1,0:T(8,128)(2,1)}, u32[]{:S(2)}) copy-start(bf16[32,6,32,256]{3,2,1,0:T(8,128)(2,1)} %apply_weights.2.rest_0_) | copy-start | bytes 9437188
  135.2 15.7 %copy-start.4 = (s32[16]{0:T(128)S(1)}, s32[16]{0:T(128)}, u32[]{:S(2)}) copy-start(s32[16]{0:T(128)} %counts_ref.7) | copy-start | bytes 196
  135.2 49.5 %all-to-all-start.2 = ((bf16[32,6,32,256]{3,2,1,0:T(8,128)(2,1)}), bf16[32,6,32,256]{3,2,1,0:T(8,128)(2,1)}, u32[]{:S(2)}, u32[]{:S(2)}) async-start(bf16[32,6,32,256]{3,2,1,0:T(8,128)(2,1)} %apply_weights.2.rest_0_), calls=%async_computation.2 | async-start | bytes 6291456 | tf_op jit(solution)/shard_map/all_to_all | solution.py:528
  157.6 8.6 %collective-permute-start.12 = (f32[2,104,128]{2,1,0:T(8,128)S(1)}, f32[2,104,128]{2,1,0:T(8,128)S(1)}, u32[]{:S(2)}, u32[]{:S(2)}) collective-permute-start(f32[2,104,128]{2,1,0:T(8,128)S(1)} %get-tuple-element.41), channel_id=1, source_target_pairs={{0,1},{1,2},{2,3},{3,0},{4,5},{5,6},{6,7},{7,4},{8,9},{9,10},{10,1... | collective-permute-start | bytes 319496 | tf_op jit(solution)/shard_map/ppermute | solution.py:484
  157.6 8.6 %collective-permute-start.13 = (f32[2,104,128]{2,1,0:T(8,128)S(1)}, f32[2,104,128]{2,1,0:T(8,128)S(1)}, u32[]{:S(2)}, u32[]{:S(2)}) collective-permute-start(f32[2,104,128]{2,1,0:T(8,128)S(1)} %get-tuple-element.42), channel_id=1, source_target_pairs={{0,2},{1,3},{2,0},{3,1},{4,6},{5,7},{6,4},{7,5},{8,10},{9,11},{10,... | collective-permute-start | bytes 319496 | tf_op jit(solution)/shard_map/ppermute | solution.py:484
  158.7 7.8 %collective-permute-start.14 = (f32[2,104,128]{2,1,0:T(8,128)S(1)}, f32[2,104,128]{2,1,0:T(8,128)S(1)}, u32[]{:S(2)}, u32[]{:S(2)}) collective-permute-start(f32[2,104,128]{2,1,0:T(8,128)S(1)} %get-tuple-element.43), channel_id=1, source_target_pairs={{0,3},{1,0},{2,1},{3,2},{4,7},{5,4},{6,5},{7,6},{8,11},{9,8},{10,9... | collective-permute-start | bytes 319496 | tf_op jit(solution)/shard_map/ppermute | solution.py:484
  171.3 7.3 %copy-start.2 = (bf16[2,128,128]{2,1,0:T(8,128)(2,1)}, bf16[2,128,128]{2,1,0:T(8,128)(2,1)S(1)}, u32[]{:S(2)}) copy-start(bf16[2,128,128]{2,1,0:T(8,128)(2,1)S(1)} %newton_schulz.3.rest_0_) | copy-start | bytes 196612
  171.3 4.8 %collective-permute-start.15 = (bf16[2,128,128]{2,1,0:T(8,128)(2,1)S(1)}, bf16[2,128,128]{2,1,0:T(8,128)(2,1)S(1)}, u32[]{:S(2)}, u32[]{:S(2)}) collective-permute-start(bf16[2,128,128]{2,1,0:T(8,128)(2,1)S(1)} %newton_schulz.3.rest_0_), channel_id=1, source_target_pairs={{0,1},{1,2},{2,3},{3,0},{4,5},{5,6},{6,7},{7,4},{8,9},{9,10},{10,1... | collective-permute-start | bytes 196616 | tf_op jit(solution)/shard_map/ppermute | solution.py:484
  171.6 5.9 %collective-permute-start.16 = (bf16[2,128,128]{2,1,0:T(8,128)(2,1)S(1)}, bf16[2,128,128]{2,1,0:T(8,128)(2,1)S(1)}, u32[]{:S(2)}, u32[]{:S(2)}) collective-permute-start(bf16[2,128,128]{2,1,0:T(8,128)(2,1)S(1)} %newton_schulz.3.rest_0_), channel_id=1, source_target_pairs={{0,2},{1,3},{2,0},{3,1},{4,6},{5,7},{6,4},{7,5},{8,10},{9,11},{10,... | collective-permute-start | bytes 196616 | tf_op jit(solution)/shard_map/ppermute | solution.py:484
  174.6 4.0 %collective-permute-start.17 = (bf16[2,128,128]{2,1,0:T(8,128)(2,1)S(1)}, bf16[2,128,128]{2,1,0:T(8,128)(2,1)S(1)}, u32[]{:S(2)}, u32[]{:S(2)}) collective-permute-start(bf16[2,128,128]{2,1,0:T(8,128)(2,1)S(1)} %newton_schulz.3.rest_0_), channel_id=1, source_target_pairs={{0,3},{1,0},{2,1},{3,2},{4,7},{5,4},{6,5},{7,6},{8,11},{9,8},{10,9... | collective-permute-start | bytes 196616 | tf_op jit(solution)/shard_map/ppermute | solution.py:484
  176.1 2.5 %copy-start.12 = (bf16[2,128,128]{2,1,0:T(8,128)(2,1)}, bf16[2,128,128]{2,1,0:T(8,128)(2,1)S(1)}, u32[]{:S(2)}) copy-start(bf16[2,128,128]{2,1,0:T(8,128)(2,1)S(1)} %collective-permute-done.15.rest_1_) | copy-start | bytes 196612
  177.5 1.1 copy-start.13
  (7 other events, 5.1 us)

commit v3 on v2

--- a/solution.py
+++ b/solution.py
@@ -473,7 +473,7 @@
             pltpu.SemaphoreType.DMA((fields, len(recvs))),
             pltpu.SemaphoreType.DMA((fields,)),
         ],
-        compiler_params=params(62),
+        compiler_params=params(40),
         cost_estimate=cost(6),
         name="restore_order",
     )(order, *recvs)

time: 238 us -> 236 us (level)
  transfers between devices with their start and end apart: 21 -> 21, of which waited for: 14 -> 13; matrix products, arithmetic and copies ran while one was open for 1% -> 1% of each run, Pallas kernels for 18% -> 17%
where the time goes in v3:
time: 236 us; the launch traced here: 237 us
  waiting for transfers between devices  72.9 us (31%)
  Pallas kernels  62.5 us (26%)
  starting transfers between devices  49.7 us (21%)
  blocking collectives  46.4 us (20%)
  local copies, waits for them, and re-layouts  4.41 us (2%)
    all_to_all x1, blocking collectives, analyse(): lax.all_to_all(out, 'patch', split_axis=0, concat_axis=0, tiled=True)  46.4 us
    all_to_all x2, waiting for transfers between devices, body(): lax.all_to_all(sent, 'patch', split_axis=0, concat_axis=0, tiled=True)  42.9 us
    ppermute x18, waiting for transfers between devices, exchange(): lax.ppermute(blocks[d], 'lev', [(i, (i + d) % 4) for i in range(4)])  30 us
    ppermute x18, starting transfers between devices, exchange(): lax.ppermute(blocks[d], 'lev', [(i, (i + d) % 4) for i in range(4)])  23.4 us
    all_to_all x2, starting transfers between devices, body(): lax.all_to_all(sent, 'patch', split_axis=0, concat_axis=0, tiled=True)  19.3 us
    pallas_call x2, Pallas kernels, observe(): pl.pallas_call(functools.partial(observe_kernel, first), in_specs=[smem()...  18.1 us
    pallas_call x2, Pallas kernels, send(): pl.pallas_call(functools.partial(send_kernel, first), in_specs=[vmem(), h...  11 us
    pallas_call x2, Pallas kernels, apply(): pl.pallas_call(apply_kernel, in_specs=[smem()] + [hbm()] * 5 + [hbm() for...  10.9 us
  transfers between devices with their start and end apart: 21, of which 13 were waited for; matrix products, arithmetic and copies ran while one was open for 1% of the time, Pallas kernels for 17%

profile of v3, /device:TPU:1, one launch (start us, length us, event | category | flops | bytes accessed | tf_op | source)
XLA Modules:
  0.0 237.2 jit_solution(8526629899462386200)
XLA Ops:
  0.0 5.5 %send_permute.2 = bf16[32,6,32,256]{3,2,1,0:T(8,128)(2,1)} custom-call(s32[1,512]{1,0:T(1,128)} %bitcast.20, bf16[4,6,512,256]{3,2,1,0:T(8,128)(2,1)} %bitcast.26), custom_call_target="tpu_custom_call" | custom-call | flops 5750000128 | tf_op jit(solution)/shard_map/send_permute/pallas_call | solution.py:98
  5.5 9.7 %all-to-all-start = ((bf16[32,6,32,256]{3,2,1,0:T(8,128)(2,1)}), bf16[32,6,32,256]{3,2,1,0:T(8,128)(2,1)}, u32[]{:S(2)}, u32[]{:S(2)}) async-start(bf16[32,6,32,256]{3,2,1,0:T(8,128)(2,1)} %send_permute.2), calls=%async_computation | async-start | bytes 6291456 | tf_op jit(solution)/shard_map/all_to_all | solution.py:510
  16.5 5.5 %send_permute.3.rest_0_ = bf16[32,6,32,256]{3,2,1,0:T(8,128)(2,1)} custom-call(s32[1,512]{1,0:T(1,128)} %bitcast.21, bf16[4,6,512,256]{3,2,1,0:T(8,128)(2,1)} %bitcast.27), custom_call_target="tpu_custom_call" | custom-call | flops 5750000128 | tf_op jit(solution)/shard_map/send_permute/pallas_call | solution.py:98
  22.0 32.4 %all-to-all-done.recv_ref = bf16[32,6,32,256]{3,2,1,0:T(8,128)(2,1)} async-done(((bf16[32,6,32,256]{3,2,1,0:T(8,128)(2,1)}), bf16[32,6,32,256]{3,2,1,0:T(8,128)(2,1)}, u32[]{:S(2)}, u32[]{:S(2)}) %all-to-all-start) | async-done | bytes 3145760 | tf_op jit(solution)/shard_map/all_to_all | solution.py:510
  54.4 9.8 %observe.2 = (bf16[6,8,128,256]{3,2,1,0:T(8,128)(2,1)}, bf16[1840,128]{1,0:T(8,128)(2,1)}, bf16[1840,128]{1,0:T(8,128)(2,1)}, bf16[1840,128]{1,0:T(8,128)(2,1)}, bf16[1840,128]{1,0:T(8,128)(2,1)}) custom-call(s32[16]{0:T(128)} %counts_ref.7, s32[1]{0:T(128)} %bitcast.2.lev_ref, bf16[32,6,32,256]{3,2,1,0:T(8,128)(2,1)} %all-to-all-done.recv_ref, ...), custom_call_target="tpu_custom_call" | custom-call | flops 1150000000 | tf_op jit(solution)/shard_map/observe/pallas_call | solution.py:222
  65.4 2.4 %collective-permute-start.1 = (bf16[1840,128]{1,0:T(8,128)(2,1)}, bf16[1840,128]{1,0:T(8,128)(2,1)S(1)}, u32[]{:S(2)}, u32[]{:S(2)}) collective-permute-start(bf16[1840,128]{1,0:T(8,128)(2,1)} %get-tuple-element.29), channel_id=1, source_target_pairs={{0,2},{1,3},{2,0},{3,1},{4,6},{5,7},{6,4},{7,5},{8,10},{9,11},{10,... | collective-permute-start | bytes 1413128 | tf_op jit(solution)/shard_map/ppermute | solution.py:484
  69.1 9.6 %all-to-all-start.1 = ((bf16[32,6,32,256]{3,2,1,0:T(8,128)(2,1)}), bf16[32,6,32,256]{3,2,1,0:T(8,128)(2,1)}, u32[]{:S(2)}, u32[]{:S(2)}) async-start(bf16[32,6,32,256]{3,2,1,0:T(8,128)(2,1)} %send_permute.3.rest_0_), calls=%async_computation.1 | async-start | bytes 6291456 | tf_op jit(solution)/shard_map/all_to_all | solution.py:510
  78.8 5.8 %collective-permute-done.1.y2 = bf16[1840,128]{1,0:T(8,128)(2,1)S(1)} collective-permute-done((bf16[1840,128]{1,0:T(8,128)(2,1)}, bf16[1840,128]{1,0:T(8,128)(2,1)S(1)}, u32[]{:S(2)}, u32[]{:S(2)}) %collective-permute-start.1) | collective-permute-done | bytes 471072 | tf_op jit(solution)/shard_map/ppermute | solution.py:484
  84.6 2.3 collective-permute-done.2.y3
  86.9 3.2 %gram.2 = (f32[2,104,128]{2,1,0:T(8,128)S(1)}, f32[2,104,128]{2,1,0:T(8,128)S(1)}, f32[2,104,128]{2,1,0:T(8,128)S(1)}, f32[2,104,128]{2,1,0:T(8,128)S(1)}) custom-call(s32[16]{0:T(128)S(1)} %copy-done.3, s32[1]{0:T(128)} %bitcast.2.lev_ref, bf16[1840,128]{1,0:T(8,128)(2,1)S(1)} %copy-done.5, bf16[1840,128]{1,0:T(8,128)(2,1)S(1)} %collective-permute-done.y1, ...), custom_call_target="tpu_custom_call" | custom-call | flops 230000001024 | tf_op jit(solution)/shard_map/gram/pallas_call | solution.py:305
  90.2 3.1 %collective-permute-start.3 = (f32[2,104,128]{2,1,0:T(8,128)S(1)}, f32[2,104,128]{2,1,0:T(8,128)S(1)}, u32[]{:S(2)}, u32[]{:S(2)}) collective-permute-start(f32[2,104,128]{2,1,0:T(8,128)S(1)} %get-tuple-element.32), channel_id=1, source_target_pairs={{0,1},{1,2},{2,3},{3,0},{4,5},{5,6},{6,7},{7,4},{8,9},{9,10},{10,1... | collective-permute-start | bytes 319496 | tf_op jit(solution)/shard_map/ppermute | solution.py:484
  93.3 1.5 collective-permute-start.4
  96.1 2.6 %collective-permute-done.4.g2 = f32[2,104,128]{2,1,0:T(8,128)S(1)} collective-permute-done((f32[2,104,128]{2,1,0:T(8,128)S(1)}, f32[2,104,128]{2,1,0:T(8,128)S(1)}, u32[]{:S(2)}, u32[]{:S(2)}) %collective-permute-start.4) | collective-permute-done | bytes 106528 | tf_op jit(solution)/shard_map/ppermute | solution.py:484
  98.8 4.8 %newton_schulz.2.rest_0_ = bf16[2,128,128]{2,1,0:T(8,128)(2,1)S(1)} custom-call(f32[2,104,128]{2,1,0:T(8,128)S(1)} %get-tuple-element.31.g0, f32[2,104,128]{2,1,0:T(8,128)S(1)} %collective-permute-done.3.g1, f32[2,104,128]{2,1,0:T(8,128)S(1)} %collective-permute-done.4.g2, f32[2,104,128]{2,1,0:T(8,128)S(1)} %collective-permute-done.5.g3), custom_call_target="tpu_custom_call" | custom-call | flops 8049999872 | tf_op jit(solution)/shard_map/newton_schulz/pallas_call | solution.py:360
  104.4 2.6 %collective-permute-start.7 = (bf16[2,128,128]{2,1,0:T(8,128)(2,1)S(1)}, bf16[2,128,128]{2,1,0:T(8,128)(2,1)S(1)}, u32[]{:S(2)}, u32[]{:S(2)}) collective-permute-start(bf16[2,128,128]{2,1,0:T(8,128)(2,1)S(1)} %newton_schulz.2.rest_0_), channel_id=1, source_target_pairs={{0,2},{1,3},{2,0},{3,1},{4,6},{5,7},{6,4},{7,5},{8,10},{9,11},{10,... | collective-permute-start | bytes 196616 | tf_op jit(solution)/shard_map/ppermute | solution.py:484
  107.6 10.5 %all-to-all-done.1.recv_ref = bf16[32,6,32,256]{3,2,1,0:T(8,128)(2,1)} async-done(((bf16[32,6,32,256]{3,2,1,0:T(8,128)(2,1)}), bf16[32,6,32,256]{3,2,1,0:T(8,128)(2,1)}, u32[]{:S(2)}, u32[]{:S(2)}) %all-to-all-start.1) | async-done | bytes 3145760 | tf_op jit(solution)/shard_map/all_to_all | solution.py:510
  118.1 8.3 %observe.3 = (bf16[6,8,128,256]{3,2,1,0:T(8,128)(2,1)}, bf16[1840,128]{1,0:T(8,128)(2,1)}, bf16[1840,128]{1,0:T(8,128)(2,1)}, bf16[1840,128]{1,0:T(8,128)(2,1)}, bf16[1840,128]{1,0:T(8,128)(2,1)}) custom-call(s32[16]{0:T(128)} %counts_ref.7, s32[1]{0:T(128)} %bitcast.2.lev_ref, bf16[32,6,32,256]{3,2,1,0:T(8,128)(2,1)} %all-to-all-done.1.recv_ref, ...), custom_call_target="tpu_custom_call" | custom-call | flops 23000000512 | tf_op jit(solution)/shard_map/observe/pallas_call | solution.py:222
  126.8 2.5 %collective-permute-start.11 = (bf16[1840,128]{1,0:T(8,128)(2,1)}, bf16[1840,128]{1,0:T(8,128)(2,1)}, u32[]{:S(2)}, u32[]{:S(2)}) collective-permute-start(bf16[1840,128]{1,0:T(8,128)(2,1)} %get-tuple-element.39), channel_id=1, source_target_pairs={{0,3},{1,0},{2,1},{3,2},{4,7},{5,4},{6,5},{7,6},{8,11},{9,8},{10,9... | collective-permute-start | bytes 1413128 | tf_op jit(solution)/shard_map/ppermute | solution.py:484
  129.9 5.4 %apply_weights.2.rest_0_ = bf16[32,6,32,256]{3,2,1,0:T(8,128)(2,1)} custom-call(s32[1]{0:T(128)} %bitcast.2.lev_ref, bf16[2,128,128]{2,1,0:T(8,128)(2,1)} %copy-done.6, bf16[2,128,128]{2,1,0:T(8,128)(2,1)} %copy-done.16, bf16[2,128,128]{2,1,0:T(8,128)(2,1)} %copy-done.17, bf16[2,128,128]{2,1,0:T(8,128)(2,1)} %copy-done.18, ...), custom_call_target="tpu_custom_call" | custom-call | flops 115000000512 | tf_op jit(solution)/shard_map/apply_weights/pallas_call | solution.py:407
  135.4 7.1 %all-to-all-start.2 = ((bf16[32,6,32,256]{3,2,1,0:T(8,128)(2,1)}), bf16[32,6,32,256]{3,2,1,0:T(8,128)(2,1)}, u32[]{:S(2)}, u32[]{:S(2)}) async-start(bf16[32,6,32,256]{3,2,1,0:T(8,128)(2,1)} %apply_weights.2.rest_0_), calls=%async_computation.2 | async-start | bytes 6291456 | tf_op jit(solution)/shard_map/all_to_all | solution.py:528
  142.5 5.1 %collective-permute-done.11.y3 = bf16[1840,128]{1,0:T(8,128)(2,1)} collective-permute-done((bf16[1840,128]{1,0:T(8,128)(2,1)}, bf16[1840,128]{1,0:T(8,128)(2,1)}, u32[]{:S(2)}, u32[]{:S(2)}) %collective-permute-start.11) | collective-permute-done | bytes 471072 | tf_op jit(solution)/shard_map/ppermute | solution.py:484
  147.6 3.5 %collective-permute-done.9.y1 = bf16[1840,128]{1,0:T(8,128)(2,1)} collective-permute-done((bf16[1840,128]{1,0:T(8,128)(2,1)}, bf16[1840,128]{1,0:T(8,128)(2,1)}, u32[]{:S(2)}, u32[]{:S(2)}) %collective-permute-start.9) | collective-permute-done | bytes 471072 | tf_op jit(solution)/shard_map/ppermute | solution.py:484
  153.7 3.3 %gram.3 = (f32[2,104,128]{2,1,0:T(8,128)S(1)}, f32[2,104,128]{2,1,0:T(8,128)S(1)}, f32[2,104,128]{2,1,0:T(8,128)S(1)}, f32[2,104,128]{2,1,0:T(8,128)S(1)}) custom-call(s32[16]{0:T(128)S(1)} %copy-done.4, s32[1]{0:T(128)} %bitcast.2.lev_ref, bf16[1840,128]{1,0:T(8,128)(2,1)S(1)} %copy-done.12, bf16[1840,128]{1,0:T(8,128)(2,1)} %collective-permute-done.9.y1, ...), custom_call_target="tpu_custom_call" | custom-call | flops 230000001024 | tf_op jit(solution)/shard_map/gram/pallas_call | solution.py:305
  157.8 1.8 collective-permute-start.14
  159.6 5.6 %collective-permute-done.12.g1 = f32[2,104,128]{2,1,0:T(8,128)S(1)} collective-permute-done((f32[2,104,128]{2,1,0:T(8,128)S(1)}, f32[2,104,128]{2,1,0:T(8,128)S(1)}, u32[]{:S(2)}, u32[]{:S(2)}) %collective-permute-start.12) | collective-permute-done | bytes 106528 | tf_op jit(solution)/shard_map/ppermute | solution.py:484
  165.7 4.8 %newton_schulz.3.rest_0_ = bf16[2,128,128]{2,1,0:T(8,128)(2,1)S(1)} custom-call(f32[2,104,128]{2,1,0:T(8,128)S(1)} %get-tuple-element.40.g0, f32[2,104,128]{2,1,0:T(8,128)S(1)} %collective-permute-done.12.g1, f32[2,104,128]{2,1,0:T(8,128)S(1)} %collective-permute-done.13.g2, f32[2,104,128]{2,1,0:T(8,128)S(1)} %collective-permute-done.14.g3), custom_call_target="tpu_custom_call" | custom-call | flops 1150000000 | tf_op jit(solution)/shard_map/newton_schulz/pallas_call | solution.py:360
  170.6 3.2 %collective-permute-start.16 = (bf16[2,128,128]{2,1,0:T(8,128)(2,1)S(1)}, bf16[2,128,128]{2,1,0:T(8,128)(2,1)S(1)}, u32[]{:S(2)}, u32[]{:S(2)}) collective-permute-start(bf16[2,128,128]{2,1,0:T(8,128)(2,1)S(1)} %newton_schulz.3.rest_0_), channel_id=1, source_target_pairs={{0,2},{1,3},{2,0},{3,1},{4,6},{5,7},{6,4},{7,5},{8,10},{9,11},{10,... | collective-permute-start | bytes 196616 | tf_op jit(solution)/shard_map/ppermute | solution.py:484
  173.8 1.5 collective-permute-done.15.rest_1_
  175.3 1.5 collective-permute-done.16.rest_2_
  178.7 5.4 %apply_weights.3 = bf16[32,6,32,256]{3,2,1,0:T(8,128)(2,1)} custom-call(s32[1]{0:T(128)} %bitcast.2.lev_ref, bf16[2,128,128]{2,1,0:T(8,128)(2,1)} %copy-done.2, bf16[2,128,128]{2,1,0:T(8,128)(2,1)} %copy-done.13, bf16[2,128,128]{2,1,0:T(8,128)(2,1)} %copy-done.14, bf16[2,128,128]{2,1,0:T(8,128)(2,1)} %copy-done.15, ...), custom_call_target="tpu_custom_call" | custom-call | flops 1150000000 | tf_op jit(solution)/shard_map/apply_weights/pallas_call | solution.py:407
  184.1 46.4 %all_to_all.20.refs_1_ = bf16[32,6,32,256]{3,2,1,0:T(8,128)(2,1)S(1)} all-to-all(bf16[32,6,32,256]{3,2,1,0:T(8,128)(2,1)} %apply_weights.3), channel_id=1, replica_groups=mesh['patch'=32,'lev'=4] {'patch'}, dimensions={0} | all-to-all | bytes 6291456 | tf_op jit(solution)/shard_map/all_to_all | solution.py:528
  230.5 6.5 %restore_order.1 = bf16[4,6,512,256]{3,2,1,0:T(8,128)(2,1)} custom-call(s32[1,512]{1,0:T(1,128)S(1)} %bitcast.22, bf16[32,6,32,256]{3,2,1,0:T(8,128)(2,1)} %all-to-all-done.2.refs_0_, bf16[32,6,32,256]{3,2,1,0:T(8,128)(2,1)S(1)} %all_to_all.20.refs_1_), custom_call_target="tpu_custom_call" | custom-call | flops 6899999744 | tf_op jit(solution)/shard_map/restore_order/pallas_call | solution.py:463
  (62 shorter events, 13.4 us)
Async XLA Ops:
  0.0 15.2 %copy-start = (bf16[4,6,8192]{2,0,1:T(4,128)(2,1)S(1)}, bf16[4,6,8192]{2,0,1:T(4,128)(2,1)}, u32[]{:S(2)}) copy-start(bf16[4,6,8192]{2,0,1:T(4,128)(2,1)} %param.11) | copy-start | bytes 1179652
  5.5 48.9 %all-to-all-start = ((bf16[32,6,32,256]{3,2,1,0:T(8,128)(2,1)}), bf16[32,6,32,256]{3,2,1,0:T(8,128)(2,1)}, u32[]{:S(2)}, u32[]{:S(2)}) async-start(bf16[32,6,32,256]{3,2,1,0:T(8,128)(2,1)} %send_permute.2), calls=%async_computation | async-start | bytes 6291456 | tf_op jit(solution)/shard_map/all_to_all | solution.py:510
  64.2 14.6 %collective-permute-start = (bf16[1840,128]{1,0:T(8,128)(2,1)}, bf16[1840,128]{1,0:T(8,128)(2,1)S(1)}, u32[]{:S(2)}, u32[]{:S(2)}) collective-permute-start(bf16[1840,128]{1,0:T(8,128)(2,1)} %get-tuple-element.28), channel_id=1, source_target_pairs={{0,1},{1,2},{2,3},{3,0},{4,5},{5,6},{6,7},{7,4},{8,9},{9,10},{10,1... | collective-permute-start | bytes 1413128 | tf_op jit(solution)/shard_map/ppermute | solution.py:484
  65.4 19.1 %collective-permute-start.1 = (bf16[1840,128]{1,0:T(8,128)(2,1)}, bf16[1840,128]{1,0:T(8,128)(2,1)S(1)}, u32[]{:S(2)}, u32[]{:S(2)}) collective-permute-start(bf16[1840,128]{1,0:T(8,128)(2,1)} %get-tuple-element.29), channel_id=1, source_target_pairs={{0,2},{1,3},{2,0},{3,1},{4,6},{5,7},{6,4},{7,5},{8,10},{9,11},{10,... | collective-permute-start | bytes 1413128 | tf_op jit(solution)/shard_map/ppermute | solution.py:484
  67.9 19.0 %copy-start.3 = (s32[16]{0:T(128)S(1)}, s32[16]{0:T(128)}, u32[]{:S(2)}) copy-start(s32[16]{0:T(128)} %counts_ref.7) | copy-start | bytes 196
  67.9 19.0 %copy-start.5 = (bf16[1840,128]{1,0:T(8,128)(2,1)S(1)}, bf16[1840,128]{1,0:T(8,128)(2,1)}, u32[]{:S(2)}) copy-start(bf16[1840,128]{1,0:T(8,128)(2,1)} %get-tuple-element.27.y0) | copy-start | bytes 1413124
  67.9 19.0 %copy-start.7 = (f32[8192]{0:T(1024)S(1)}, f32[8192]{0:T(1024)}, u32[]{:S(2)}) copy-start(f32[8192]{0:T(1024)} %param.12) | copy-start | bytes 98308
  67.9 19.0 %copy-start.9 = (f32[8192]{0:T(1024)S(1)}, f32[8192]{0:T(1024)}, u32[]{:S(2)}) copy-start(f32[8192]{0:T(1024)} %param.13) | copy-start | bytes 98308
  67.9 19.0 %collective-permute-start.2 = (bf16[1840,128]{1,0:T(8,128)(2,1)}, bf16[1840,128]{1,0:T(8,128)(2,1)S(1)}, u32[]{:S(2)}, u32[]{:S(2)}) collective-permute-start(bf16[1840,128]{1,0:T(8,128)(2,1)} %get-tuple-element.30), channel_id=1, source_target_pairs={{0,3},{1,0},{2,1},{3,2},{4,7},{5,4},{6,5},{7,6},{8,11},{9,8},{10,9... | collective-permute-start | bytes 1413128 | tf_op jit(solution)/shard_map/ppermute | solution.py:484
  69.1 49.0 %all-to-all-start.1 = ((bf16[32,6,32,256]{3,2,1,0:T(8,128)(2,1)}), bf16[32,6,32,256]{3,2,1,0:T(8,128)(2,1)}, u32[]{:S(2)}, u32[]{:S(2)}) async-start(bf16[32,6,32,256]{3,2,1,0:T(8,128)(2,1)} %send_permute.3.rest_0_), calls=%async_computation.1 | async-start | bytes 6291456 | tf_op jit(solution)/shard_map/all_to_all | solution.py:510
  90.2 6.0 %collective-permute-start.3 = (f32[2,104,128]{2,1,0:T(8,128)S(1)}, f32[2,104,128]{2,1,0:T(8,128)S(1)}, u32[]{:S(2)}, u32[]{:S(2)}) collective-permute-start(f32[2,104,128]{2,1,0:T(8,128)S(1)} %get-tuple-element.32), channel_id=1, source_target_pairs={{0,1},{1,2},{2,3},{3,0},{4,5},{5,6},{6,7},{7,4},{8,9},{9,10},{10,1... | collective-permute-start | bytes 319496 | tf_op jit(solution)/shard_map/ppermute | solution.py:484
  93.3 5.5 %collective-permute-start.4 = (f32[2,104,128]{2,1,0:T(8,128)S(1)}, f32[2,104,128]{2,1,0:T(8,128)S(1)}, u32[]{:S(2)}, u32[]{:S(2)}) collective-permute-start(f32[2,104,128]{2,1,0:T(8,128)S(1)} %get-tuple-element.33), channel_id=1, source_target_pairs={{0,2},{1,3},{2,0},{3,1},{4,6},{5,7},{6,4},{7,5},{8,10},{9,11},{10,... | collective-permute-start | bytes 319496 | tf_op jit(solution)/shard_map/ppermute | solution.py:484
  94.8 4.0 %collective-permute-start.5 = (f32[2,104,128]{2,1,0:T(8,128)S(1)}, f32[2,104,128]{2,1,0:T(8,128)S(1)}, u32[]{:S(2)}, u32[]{:S(2)}) collective-permute-start(f32[2,104,128]{2,1,0:T(8,128)S(1)} %get-tuple-element.34), channel_id=1, source_target_pairs={{0,3},{1,0},{2,1},{3,2},{4,7},{5,4},{6,5},{7,6},{8,11},{9,8},{10,9... | collective-permute-start | bytes 319496 | tf_op jit(solution)/shard_map/ppermute | solution.py:484
  103.6 14.5 %copy-start.6 = (bf16[2,128,128]{2,1,0:T(8,128)(2,1)}, bf16[2,128,128]{2,1,0:T(8,128)(2,1)S(1)}, u32[]{:S(2)}) copy-start(bf16[2,128,128]{2,1,0:T(8,128)(2,1)S(1)} %newton_schulz.2.rest_0_) | copy-start | bytes 196612
  103.6 25.7 %collective-permute-start.6 = (bf16[2,128,128]{2,1,0:T(8,128)(2,1)S(1)}, bf16[2,128,128]{2,1,0:T(8,128)(2,1)S(1)}, u32[]{:S(2)}, u32[]{:S(2)}) collective-permute-start(bf16[2,128,128]{2,1,0:T(8,128)(2,1)S(1)} %newton_schulz.2.rest_0_), channel_id=1, source_target_pairs={{0,1},{1,2},{2,3},{3,0},{4,5},{5,6},{6,7},{7,4},{8,9},{9,10},{10,1... | collective-permute-start | bytes 196616 | tf_op jit(solution)/shard_map/ppermute | solution.py:484
  104.4 24.8 %collective-permute-start.7 = (bf16[2,128,128]{2,1,0:T(8,128)(2,1)S(1)}, bf16[2,128,128]{2,1,0:T(8,128)(2,1)S(1)}, u32[]{:S(2)}, u32[]{:S(2)}) collective-permute-start(bf16[2,128,128]{2,1,0:T(8,128)(2,1)S(1)} %newton_schulz.2.rest_0_), channel_id=1, source_target_pairs={{0,2},{1,3},{2,0},{3,1},{4,6},{5,7},{6,4},{7,5},{8,10},{9,11},{10,... | collective-permute-start | bytes 196616 | tf_op jit(solution)/shard_map/ppermute | solution.py:484
  107.0 22.3 %collective-permute-start.8 = (bf16[2,128,128]{2,1,0:T(8,128)(2,1)S(1)}, bf16[2,128,128]{2,1,0:T(8,128)(2,1)S(1)}, u32[]{:S(2)}, u32[]{:S(2)}) collective-permute-start(bf16[2,128,128]{2,1,0:T(8,128)(2,1)S(1)} %newton_schulz.2.rest_0_), channel_id=1, source_target_pairs={{0,3},{1,0},{2,1},{3,2},{4,7},{5,4},{6,5},{7,6},{8,11},{9,8},{10,9... | collective-permute-start | bytes 196616 | tf_op jit(solution)/shard_map/ppermute | solution.py:484
  126.4 16.0 %collective-permute-start.10 = (bf16[1840,128]{1,0:T(8,128)(2,1)}, bf16[1840,128]{1,0:T(8,128)(2,1)}, u32[]{:S(2)}, u32[]{:S(2)}) collective-permute-start(bf16[1840,128]{1,0:T(8,128)(2,1)} %get-tuple-element.38), channel_id=1, source_target_pairs={{0,2},{1,3},{2,0},{3,1},{4,6},{5,7},{6,4},{7,5},{8,10},{9,11},{10,... | collective-permute-start | bytes 1413128 | tf_op jit(solution)/shard_map/ppermute | solution.py:484
  126.8 20.8 %collective-permute-start.11 = (bf16[1840,128]{1,0:T(8,128)(2,1)}, bf16[1840,128]{1,0:T(8,128)(2,1)}, u32[]{:S(2)}, u32[]{:S(2)}) collective-permute-start(bf16[1840,128]{1,0:T(8,128)(2,1)} %get-tuple-element.39), channel_id=1, source_target_pairs={{0,3},{1,0},{2,1},{3,2},{4,7},{5,4},{6,5},{7,6},{8,11},{9,8},{10,9... | collective-permute-start | bytes 1413128 | tf_op jit(solution)/shard_map/ppermute | solution.py:484
  129.2 21.9 %collective-permute-start.9 = (bf16[1840,128]{1,0:T(8,128)(2,1)}, bf16[1840,128]{1,0:T(8,128)(2,1)}, u32[]{:S(2)}, u32[]{:S(2)}) collective-permute-start(bf16[1840,128]{1,0:T(8,128)(2,1)} %get-tuple-element.37), channel_id=1, source_target_pairs={{0,1},{1,2},{2,3},{3,0},{4,5},{5,6},{6,7},{7,4},{8,9},{9,10},{10,1... | collective-permute-start | bytes 1413128 | tf_op jit(solution)/shard_map/ppermute | solution.py:484
  135.4 15.8 %copy-start.1 = (bf16[32,6,32,256]{3,2,1,0:T(8,128)(2,1)S(1)}, bf16[32,6,32,256]{3,2,1,0:T(8,128)(2,1)}, u32[]{:S(2)}) copy-start(bf16[32,6,32,256]{3,2,1,0:T(8,128)(2,1)} %apply_weights.2.rest_0_) | copy-start | bytes 9437188
  135.4 15.8 %copy-start.4 = (s32[16]{0:T(128)S(1)}, s32[16]{0:T(128)}, u32[]{:S(2)}) copy-start(s32[16]{0:T(128)} %counts_ref.7) | copy-start | bytes 196
  135.4 48.7 %all-to-all-start.2 = ((bf16[32,6,32,256]{3,2,1,0:T(8,128)(2,1)}), bf16[32,6,32,256]{3,2,1,0:T(8,128)(2,1)}, u32[]{:S(2)}, u32[]{:S(2)}) async-start(bf16[32,6,32,256]{3,2,1,0:T(8,128)(2,1)} %apply_weights.2.rest_0_), calls=%async_computation.2 | async-start | bytes 6291456 | tf_op jit(solution)/shard_map/all_to_all | solution.py:528
  157.0 8.3 %collective-permute-start.12 = (f32[2,104,128]{2,1,0:T(8,128)S(1)}, f32[2,104,128]{2,1,0:T(8,128)S(1)}, u32[]{:S(2)}, u32[]{:S(2)}) collective-permute-start(f32[2,104,128]{2,1,0:T(8,128)S(1)} %get-tuple-element.41), channel_id=1, source_target_pairs={{0,1},{1,2},{2,3},{3,0},{4,5},{5,6},{6,7},{7,4},{8,9},{9,10},{10,1... | collective-permute-start | bytes 319496 | tf_op jit(solution)/shard_map/ppermute | solution.py:484
  157.0 8.3 %collective-permute-start.13 = (f32[2,104,128]{2,1,0:T(8,128)S(1)}, f32[2,104,128]{2,1,0:T(8,128)S(1)}, u32[]{:S(2)}, u32[]{:S(2)}) collective-permute-start(f32[2,104,128]{2,1,0:T(8,128)S(1)} %get-tuple-element.42), channel_id=1, source_target_pairs={{0,2},{1,3},{2,0},{3,1},{4,6},{5,7},{6,4},{7,5},{8,10},{9,11},{10,... | collective-permute-start | bytes 319496 | tf_op jit(solution)/shard_map/ppermute | solution.py:484
  157.8 7.9 %collective-permute-start.14 = (f32[2,104,128]{2,1,0:T(8,128)S(1)}, f32[2,104,128]{2,1,0:T(8,128)S(1)}, u32[]{:S(2)}, u32[]{:S(2)}) collective-permute-start(f32[2,104,128]{2,1,0:T(8,128)S(1)} %get-tuple-element.43), channel_id=1, source_target_pairs={{0,3},{1,0},{2,1},{3,2},{4,7},{5,4},{6,5},{7,6},{8,11},{9,8},{10,9... | collective-permute-start | bytes 319496 | tf_op jit(solution)/shard_map/ppermute | solution.py:484
  170.5 7.5 %copy-start.2 = (bf16[2,128,128]{2,1,0:T(8,128)(2,1)}, bf16[2,128,128]{2,1,0:T(8,128)(2,1)S(1)}, u32[]{:S(2)}) copy-start(bf16[2,128,128]{2,1,0:T(8,128)(2,1)S(1)} %newton_schulz.3.rest_0_) | copy-start | bytes 196612
  170.5 4.8 %collective-permute-start.15 = (bf16[2,128,128]{2,1,0:T(8,128)(2,1)S(1)}, bf16[2,128,128]{2,1,0:T(8,128)(2,1)S(1)}, u32[]{:S(2)}, u32[]{:S(2)}) collective-permute-start(bf16[2,128,128]{2,1,0:T(8,128)(2,1)S(1)} %newton_schulz.3.rest_0_), channel_id=1, source_target_pairs={{0,1},{1,2},{2,3},{3,0},{4,5},{5,6},{6,7},{7,4},{8,9},{9,10},{10,1... | collective-permute-start | bytes 196616 | tf_op jit(solution)/shard_map/ppermute | solution.py:484
  170.6 6.1 %collective-permute-start.16 = (bf16[2,128,128]{2,1,0:T(8,128)(2,1)S(1)}, bf16[2,128,128]{2,1,0:T(8,128)(2,1)S(1)}, u32[]{:S(2)}, u32[]{:S(2)}) collective-permute-start(bf16[2,128,128]{2,1,0:T(8,128)(2,1)S(1)} %newton_schulz.3.rest_0_), channel_id=1, source_target_pairs={{0,2},{1,3},{2,0},{3,1},{4,6},{5,7},{6,4},{7,5},{8,10},{9,11},{10,... | collective-permute-start | bytes 196616 | tf_op jit(solution)/shard_map/ppermute | solution.py:484
  173.8 4.2 %collective-permute-start.17 = (bf16[2,128,128]{2,1,0:T(8,128)(2,1)S(1)}, bf16[2,128,128]{2,1,0:T(8,128)(2,1)S(1)}, u32[]{:S(2)}, u32[]{:S(2)}) collective-permute-start(bf16[2,128,128]{2,1,0:T(8,128)(2,1)S(1)} %newton_schulz.3.rest_0_), channel_id=1, source_target_pairs={{0,3},{1,0},{2,1},{3,2},{4,7},{5,4},{6,5},{7,6},{8,11},{9,8},{10,9... | collective-permute-start | bytes 196616 | tf_op jit(solution)/shard_map/ppermute | solution.py:484
  175.3 2.7 %copy-start.13 = (bf16[2,128,128]{2,1,0:T(8,128)(2,1)}, bf16[2,128,128]{2,1,0:T(8,128)(2,1)S(1)}, u32[]{:S(2)}) copy-start(bf16[2,128,128]{2,1,0:T(8,128)(2,1)S(1)} %collective-permute-done.15.rest_1_) | copy-start | bytes 196612
  184.1 46.4 %copy-start.11 = (s32[512]{0:T(512)S(1)}, s32[512]{0:T(512)}, u32[]{:S(2)}) copy-start(s32[512]{0:T(512)} %param.8) | copy-start | bytes 6148
  (8 other events, 6.3 us)

commit v4 on v3

--- a/solution.py
+++ b/solution.py
@@ -203,14 +203,14 @@
         return base + count
 
     lax.fori_loop(0, slots, slot_step, jnp.int32(0))
+    outs = [pltpu.make_async_copy(y_buf.at[d], y_refs[d], y_sem.at[d]) for d in range(4)]
     for d in range(4):
         mean = mean_ref[d]
         hi = mean.astype(BF16)
         mid = (mean - hi.astype(F32)).astype(BF16)
         low = (mean - hi.astype(F32) - mid.astype(F32)).astype(BF16)
         y_buf[d, y_buf.shape[1] - 48 :, :] = jnp.concatenate([hi, mid, low], axis=0)
-    outs = [pltpu.make_async_copy(y_buf.at[d], y_refs[d], y_sem.at[d]) for d in range(4)]
-    start(outs)
+        outs[d].start()
     wait(outs)
     wait(stores)
 
@@ -480,9 +480,10 @@
 
 
 def exchange(blocks):
-    return [blocks[0]] + [
-        lax.ppermute(blocks[d], "lev", [(i, (i + d) % 4) for i in range(4)]) for d in range(1, 4)
-    ]
+    came = {0: blocks[0]}
+    for d in (2, 1, 3):
+        came[d] = lax.ppermute(blocks[d], "lev", [(i, (i + d) % 4) for i in range(4)])
+    return [came[d] for d in range(4)]
 
 
 def body(background, patch_order, tile_counts, obs_column, obs_operator, obs_value, obs_weight):

time: 236 us -> 235 us (level)
  starting transfers between devices: 49.7 us -> 46.8 us
    ppermute x18, waiting for transfers between devices: 30 us -> 33.5 us  [exchange(): lax.ppermute(blocks[d], 'lev', [(i, (i + d) % 4) for i in range(4)])]
  transfers between devices with their start and end apart: 21 -> 21, of which waited for: 13 -> 12; matrix products, arithmetic and copies ran while one was open for 1% -> 1% of each run, Pallas kernels for 17% -> 17%
where the time goes in v4:
time: 235 us; the launch traced here: 234 us
  waiting for transfers between devices  74.3 us (32%)
  Pallas kernels  60.6 us (26%)
  blocking collectives  46.9 us (20%)
  starting transfers between devices  46.8 us (20%)
  local copies, waits for them, and re-layouts  4.41 us (2%)
    all_to_all x1, blocking collectives, analyse(): lax.all_to_all(out, 'patch', split_axis=0, concat_axis=0, tiled=True)  46.9 us
    all_to_all x2, waiting for transfers between devices, body(): lax.all_to_all(sent, 'patch', split_axis=0, concat_axis=0, tiled=True)  40.8 us
    ppermute x18, waiting for transfers between devices, exchange(): lax.ppermute(blocks[d], 'lev', [(i, (i + d) % 4) for i in range(4)])  33.5 us
    ppermute x18, starting transfers between devices, exchange(): lax.ppermute(blocks[d], 'lev', [(i, (i + d) % 4) for i in range(4)])  21.5 us
    all_to_all x2, starting transfers between devices, body(): lax.all_to_all(sent, 'patch', split_axis=0, concat_axis=0, tiled=True)  17.5 us
    pallas_call x2, Pallas kernels, observe(): pl.pallas_call(functools.partial(observe_kernel, first), in_specs=[smem()...  17.1 us
    pallas_call x2, Pallas kernels, send(): pl.pallas_call(functools.partial(send_kernel, first), in_specs=[vmem(), h...  11 us
    pallas_call x2, Pallas kernels, apply(): pl.pallas_call(apply_kernel, in_specs=[smem()] + [hbm()] * 5 + [hbm() for...  10.9 us
  transfers between devices with their start and end apart: 21, of which 12 were waited for; matrix products, arithmetic and copies ran while one was open for 1% of the time, Pallas kernels for 17%

profile of v4, /device:TPU:1, one launch (start us, length us, event | category | flops | bytes accessed | tf_op | source)
XLA Modules:
  0.0 234.2 jit_solution(14415330191575991767)
XLA Ops:
  0.0 5.5 %send_permute.2 = bf16[32,6,32,256]{3,2,1,0:T(8,128)(2,1)} custom-call(s32[1,512]{1,0:T(1,128)} %bitcast.20, bf16[4,6,512,256]{3,2,1,0:T(8,128)(2,1)} %bitcast.26), custom_call_target="tpu_custom_call" | custom-call | flops 5750000128 | tf_op jit(solution)/shard_map/send_permute/pallas_call | solution.py:98
  5.5 9.7 %all-to-all-start = ((bf16[32,6,32,256]{3,2,1,0:T(8,128)(2,1)}), bf16[32,6,32,256]{3,2,1,0:T(8,128)(2,1)}, u32[]{:S(2)}, u32[]{:S(2)}) async-start(bf16[32,6,32,256]{3,2,1,0:T(8,128)(2,1)} %send_permute.2), calls=%async_computation | async-start | bytes 6291456 | tf_op jit(solution)/shard_map/all_to_all | solution.py:511
  16.5 5.5 %send_permute.3.rest_0_ = bf16[32,6,32,256]{3,2,1,0:T(8,128)(2,1)} custom-call(s32[1,512]{1,0:T(1,128)} %bitcast.21, bf16[4,6,512,256]{3,2,1,0:T(8,128)(2,1)} %bitcast.27), custom_call_target="tpu_custom_call" | custom-call | flops 5750000128 | tf_op jit(solution)/shard_map/send_permute/pallas_call | solution.py:98
  22.0 32.4 %all-to-all-done.recv_ref = bf16[32,6,32,256]{3,2,1,0:T(8,128)(2,1)} async-done(((bf16[32,6,32,256]{3,2,1,0:T(8,128)(2,1)}), bf16[32,6,32,256]{3,2,1,0:T(8,128)(2,1)}, u32[]{:S(2)}, u32[]{:S(2)}) %all-to-all-start) | async-done | bytes 3145760 | tf_op jit(solution)/shard_map/all_to_all | solution.py:511
  54.4 8.9 %observe.2 = (bf16[6,8,128,256]{3,2,1,0:T(8,128)(2,1)}, bf16[1840,128]{1,0:T(8,128)(2,1)}, bf16[1840,128]{1,0:T(8,128)(2,1)}, bf16[1840,128]{1,0:T(8,128)(2,1)}, bf16[1840,128]{1,0:T(8,128)(2,1)}) custom-call(s32[16]{0:T(128)} %counts_ref.7, s32[1]{0:T(128)} %bitcast.2.lev_ref, bf16[32,6,32,256]{3,2,1,0:T(8,128)(2,1)} %all-to-all-done.recv_ref, ...), custom_call_target="tpu_custom_call" | custom-call | flops 1150000000 | tf_op jit(solution)/shard_map/observe/pallas_call | solution.py:222
  64.6 2.5 %collective-permute-start.1 = (bf16[1840,128]{1,0:T(8,128)(2,1)}, bf16[1840,128]{1,0:T(8,128)(2,1)S(1)}, u32[]{:S(2)}, u32[]{:S(2)}) collective-permute-start(bf16[1840,128]{1,0:T(8,128)(2,1)} %get-tuple-element.29), channel_id=1, source_target_pairs={{0,2},{1,3},{2,0},{3,1},{4,6},{5,7},{6,4},{7,5},{8,10},{9,11},{10,... | collective-permute-start | bytes 1413128 | tf_op jit(solution)/shard_map/ppermute | solution.py:485
  68.3 7.8 %all-to-all-start.1 = ((bf16[32,6,32,256]{3,2,1,0:T(8,128)(2,1)}), bf16[32,6,32,256]{3,2,1,0:T(8,128)(2,1)}, u32[]{:S(2)}, u32[]{:S(2)}) async-start(bf16[32,6,32,256]{3,2,1,0:T(8,128)(2,1)} %send_permute.3.rest_0_), calls=%async_computation.1 | async-start | bytes 6291456 | tf_op jit(solution)/shard_map/all_to_all | solution.py:511
  76.1 9.6 %collective-permute-done.1.y2 = bf16[1840,128]{1,0:T(8,128)(2,1)S(1)} collective-permute-done((bf16[1840,128]{1,0:T(8,128)(2,1)}, bf16[1840,128]{1,0:T(8,128)(2,1)S(1)}, u32[]{:S(2)}, u32[]{:S(2)}) %collective-permute-start.1) | collective-permute-done | bytes 471072 | tf_op jit(solution)/shard_map/ppermute | solution.py:485
  85.7 1.6 collective-permute-done.2.y3
  87.3 2.5 %gram.2 = (f32[2,104,128]{2,1,0:T(8,128)S(1)}, f32[2,104,128]{2,1,0:T(8,128)S(1)}, f32[2,104,128]{2,1,0:T(8,128)S(1)}, f32[2,104,128]{2,1,0:T(8,128)S(1)}) custom-call(s32[16]{0:T(128)S(1)} %copy-done.3, s32[1]{0:T(128)} %bitcast.2.lev_ref, bf16[1840,128]{1,0:T(8,128)(2,1)S(1)} %copy-done.5, bf16[1840,128]{1,0:T(8,128)(2,1)S(1)} %collective-permute-done.y1, ...), custom_call_target="tpu_custom_call" | custom-call | flops 230000001024 | tf_op jit(solution)/shard_map/gram/pallas_call | solution.py:305
  89.8 1.9 collective-permute-start.3
  91.7 2.5 %collective-permute-start.4 = (f32[2,104,128]{2,1,0:T(8,128)S(1)}, f32[2,104,128]{2,1,0:T(8,128)S(1)}, u32[]{:S(2)}, u32[]{:S(2)}) collective-permute-start(f32[2,104,128]{2,1,0:T(8,128)S(1)} %get-tuple-element.33), channel_id=1, source_target_pairs={{0,2},{1,3},{2,0},{3,1},{4,6},{5,7},{6,4},{7,5},{8,10},{9,11},{10,... | collective-permute-start | bytes 319496 | tf_op jit(solution)/shard_map/ppermute | solution.py:485
  94.2 1.3 collective-permute-done.3.g1
  95.5 3.8 %collective-permute-done.4.g2 = f32[2,104,128]{2,1,0:T(8,128)S(1)} collective-permute-done((f32[2,104,128]{2,1,0:T(8,128)S(1)}, f32[2,104,128]{2,1,0:T(8,128)S(1)}, u32[]{:S(2)}, u32[]{:S(2)}) %collective-permute-start.4) | collective-permute-done | bytes 106528 | tf_op jit(solution)/shard_map/ppermute | solution.py:485
  99.3 4.8 %newton_schulz.2.rest_0_ = bf16[2,128,128]{2,1,0:T(8,128)(2,1)S(1)} custom-call(f32[2,104,128]{2,1,0:T(8,128)S(1)} %get-tuple-element.31.g0, f32[2,104,128]{2,1,0:T(8,128)S(1)} %collective-permute-done.3.g1, f32[2,104,128]{2,1,0:T(8,128)S(1)} %collective-permute-done.4.g2, f32[2,104,128]{2,1,0:T(8,128)S(1)} %collective-permute-done.5.g3), custom_call_target="tpu_custom_call" | custom-call | flops 8049999872 | tf_op jit(solution)/shard_map/newton_schulz/pallas_call | solution.py:360
  104.2 2.0 collective-permute-start.7
  106.9 8.5 %all-to-all-done.1.recv_ref = bf16[32,6,32,256]{3,2,1,0:T(8,128)(2,1)} async-done(((bf16[32,6,32,256]{3,2,1,0:T(8,128)(2,1)}), bf16[32,6,32,256]{3,2,1,0:T(8,128)(2,1)}, u32[]{:S(2)}, u32[]{:S(2)}) %all-to-all-start.1) | async-done | bytes 3145760 | tf_op jit(solution)/shard_map/all_to_all | solution.py:511
  115.4 8.2 %observe.3 = (bf16[6,8,128,256]{3,2,1,0:T(8,128)(2,1)}, bf16[1840,128]{1,0:T(8,128)(2,1)}, bf16[1840,128]{1,0:T(8,128)(2,1)}, bf16[1840,128]{1,0:T(8,128)(2,1)}, bf16[1840,128]{1,0:T(8,128)(2,1)}) custom-call(s32[16]{0:T(128)} %counts_ref.7, s32[1]{0:T(128)} %bitcast.2.lev_ref, bf16[32,6,32,256]{3,2,1,0:T(8,128)(2,1)} %all-to-all-done.1.recv_ref, ...), custom_call_target="tpu_custom_call" | custom-call | flops 23000000512 | tf_op jit(solution)/shard_map/observe/pallas_call | solution.py:222
  123.9 2.5 %collective-permute-start.11 = (bf16[1840,128]{1,0:T(8,128)(2,1)}, bf16[1840,128]{1,0:T(8,128)(2,1)}, u32[]{:S(2)}, u32[]{:S(2)}) collective-permute-start(bf16[1840,128]{1,0:T(8,128)(2,1)} %get-tuple-element.39), channel_id=1, source_target_pairs={{0,3},{1,0},{2,1},{3,2},{4,7},{5,4},{6,5},{7,6},{8,11},{9,8},{10,9... | collective-permute-start | bytes 1413128 | tf_op jit(solution)/shard_map/ppermute | solution.py:485
  127.1 5.4 %apply_weights.2.rest_0_ = bf16[32,6,32,256]{3,2,1,0:T(8,128)(2,1)} custom-call(s32[1]{0:T(128)} %bitcast.2.lev_ref, bf16[2,128,128]{2,1,0:T(8,128)(2,1)} %copy-done.6, bf16[2,128,128]{2,1,0:T(8,128)(2,1)} %copy-done.16, bf16[2,128,128]{2,1,0:T(8,128)(2,1)} %copy-done.17, bf16[2,128,128]{2,1,0:T(8,128)(2,1)} %copy-done.18, ...), custom_call_target="tpu_custom_call" | custom-call | flops 115000000512 | tf_op jit(solution)/shard_map/apply_weights/pallas_call | solution.py:407
  132.6 7.8 %all-to-all-start.2 = ((bf16[32,6,32,256]{3,2,1,0:T(8,128)(2,1)}), bf16[32,6,32,256]{3,2,1,0:T(8,128)(2,1)}, u32[]{:S(2)}, u32[]{:S(2)}) async-start(bf16[32,6,32,256]{3,2,1,0:T(8,128)(2,1)} %apply_weights.2.rest_0_), calls=%async_computation.2 | async-start | bytes 6291456 | tf_op jit(solution)/shard_map/all_to_all | solution.py:529
  140.4 4.4 %collective-permute-done.11.y3 = bf16[1840,128]{1,0:T(8,128)(2,1)} collective-permute-done((bf16[1840,128]{1,0:T(8,128)(2,1)}, bf16[1840,128]{1,0:T(8,128)(2,1)}, u32[]{:S(2)}, u32[]{:S(2)}) %collective-permute-start.11) | collective-permute-done | bytes 471072 | tf_op jit(solution)/shard_map/ppermute | solution.py:485
  144.8 3.5 %collective-permute-done.9.y1 = bf16[1840,128]{1,0:T(8,128)(2,1)} collective-permute-done((bf16[1840,128]{1,0:T(8,128)(2,1)}, bf16[1840,128]{1,0:T(8,128)(2,1)}, u32[]{:S(2)}, u32[]{:S(2)}) %collective-permute-start.9) | collective-permute-done | bytes 471072 | tf_op jit(solution)/shard_map/ppermute | solution.py:485
  150.9 3.0 %gram.3 = (f32[2,104,128]{2,1,0:T(8,128)S(1)}, f32[2,104,128]{2,1,0:T(8,128)S(1)}, f32[2,104,128]{2,1,0:T(8,128)S(1)}, f32[2,104,128]{2,1,0:T(8,128)S(1)}) custom-call(s32[16]{0:T(128)S(1)} %copy-done.4, s32[1]{0:T(128)} %bitcast.2.lev_ref, bf16[1840,128]{1,0:T(8,128)(2,1)S(1)} %copy-done.12, bf16[1840,128]{1,0:T(8,128)(2,1)} %collective-permute-done.9.y1, ...), custom_call_target="tpu_custom_call" | custom-call | flops 230000001024 | tf_op jit(solution)/shard_map/gram/pallas_call | solution.py:305
  155.0 1.6 collective-permute-start.14
  156.6 5.3 %collective-permute-done.12.g1 = f32[2,104,128]{2,1,0:T(8,128)S(1)} collective-permute-done((f32[2,104,128]{2,1,0:T(8,128)S(1)}, f32[2,104,128]{2,1,0:T(8,128)S(1)}, u32[]{:S(2)}, u32[]{:S(2)}) %collective-permute-start.12) | collective-permute-done | bytes 106528 | tf_op jit(solution)/shard_map/ppermute | solution.py:485
  161.9 4.8 %newton_schulz.3.rest_0_ = bf16[2,128,128]{2,1,0:T(8,128)(2,1)S(1)} custom-call(f32[2,104,128]{2,1,0:T(8,128)S(1)} %get-tuple-element.40.g0, f32[2,104,128]{2,1,0:T(8,128)S(1)} %collective-permute-done.12.g1, f32[2,104,128]{2,1,0:T(8,128)S(1)} %collective-permute-done.13.g2, f32[2,104,128]{2,1,0:T(8,128)S(1)} %collective-permute-done.14.g3), custom_call_target="tpu_custom_call" | custom-call | flops 1150000000 | tf_op jit(solution)/shard_map/newton_schulz/pallas_call | solution.py:360
  167.3 3.3 %collective-permute-start.16 = (bf16[2,128,128]{2,1,0:T(8,128)(2,1)S(1)}, bf16[2,128,128]{2,1,0:T(8,128)(2,1)S(1)}, u32[]{:S(2)}, u32[]{:S(2)}) collective-permute-start(bf16[2,128,128]{2,1,0:T(8,128)(2,1)S(1)} %newton_schulz.3.rest_0_), channel_id=1, source_target_pairs={{0,2},{1,3},{2,0},{3,1},{4,6},{5,7},{6,4},{7,5},{8,10},{9,11},{10,... | collective-permute-start | bytes 196616 | tf_op jit(solution)/shard_map/ppermute | solution.py:485
  171.5 1.8 collective-permute-done.16.rest_2_
  175.2 5.4 %apply_weights.3 = bf16[32,6,32,256]{3,2,1,0:T(8,128)(2,1)} custom-call(s32[1]{0:T(128)} %bitcast.2.lev_ref, bf16[2,128,128]{2,1,0:T(8,128)(2,1)} %copy-done.2, bf16[2,128,128]{2,1,0:T(8,128)(2,1)} %copy-done.13, bf16[2,128,128]{2,1,0:T(8,128)(2,1)} %copy-done.14, bf16[2,128,128]{2,1,0:T(8,128)(2,1)} %copy-done.15, ...), custom_call_target="tpu_custom_call" | custom-call | flops 1150000000 | tf_op jit(solution)/shard_map/apply_weights/pallas_call | solution.py:407
  180.6 46.9 %all_to_all.20.refs_1_ = bf16[32,6,32,256]{3,2,1,0:T(8,128)(2,1)S(1)} all-to-all(bf16[32,6,32,256]{3,2,1,0:T(8,128)(2,1)} %apply_weights.3), channel_id=1, replica_groups=mesh['patch'=32,'lev'=4] {'patch'}, dimensions={0} | all-to-all | bytes 6291456 | tf_op jit(solution)/shard_map/all_to_all | solution.py:529
  227.6 6.5 %restore_order.1 = bf16[4,6,512,256]{3,2,1,0:T(8,128)(2,1)} custom-call(s32[1,512]{1,0:T(1,128)S(1)} %bitcast.22, bf16[32,6,32,256]{3,2,1,0:T(8,128)(2,1)} %all-to-all-done.2.refs_0_, bf16[32,6,32,256]{3,2,1,0:T(8,128)(2,1)S(1)} %all_to_all.20.refs_1_), custom_call_target="tpu_custom_call" | custom-call | flops 6899999744 | tf_op jit(solution)/shard_map/restore_order/pallas_call | solution.py:463
  (62 shorter events, 12.7 us)
Async XLA Ops:
  0.0 15.2 %copy-start = (bf16[4,6,8192]{2,0,1:T(4,128)(2,1)S(1)}, bf16[4,6,8192]{2,0,1:T(4,128)(2,1)}, u32[]{:S(2)}) copy-start(bf16[4,6,8192]{2,0,1:T(4,128)(2,1)} %param.11) | copy-start | bytes 1179652
  5.5 48.9 %all-to-all-start = ((bf16[32,6,32,256]{3,2,1,0:T(8,128)(2,1)}), bf16[32,6,32,256]{3,2,1,0:T(8,128)(2,1)}, u32[]{:S(2)}, u32[]{:S(2)}) async-start(bf16[32,6,32,256]{3,2,1,0:T(8,128)(2,1)} %send_permute.2), calls=%async_computation | async-start | bytes 6291456 | tf_op jit(solution)/shard_map/all_to_all | solution.py:511
  63.3 12.8 %collective-permute-start = (bf16[1840,128]{1,0:T(8,128)(2,1)}, bf16[1840,128]{1,0:T(8,128)(2,1)S(1)}, u32[]{:S(2)}, u32[]{:S(2)}) collective-permute-start(bf16[1840,128]{1,0:T(8,128)(2,1)} %get-tuple-element.28), channel_id=1, source_target_pairs={{0,1},{1,2},{2,3},{3,0},{4,5},{5,6},{6,7},{7,4},{8,9},{9,10},{10,1... | collective-permute-start | bytes 1413128 | tf_op jit(solution)/shard_map/ppermute | solution.py:485
  64.6 21.1 %collective-permute-start.1 = (bf16[1840,128]{1,0:T(8,128)(2,1)}, bf16[1840,128]{1,0:T(8,128)(2,1)S(1)}, u32[]{:S(2)}, u32[]{:S(2)}) collective-permute-start(bf16[1840,128]{1,0:T(8,128)(2,1)} %get-tuple-element.29), channel_id=1, source_target_pairs={{0,2},{1,3},{2,0},{3,1},{4,6},{5,7},{6,4},{7,5},{8,10},{9,11},{10,... | collective-permute-start | bytes 1413128 | tf_op jit(solution)/shard_map/ppermute | solution.py:485
  67.0 20.2 %copy-start.3 = (s32[16]{0:T(128)S(1)}, s32[16]{0:T(128)}, u32[]{:S(2)}) copy-start(s32[16]{0:T(128)} %counts_ref.7) | copy-start | bytes 196
  67.0 20.2 %copy-start.5 = (bf16[1840,128]{1,0:T(8,128)(2,1)S(1)}, bf16[1840,128]{1,0:T(8,128)(2,1)}, u32[]{:S(2)}) copy-start(bf16[1840,128]{1,0:T(8,128)(2,1)} %get-tuple-element.27.y0) | copy-start | bytes 1413124
  67.0 20.2 %copy-start.7 = (f32[8192]{0:T(1024)S(1)}, f32[8192]{0:T(1024)}, u32[]{:S(2)}) copy-start(f32[8192]{0:T(1024)} %param.12) | copy-start | bytes 98308
  67.0 20.2 %copy-start.9 = (f32[8192]{0:T(1024)S(1)}, f32[8192]{0:T(1024)}, u32[]{:S(2)}) copy-start(f32[8192]{0:T(1024)} %param.13) | copy-start | bytes 98308
  67.0 20.2 %collective-permute-start.2 = (bf16[1840,128]{1,0:T(8,128)(2,1)}, bf16[1840,128]{1,0:T(8,128)(2,1)S(1)}, u32[]{:S(2)}, u32[]{:S(2)}) collective-permute-start(bf16[1840,128]{1,0:T(8,128)(2,1)} %get-tuple-element.30), channel_id=1, source_target_pairs={{0,3},{1,0},{2,1},{3,2},{4,7},{5,4},{6,5},{7,6},{8,11},{9,8},{10,9... | collective-permute-start | bytes 1413128 | tf_op jit(solution)/shard_map/ppermute | solution.py:485
  68.3 47.1 %all-to-all-start.1 = ((bf16[32,6,32,256]{3,2,1,0:T(8,128)(2,1)}), bf16[32,6,32,256]{3,2,1,0:T(8,128)(2,1)}, u32[]{:S(2)}, u32[]{:S(2)}) async-start(bf16[32,6,32,256]{3,2,1,0:T(8,128)(2,1)} %send_permute.3.rest_0_), calls=%async_computation.1 | async-start | bytes 6291456 | tf_op jit(solution)/shard_map/all_to_all | solution.py:511
  89.8 5.7 %collective-permute-start.3 = (f32[2,104,128]{2,1,0:T(8,128)S(1)}, f32[2,104,128]{2,1,0:T(8,128)S(1)}, u32[]{:S(2)}, u32[]{:S(2)}) collective-permute-start(f32[2,104,128]{2,1,0:T(8,128)S(1)} %get-tuple-element.32), channel_id=1, source_target_pairs={{0,1},{1,2},{2,3},{3,0},{4,5},{5,6},{6,7},{7,4},{8,9},{9,10},{10,1... | collective-permute-start | bytes 319496 | tf_op jit(solution)/shard_map/ppermute | solution.py:485
  91.7 7.6 %collective-permute-start.4 = (f32[2,104,128]{2,1,0:T(8,128)S(1)}, f32[2,104,128]{2,1,0:T(8,128)S(1)}, u32[]{:S(2)}, u32[]{:S(2)}) collective-permute-start(f32[2,104,128]{2,1,0:T(8,128)S(1)} %get-tuple-element.33), channel_id=1, source_target_pairs={{0,2},{1,3},{2,0},{3,1},{4,6},{5,7},{6,4},{7,5},{8,10},{9,11},{10,... | collective-permute-start | bytes 319496 | tf_op jit(solution)/shard_map/ppermute | solution.py:485
  94.2 5.1 %collective-permute-start.5 = (f32[2,104,128]{2,1,0:T(8,128)S(1)}, f32[2,104,128]{2,1,0:T(8,128)S(1)}, u32[]{:S(2)}, u32[]{:S(2)}) collective-permute-start(f32[2,104,128]{2,1,0:T(8,128)S(1)} %get-tuple-element.34), channel_id=1, source_target_pairs={{0,3},{1,0},{2,1},{3,2},{4,7},{5,4},{6,5},{7,6},{8,11},{9,8},{10,9... | collective-permute-start | bytes 319496 | tf_op jit(solution)/shard_map/ppermute | solution.py:485
  104.1 11.3 %copy-start.6 = (bf16[2,128,128]{2,1,0:T(8,128)(2,1)}, bf16[2,128,128]{2,1,0:T(8,128)(2,1)S(1)}, u32[]{:S(2)}) copy-start(bf16[2,128,128]{2,1,0:T(8,128)(2,1)S(1)} %newton_schulz.2.rest_0_) | copy-start | bytes 196612
  104.1 22.3 %collective-permute-start.6 = (bf16[2,128,128]{2,1,0:T(8,128)(2,1)S(1)}, bf16[2,128,128]{2,1,0:T(8,128)(2,1)S(1)}, u32[]{:S(2)}, u32[]{:S(2)}) collective-permute-start(bf16[2,128,128]{2,1,0:T(8,128)(2,1)S(1)} %newton_schulz.2.rest_0_), channel_id=1, source_target_pairs={{0,1},{1,2},{2,3},{3,0},{4,5},{5,6},{6,7},{7,4},{8,9},{9,10},{10,1... | collective-permute-start | bytes 196616 | tf_op jit(solution)/shard_map/ppermute | solution.py:485
  104.2 22.2 %collective-permute-start.7 = (bf16[2,128,128]{2,1,0:T(8,128)(2,1)S(1)}, bf16[2,128,128]{2,1,0:T(8,128)(2,1)S(1)}, u32[]{:S(2)}, u32[]{:S(2)}) collective-permute-start(bf16[2,128,128]{2,1,0:T(8,128)(2,1)S(1)} %newton_schulz.2.rest_0_), channel_id=1, source_target_pairs={{0,2},{1,3},{2,0},{3,1},{4,6},{5,7},{6,4},{7,5},{8,10},{9,11},{10,... | collective-permute-start | bytes 196616 | tf_op jit(solution)/shard_map/ppermute | solution.py:485
  106.2 20.3 %collective-permute-start.8 = (bf16[2,128,128]{2,1,0:T(8,128)(2,1)S(1)}, bf16[2,128,128]{2,1,0:T(8,128)(2,1)S(1)}, u32[]{:S(2)}, u32[]{:S(2)}) collective-permute-start(bf16[2,128,128]{2,1,0:T(8,128)(2,1)S(1)} %newton_schulz.2.rest_0_), channel_id=1, source_target_pairs={{0,3},{1,0},{2,1},{3,2},{4,7},{5,4},{6,5},{7,6},{8,11},{9,8},{10,9... | collective-permute-start | bytes 196616 | tf_op jit(solution)/shard_map/ppermute | solution.py:485
  123.6 16.7 %collective-permute-start.10 = (bf16[1840,128]{1,0:T(8,128)(2,1)}, bf16[1840,128]{1,0:T(8,128)(2,1)}, u32[]{:S(2)}, u32[]{:S(2)}) collective-permute-start(bf16[1840,128]{1,0:T(8,128)(2,1)} %get-tuple-element.38), channel_id=1, source_target_pairs={{0,2},{1,3},{2,0},{3,1},{4,6},{5,7},{6,4},{7,5},{8,10},{9,11},{10,... | collective-permute-start | bytes 1413128 | tf_op jit(solution)/shard_map/ppermute | solution.py:485
  123.9 20.9 %collective-permute-start.11 = (bf16[1840,128]{1,0:T(8,128)(2,1)}, bf16[1840,128]{1,0:T(8,128)(2,1)}, u32[]{:S(2)}, u32[]{:S(2)}) collective-permute-start(bf16[1840,128]{1,0:T(8,128)(2,1)} %get-tuple-element.39), channel_id=1, source_target_pairs={{0,3},{1,0},{2,1},{3,2},{4,7},{5,4},{6,5},{7,6},{8,11},{9,8},{10,9... | collective-permute-start | bytes 1413128 | tf_op jit(solution)/shard_map/ppermute | solution.py:485
  126.4 21.9 %collective-permute-start.9 = (bf16[1840,128]{1,0:T(8,128)(2,1)}, bf16[1840,128]{1,0:T(8,128)(2,1)}, u32[]{:S(2)}, u32[]{:S(2)}) collective-permute-start(bf16[1840,128]{1,0:T(8,128)(2,1)} %get-tuple-element.37), channel_id=1, source_target_pairs={{0,1},{1,2},{2,3},{3,0},{4,5},{5,6},{6,7},{7,4},{8,9},{9,10},{10,1... | collective-permute-start | bytes 1413128 | tf_op jit(solution)/shard_map/ppermute | solution.py:485
  132.5 15.8 %copy-start.1 = (bf16[32,6,32,256]{3,2,1,0:T(8,128)(2,1)S(1)}, bf16[32,6,32,256]{3,2,1,0:T(8,128)(2,1)}, u32[]{:S(2)}) copy-start(bf16[32,6,32,256]{3,2,1,0:T(8,128)(2,1)} %apply_weights.2.rest_0_) | copy-start | bytes 9437188
  132.5 15.8 %copy-start.4 = (s32[16]{0:T(128)S(1)}, s32[16]{0:T(128)}, u32[]{:S(2)}) copy-start(s32[16]{0:T(128)} %counts_ref.7) | copy-start | bytes 196
  132.6 48.1 %all-to-all-start.2 = ((bf16[32,6,32,256]{3,2,1,0:T(8,128)(2,1)}), bf16[32,6,32,256]{3,2,1,0:T(8,128)(2,1)}, u32[]{:S(2)}, u32[]{:S(2)}) async-start(bf16[32,6,32,256]{3,2,1,0:T(8,128)(2,1)} %apply_weights.2.rest_0_), calls=%async_computation.2 | async-start | bytes 6291456 | tf_op jit(solution)/shard_map/all_to_all | solution.py:529
  153.9 8.0 %collective-permute-start.12 = (f32[2,104,128]{2,1,0:T(8,128)S(1)}, f32[2,104,128]{2,1,0:T(8,128)S(1)}, u32[]{:S(2)}, u32[]{:S(2)}) collective-permute-start(f32[2,104,128]{2,1,0:T(8,128)S(1)} %get-tuple-element.41), channel_id=1, source_target_pairs={{0,1},{1,2},{2,3},{3,0},{4,5},{5,6},{6,7},{7,4},{8,9},{9,10},{10,1... | collective-permute-start | bytes 319496 | tf_op jit(solution)/shard_map/ppermute | solution.py:485
  153.9 7.9 %collective-permute-start.13 = (f32[2,104,128]{2,1,0:T(8,128)S(1)}, f32[2,104,128]{2,1,0:T(8,128)S(1)}, u32[]{:S(2)}, u32[]{:S(2)}) collective-permute-start(f32[2,104,128]{2,1,0:T(8,128)S(1)} %get-tuple-element.42), channel_id=1, source_target_pairs={{0,2},{1,3},{2,0},{3,1},{4,6},{5,7},{6,4},{7,5},{8,10},{9,11},{10,... | collective-permute-start | bytes 319496 | tf_op jit(solution)/shard_map/ppermute | solution.py:485
  155.0 6.9 %collective-permute-start.14 = (f32[2,104,128]{2,1,0:T(8,128)S(1)}, f32[2,104,128]{2,1,0:T(8,128)S(1)}, u32[]{:S(2)}, u32[]{:S(2)}) collective-permute-start(f32[2,104,128]{2,1,0:T(8,128)S(1)} %get-tuple-element.43), channel_id=1, source_target_pairs={{0,3},{1,0},{2,1},{3,2},{4,7},{5,4},{6,5},{7,6},{8,11},{9,8},{10,9... | collective-permute-start | bytes 319496 | tf_op jit(solution)/shard_map/ppermute | solution.py:485
  166.7 7.9 %copy-start.2 = (bf16[2,128,128]{2,1,0:T(8,128)(2,1)}, bf16[2,128,128]{2,1,0:T(8,128)(2,1)S(1)}, u32[]{:S(2)}) copy-start(bf16[2,128,128]{2,1,0:T(8,128)(2,1)S(1)} %newton_schulz.3.rest_0_) | copy-start | bytes 196612
  166.7 4.8 %collective-permute-start.15 = (bf16[2,128,128]{2,1,0:T(8,128)(2,1)S(1)}, bf16[2,128,128]{2,1,0:T(8,128)(2,1)S(1)}, u32[]{:S(2)}, u32[]{:S(2)}) collective-permute-start(bf16[2,128,128]{2,1,0:T(8,128)(2,1)S(1)} %newton_schulz.3.rest_0_), channel_id=1, source_target_pairs={{0,1},{1,2},{2,3},{3,0},{4,5},{5,6},{6,7},{7,4},{8,9},{9,10},{10,1... | collective-permute-start | bytes 196616 | tf_op jit(solution)/shard_map/ppermute | solution.py:485
  167.3 6.0 %collective-permute-start.16 = (bf16[2,128,128]{2,1,0:T(8,128)(2,1)S(1)}, bf16[2,128,128]{2,1,0:T(8,128)(2,1)S(1)}, u32[]{:S(2)}, u32[]{:S(2)}) collective-permute-start(bf16[2,128,128]{2,1,0:T(8,128)(2,1)S(1)} %newton_schulz.3.rest_0_), channel_id=1, source_target_pairs={{0,2},{1,3},{2,0},{3,1},{4,6},{5,7},{6,4},{7,5},{8,10},{9,11},{10,... | collective-permute-start | bytes 196616 | tf_op jit(solution)/shard_map/ppermute | solution.py:485
  170.6 4.0 %collective-permute-start.17 = (bf16[2,128,128]{2,1,0:T(8,128)(2,1)S(1)}, bf16[2,128,128]{2,1,0:T(8,128)(2,1)S(1)}, u32[]{:S(2)}, u32[]{:S(2)}) collective-permute-start(bf16[2,128,128]{2,1,0:T(8,128)(2,1)S(1)} %newton_schulz.3.rest_0_), channel_id=1, source_target_pairs={{0,3},{1,0},{2,1},{3,2},{4,7},{5,4},{6,5},{7,6},{8,11},{9,8},{10,9... | collective-permute-start | bytes 196616 | tf_op jit(solution)/shard_map/ppermute | solution.py:485
  171.5 3.1 %copy-start.13 = (bf16[2,128,128]{2,1,0:T(8,128)(2,1)}, bf16[2,128,128]{2,1,0:T(8,128)(2,1)S(1)}, u32[]{:S(2)}) copy-start(bf16[2,128,128]{2,1,0:T(8,128)(2,1)S(1)} %collective-permute-done.15.rest_1_) | copy-start | bytes 196612
  180.6 47.0 %copy-start.11 = (s32[512]{0:T(512)S(1)}, s32[512]{0:T(512)}, u32[]{:S(2)}) copy-start(s32[512]{0:T(512)} %param.8) | copy-start | bytes 6148
  (8 other events, 6.3 us)
